TPU v7x, 32 devices: a whole 2x2x4 slice. The times are simulated.
32 devices in a mesh: dp: 16 (over z, x, core), proto: 2 (over y).
Axes of the slice: x: 2, y: 2, z: 4, core: 2. Of those that a mesh axis runs over, the one named last changes fastest.
Arguments:
- packed: float32 [16384, 256], P('dp'), may hold values from -120 to 120
- crop_offsets: int32 [48], P('dp'), may hold values from 0 to 768, as said below
- masked_patch: int32 [3072], P('dp'), may hold values from 0 to 255, as said below
- teacher_logits: bfloat16 [3072, 65536], P('dp', 'proto'), may hold values from -6 to 26
- prototypes: float32 [65536, 256], P(('proto', 'dp')), may hold values from -4 to 4
- gain: float32 [65536], P(('proto', 'dp')), may hold values from 0.5 to 30
Outputs:
- grad_packed: float32 [16384, 256], P('dp')
- grad_proto: float32 [65536, 256], P(('proto', 'dp'))
- grad_gain: float32 [65536], P(('proto', 'dp'))
Inputs may be any that keep to these rules, and one draw needn't show every extreme that they name: `crop_offsets`: within one index of dp the 3 crops of 256 rows lie inside the 1024 packed rows without intersecting, in increasing order. `masked_patch`: each crop has exactly 64 masked tokens, all with distinct patch indices; token t belongs to crop (t % 192) // 64 of its index of dp.
All inputs are finite; a program needn't handle non-finite values.
Results may differ from a plain program's by a relative error of at most 0.0003.
Values sent between devices are 32-bit elements; how exact they have to be, the bound alone decides.
No kernel may reach another device: no remote copies, remote signals or barrier semaphores. Data moves between devices by JAX's collectives and lax.ppermute only.
A program may use at most 256 MiB of HBM per device.

v0:
```python
import math

import jax
import jax.numpy as jnp
import numpy as np
from jax import lax
from jax.experimental import pallas as pl
from jax.experimental.pallas import tpu as pltpu
from jax.sharding import PartitionSpec as P

ITERS = 3
TEMP_S = 0.1
TEMP_T = 0.07
EPS = 1e-06
LOG2E = math.log2(math.e)
TEACH = LOG2E / TEMP_T
LANES = 128
GROUP = 16
VMEM_LIMIT = 20 * 1024 * 1024
F32 = jnp.float32
BF16 = jnp.bfloat16


def params():
    return pltpu.CompilerParams(vmem_limit_bytes=VMEM_LIMIT)


def split(x):
    hi = x.astype(BF16)
    return hi, (x - hi.astype(F32)).astype(BF16)


def dot(a, b, dims=((1,), (0,))):
    return lax.dot_general(a, b, (dims, ((), ())), preferred_element_type=F32)


def teacher_kernel(t_ref, m_ref, s_ref, copy_ref, *, width, unroll):
    copy_ref[...] = t_ref[...]
    span = LANES * unroll
    for r in range(0, t_ref.shape[0], GROUP):

        def largest(step, best):
            base = pl.multiple_of(step * span, span)
            for j in range(unroll):
                x = t_ref[r : r + GROUP, pl.ds(base + j * LANES, LANES)].astype(F32)
                best = jnp.maximum(best, x)
            return best

        best = lax.fori_loop(0, width // span, largest, jnp.full((GROUP, LANES), -jnp.inf, F32))
        top = jnp.broadcast_to(jnp.max(best, axis=1, keepdims=True), (GROUP, LANES)) * TEACH

        def total(step, acc):
            base = pl.multiple_of(step * span, span)
            for j in range(unroll):
                x = t_ref[r : r + GROUP, pl.ds(base + j * LANES, LANES)].astype(F32)
                acc = acc + jnp.exp2(x * TEACH - top)
            return acc

        acc = lax.fori_loop(0, width // span, total, jnp.zeros((GROUP, LANES), F32))
        m_ref[r : r + GROUP, :] = top
        s_ref[r : r + GROUP, :] = acc


def teacher_stats(teacher):
    tokens, width = teacher.shape
    rows = 32
    shape = jax.ShapeDtypeStruct((tokens, LANES), F32)
    spec = pl.BlockSpec((rows, LANES), lambda i: (i, 0))
    return pl.pallas_call(
        lambda *refs: teacher_kernel(*refs, width=width, unroll=16),
        grid=(tokens // rows,),
        in_specs=[pl.BlockSpec((rows, width), lambda i: (i, 0))],
        out_specs=[spec, spec, pl.BlockSpec((rows, width), lambda i: (i, 0))],
        out_shape=[shape, shape, jax.ShapeDtypeStruct(teacher.shape, teacher.dtype)],
        compiler_params=params(),
        name="teacher_stats",
    )(teacher)


def column_kernel(t_ref, a_ref, r1_ref, r2_ref, out_ref, new_ref, *, unroll):
    tokens, block = t_ref.shape

    @pl.when(pl.program_id(0) == 0)
    def _():
        total = jnp.sum(r1_ref[...], axis=1, keepdims=True) + jnp.sum(r2_ref[...], axis=1, keepdims=True)
        new_ref[...] = a_ref[...] + jnp.broadcast_to(jnp.log(total) * LOG2E, new_ref.shape)

    span = LANES * unroll

    def chunk(step, carry):
        base = pl.multiple_of(step * span, span)
        accs = [jnp.zeros((8, LANES), F32) for _ in range(unroll)]
        for r in range(0, tokens, GROUP):
            offset = new_ref[r : r + GROUP, :]
            for j in range(unroll):
                x = t_ref[r : r + GROUP, pl.ds(base + j * LANES, LANES)].astype(F32)
                e = jnp.exp2(x * TEACH - offset)
                accs[j] = accs[j] + (e[:8] + e[8:])
        for j in range(unroll):
            out_ref[0, :, pl.ds(base + j * LANES, LANES)] = jnp.sum(
                accs[j], axis=0, keepdims=True
            )
        return carry

    lax.fori_loop(0, block // span, chunk, 0)


def column_pass(teacher, offset, row_here, row_there, shard):
    tokens, width = teacher.shape
    block = shard
    owners = width // shard
    whole = pl.BlockSpec((tokens, LANES), lambda i: (0, 0))
    return pl.pallas_call(
        lambda *refs: column_kernel(*refs, unroll=min(16, shard // LANES)),
        grid=(width // block,),
        in_specs=[pl.BlockSpec((tokens, block), lambda i: (0, i)), whole, whole, whole],
        out_specs=[pl.BlockSpec((1, 1, shard), lambda i: (i, 0, 0)), whole],
        out_shape=[
            jax.ShapeDtypeStruct((owners, 1, shard), F32),
            jax.ShapeDtypeStruct((tokens, LANES), F32),
        ],
        compiler_params=params(),
        name="column_sums",
    )(teacher, offset, row_here, row_there)


def row_kernel(t_ref, a_ref, c_ref, out_ref, col_ref, *, unroll, balance):
    tokens, block = t_ref.shape
    span = LANES * unroll
    col_ref[...] = balance / c_ref[0]

    @pl.when(pl.program_id(0) == 0)
    def _():
        out_ref[...] = jnp.zeros_like(out_ref)

    def chunk(step, carry):
        base = pl.multiple_of(step * span, span)
        cols = [
            jnp.broadcast_to(col_ref[:, pl.ds(base + j * LANES, LANES)], (GROUP, LANES))
            for j in range(unroll)
        ]
        for r in range(0, tokens, GROUP):
            offset = a_ref[r : r + GROUP, :]
            acc = out_ref[r : r + GROUP, :]
            for j in range(unroll):
                x = t_ref[r : r + GROUP, pl.ds(base + j * LANES, LANES)].astype(F32)
                acc = acc + jnp.exp2(x * TEACH - offset) * cols[j]
            out_ref[r : r + GROUP, :] = acc
        return carry

    lax.fori_loop(0, block // span, chunk, 0)


def row_pass(teacher, offset, sums, balance):
    tokens, width = teacher.shape
    owners, _, block = sums.shape
    whole = pl.BlockSpec((tokens, LANES), lambda i: (0, 0))
    cols = pl.BlockSpec((1, block), lambda i: (0, i))
    return pl.pallas_call(
        lambda *refs: row_kernel(*refs, unroll=min(16, block // LANES), balance=balance),
        grid=(width // block,),
        in_specs=[pl.BlockSpec((tokens, block), lambda i: (0, i)), whole, pl.BlockSpec((1, 1, block), lambda i: (i, 0, 0))],
        out_specs=[whole, cols],
        out_shape=[
            jax.ShapeDtypeStruct((tokens, LANES), F32),
            jax.ShapeDtypeStruct((1, width), F32),
        ],
        compiler_params=params(),
        name="row_sums",
    )(teacher, offset, sums)


def parts_of_left(hi, lo, axis):
    return jnp.concatenate([hi, lo, hi], axis=axis)


def parts_of_right(hi, lo, axis):
    return jnp.concatenate([hi, hi, lo], axis=axis)


def student_kernel(u_ref, w_ref, m_ref, s_ref):
    tokens = u_ref.shape[1]

    @pl.when(pl.program_id(0) == 0)
    def _():
        m_ref[...] = jnp.full_like(m_ref, -1e30)
        s_ref[...] = jnp.zeros_like(s_ref)

    rows = w_ref.shape[0]
    chunk = min(rows, 512)
    largest, total = m_ref[...], s_ref[...]
    scores = []
    for r in range(0, rows, chunk):
        w_hi, w_lo = split(w_ref[r : r + chunk, :])
        logits = dot(parts_of_left(w_hi, w_lo, 1), u_ref[...])
        scores.append(logits.reshape(chunk // 8, 8, tokens))
    for logits in scores:
        best = jnp.maximum(largest, jnp.max(logits, axis=0))
        fresh = jnp.sum(jnp.exp2(logits - best[None]), axis=0)
        total = total * jnp.exp2(largest - best) + fresh
        largest = best
    m_ref[...] = largest
    s_ref[...] = total


def student_pass(u_turned, protos):
    tokens = u_turned.shape[1]
    rows, depth = protos.shape
    block = min(rows, 2048)
    stat = pl.BlockSpec((8, tokens), lambda i: (0, 0))
    shape = jax.ShapeDtypeStruct((8, tokens), F32)
    return pl.pallas_call(
        student_kernel,
        grid=(rows // block,),
        in_specs=[
            pl.BlockSpec(u_turned.shape, lambda i: (0, 0)),
            pl.BlockSpec((block, depth), lambda i: (i, 0)),
        ],
        out_specs=[stat, stat],
        out_shape=[shape, shape],
        compiler_params=params(),
        name="student_stats",
    )(u_turned, protos)


def grad_kernel(own, u_parts, t_parts, lse, offset, tok_in, *refs, blocks, arrivals, parity):
    teach, cols, protos = refs[:blocks], refs[blocks : 2 * blocks], refs[2 * blocks : 3 * blocks]
    arrived = refs[3 * blocks : 3 * blocks + arrivals]
    outs = refs[3 * blocks + arrivals : 4 * blocks + arrivals]
    tok_out = refs[4 * blocks + arrivals]

    @pl.when(pl.program_id(0) == 0)
    def _():
        tok_out[...] = tok_in[...]

    token_part = tok_out[...]
    lse_col = lse[:, :1]
    off_col = offset[:, :1]
    for i in range(blocks):
        w_hi, w_lo = split(protos[i][...])
        logits = dot(u_parts[...], parts_of_right(w_hi, w_lo, 1), ((1,), (1,)))
        student = jnp.exp2(logits - lse_col)
        target = jnp.exp2(teach[i][...].astype(F32) * TEACH - off_col) * cols[i][...]
        g_hi, g_lo = split(student - target)
        part = dot(t_parts[...], parts_of_right(g_hi, g_lo, 0))
        if arrivals == 1:
            odd = own[parity].astype(F32)
            part = part + arrived[0][...] * (odd if i == 0 else 1.0 - odd)
        elif arrivals:
            part = part + arrived[i][...]
        outs[i][...] = part
        token_part = token_part + dot(parts_of_left(g_hi, g_lo, 1), parts_of_right(w_hi, w_lo, 0))
    tok_out[...] = token_part


def grad_step(own, slots, consts, tok, teacher, cols, protos, arrived, width):
    tokens, depth = tok.shape
    block = min(width, 512)
    count = width // block
    blocks = len(slots)

    def whole(shape):
        return pl.BlockSpec(shape, lambda g, own: (0, 0))

    def across(shape):
        return pl.BlockSpec(shape, lambda g, own: (0, g))

    def picked(shape, slot):
        return pl.BlockSpec(shape, lambda g, own: (0, own[slot] * count + g))

    def rows(shape, slot):
        return pl.BlockSpec(shape, lambda g, own: (own[slot] * count + g, 0))

    grid = pltpu.PrefetchScalarGridSpec(
        num_scalar_prefetch=1,
        grid=(count,),
        in_specs=[whole(c.shape) for c in consts]
        + [whole(tok.shape)]
        + [picked((tokens, block), slot) for slot in slots]
        + [picked((1, block), slot) for slot in slots]
        + [rows((block, depth), slot) for slot in slots]
        + [across((depth, block)) for x in arrived],
        out_specs=[across((depth, block)) for slot in slots] + [whole(tok.shape)],
    )
    *parts, tok = pl.pallas_call(
        lambda *refs: grad_kernel(
            *refs, blocks=blocks, arrivals=len(arrived), parity=own.shape[0] - 1
        ),
        grid_spec=grid,
        out_shape=[jax.ShapeDtypeStruct((depth, width), F32) for slot in slots]
        + [jax.ShapeDtypeStruct(tok.shape, F32)],
        compiler_params=params(),
        name="grad_blocks",
    )(
        own,
        *consts,
        tok,
        *([teacher] * blocks),
        *([cols] * blocks),
        *([protos] * blocks),
        *arrived,
    )
    return parts, tok


def proto_kernel(turned_a, turned_b, gain_a, gain_b, *refs):
    grad_ref, gains_ref = refs[6:]
    for i, (turned, gain) in enumerate(((turned_a, gain_a), (turned_b, gain_b))):
        a, b, c = refs[3 * i : 3 * i + 3]
        summed = a[...] + (b[...] + c[...])
        protos = turned[...]
        norm = jnp.sqrt(jnp.sum(protos * protos, axis=0, keepdims=True) + EPS)
        unit = protos / norm
        gain_dot = jnp.sum(unit * summed, axis=0, keepdims=True)
        grad = gain[...] / (TEMP_S * norm) * (summed - unit * gain_dot)
        grad_ref[i] = grad.T
        gains_ref[i] = gain_dot / TEMP_S


def proto_grads(prototypes, gain, parts):
    depth, width = parts[0].shape
    block = min(width, 256)
    count = width // block
    turned = prototypes.T
    gain_row = gain[None, :]

    def at(shape, sub):
        return pl.BlockSpec(shape, lambda i: (0, sub * count + i))

    grad, gains = pl.pallas_call(
        proto_kernel,
        grid=(count,),
        in_specs=[at((depth, block), 0), at((depth, block), 1), at((1, block), 0), at((1, block), 1)]
        + [pl.BlockSpec((depth, block), lambda i: (0, i))] * 6,
        out_specs=[
            pl.BlockSpec((2, block, depth), lambda i: (0, i, 0)),
            pl.BlockSpec((2, 1, block), lambda i: (0, 0, i)),
        ],
        out_shape=[
            jax.ShapeDtypeStruct((2, width, depth), F32),
            jax.ShapeDtypeStruct((2, 1, width), F32),
        ],
        compiler_params=params(),
        name="proto_grads",
    )(turned, turned, gain_row, gain_row, *parts)
    return grad.reshape(2 * width, depth), gains.reshape(2 * width)


def halves(count):
    return [1 << bit for bit in range(count.bit_length() - 1)]


def swap(x, axis, count, distance):
    return lax.ppermute(x, axis, [(i, i ^ distance) for i in range(count)])


def sum_pair(x, axis, count):
    steps = halves(count)
    for distance in steps[:-1]:
        x = x + swap(x, axis, count, distance)
    return x, swap(x, axis, count, steps[-1])


def column_total(x):
    mine = jnp.sum(lax.all_to_all(x, "dp", 0, 0, tiled=True), axis=0, keepdims=True)
    return lax.all_to_all(jnp.broadcast_to(mine, x.shape), "dp", 0, 0, tiled=True)


def log_total(largest, total, axis, count):
    stats = jnp.stack([largest, total])
    for distance in halves(count):
        other = swap(stats, axis, count, distance)
        top = jnp.maximum(stats[0], other[0])
        both = stats[1] * jnp.exp2(stats[0] - top) + other[1] * jnp.exp2(other[0] - top)
        stats = jnp.stack([top, both])
    return stats[0] + jnp.log2(stats[1])


def sublane_stats(largest, total):
    top = jnp.max(largest, axis=0)
    return top, jnp.sum(total * jnp.exp2(largest - top[None, :]), axis=0)


def ring_order(count):
    depth = count // 4
    up = [z * 4 + core for z in range(depth) for core in range(2)]
    down = [z * 4 + 2 + core for z in reversed(range(depth)) for core in range(2)]
    return up + down


def body(packed, crop_offsets, masked_patch, teacher_logits, prototypes, gain):
    tokens_here = masked_patch.shape[0]
    crops_here = crop_offsets.shape[0]
    per_crop = tokens_here // crops_here
    dp_count = lax.axis_size("dp")
    proto_count = lax.axis_size("proto")
    slice_cols = teacher_logits.shape[1]
    shard = prototypes.shape[0]
    total_tokens = tokens_here * dp_count
    total_protos = slice_cols * proto_count
    loss_scale = total_protos / math.sqrt(total_tokens)
    balance = total_tokens / total_protos
    width = shard // 2
    half = dp_count // 2

    order = ring_order(dp_count)
    place = {d: p for p, d in enumerate(order)}

    def around(step):
        return [(d, order[(place[d] + step) % dp_count]) for d in range(dp_count)]

    ahead, behind = around(1), around(-1)
    slot_of = np.zeros((dp_count, 2 * dp_count + 1), np.int32)
    for d in range(dp_count):
        slot_of[d, 2 * dp_count] = place[d] % 2
        for far in range(dp_count):
            for sub in range(2):
                slot_of[d, 2 * far + sub] = 2 * order[(place[d] + far) % dp_count] + sub
    own = jnp.asarray(slot_of)[lax.axis_index("dp")]

    def slot(far, sub):
        return 2 * (far % dp_count) + sub

    proto_norm = jnp.sqrt(jnp.sum(prototypes * prototypes, axis=1, keepdims=True) + EPS)
    unit_proto = prototypes / proto_norm
    weights = unit_proto * (gain / TEMP_S)[:, None]
    gathered = lax.all_gather(weights, "dp", axis=0, tiled=True)

    crop_of = jnp.arange(tokens_here, dtype=jnp.int32) // per_crop
    match = crop_of[:, None] == jnp.arange(crops_here, dtype=jnp.int32)[None, :]
    starts = jnp.sum(jnp.where(match, crop_offsets[None, :], 0), axis=1)
    row_index = starts + masked_patch
    picked = jnp.take(packed, row_index, axis=0)
    inverse = lax.rsqrt(jnp.sum(picked * picked, axis=1, keepdims=True) + EPS)
    unit_tok = picked * inverse

    def pieces(x):
        hi = lax.reduce_precision(x, 8, 7)
        return hi.astype(BF16), (x - hi).astype(BF16)

    u_hi, u_lo = pieces(unit_tok * LOG2E)
    u_parts = parts_of_left(u_hi, u_lo, 1)
    u_turned = parts_of_right(u_hi, u_lo, 1).T
    t_parts = parts_of_left(*pieces(unit_tok.T), 1)

    top, total, teacher_logits = teacher_stats(teacher_logits)
    base = log_total(top[:, 0], jnp.sum(total, axis=1), "proto", proto_count)
    offset = jnp.broadcast_to(base[:, None], (tokens_here, LANES))
    lane = lax.broadcasted_iota(jnp.int32, (tokens_here, LANES), 1)
    row_here = jnp.where(lane == 0, 1.0, 0.0).astype(F32)
    row_there = jnp.zeros((tokens_here, LANES), F32)
    for sweep in range(ITERS):
        sums, offset = column_pass(teacher_logits, offset, row_here, row_there, shard)
        sums = column_total(sums)
        rows, cols = row_pass(teacher_logits, offset, sums, balance)
        row_here, row_there = sum_pair(rows, "proto", proto_count)
    row_sum = jnp.sum(row_here, axis=1) + jnp.sum(row_there, axis=1)
    offset = offset + jnp.log2(row_sum)[:, None]
    cols = cols * loss_scale

    largest, total = student_pass(u_turned, gathered)
    lse = log_total(*sublane_stats(largest, total), "proto", proto_count) - math.log2(loss_scale)
    lse = jnp.broadcast_to(lse[:, None], (tokens_here, LANES))

    token_part = jnp.zeros(unit_tok.shape, F32)
    consts = (u_parts, t_parts, lse, offset)

    def blocks_of(slots, arrived):
        return grad_step(
            own, slots, consts, token_part, teacher_logits, cols, gathered, arrived, width
        )

    crossed = [None, None]
    for sub in range(2):
        (part,), token_part = blocks_of((slot(half, sub),), [])
        crossed[sub] = swap(part, "dp", dp_count, 1)
    waiting = [[crossed[0]], [crossed[1]]]
    for far in range(half - 1, 0, -1):
        for sub in range(2):
            (first, second), token_part = blocks_of((slot(far, sub), slot(-far, sub)), waiting[sub])
            waiting[sub] = [
                lax.ppermute(first, "dp", ahead),
                lax.ppermute(second, "dp", behind),
            ]
    mine, token_part = blocks_of((slot(0, 0), slot(0, 1)), [])
    grad_proto, grad_gain = proto_grads(
        prototypes, gain, [x for sub in range(2) for x in (mine[sub], *waiting[sub])]
    )

    for distance in halves(proto_count):
        token_part = token_part + swap(token_part, "proto", proto_count, distance)
    inner_dot = jnp.sum(unit_tok * token_part, axis=1, keepdims=True)
    input_grad = (token_part - unit_tok * inner_dot) * inverse
    grad_packed = jnp.zeros(packed.shape, F32).at[row_index].set(input_grad)
    return (grad_packed, grad_proto, grad_gain)


def solution(mesh):
    placed = (
        P("dp", None),
        P("dp"),
        P("dp"),
        P("dp", "proto"),
        P(("proto", "dp"), None),
        P(("proto", "dp")),
    )
    return jax.shard_map(
        body,
        mesh=mesh,
        in_specs=placed,
        out_specs=(P("dp", None), P(("proto", "dp"), None), P(("proto", "dp"))),
        check_vma=False,
    )
```

profile of v0, /device:TPU:1, one launch (start us, length us, event | category | flops | bytes accessed | tf_op | source)
XLA Modules:
  0.0 438.1 jit_solution(8892095210720651895)
XLA Ops:
  11.2 4.6 %copy-done.9 = bf16[192,32768]{1,0:T(8,128)(2,1)S(1)} copy-done((bf16[192,32768]{1,0:T(8,128)(2,1)S(1)}, bf16[192,32768]{1,0:T(8,128)(2,1)}, u32[]{:S(2)}) %copy-start.9) | copy-done | bytes 12582936
  15.8 12.1 %teacher_stats.1 = (f32[192,128]{1,0:T(8,128)S(1)}, f32[192,128]{1,0:T(8,128)S(1)}, bf16[192,32768]{1,0:T(8,128)(2,1)S(1)}) custom-call(bf16[192,32768]{1,0:T(8,128)(2,1)S(1)} %copy-done.9), custom_call_target="tpu_custom_call" | custom-call | tf_op jit(solution)/shard_map/teacher_stats/pallas_call | solution.py:69
  27.9 4.6 %copy-done.3 = bf16[192,32768]{1,0:T(8,128)(2,1)} copy-done((bf16[192,32768]{1,0:T(8,128)(2,1)}, bf16[192,32768]{1,0:T(8,128)(2,1)S(1)}, u32[]{:S(2)}) %copy-start.3) | copy-done | bytes 12582936
  36.8 4.8 %copy-done.4 = bf16[192,32768]{1,0:T(8,128)(2,1)S(1)} copy-done((bf16[192,32768]{1,0:T(8,128)(2,1)S(1)}, bf16[192,32768]{1,0:T(8,128)(2,1)}, u32[]{:S(2)}) %copy-start.4) | copy-done | bytes 12582936
  41.6 5.7 %column_sums.3 = (f32[16,1,2048]{2,1,0:T(1,128)S(1)}, f32[192,128]{1,0:T(8,128)S(1)}) custom-call(bf16[192,32768]{1,0:T(8,128)(2,1)S(1)} %copy-done.4, f32[192,128]{1,0:T(8,128)S(1)} %broadcast_in_dim.94.refs_1_, f32[192,128]{1,0:T(8,128)S(1)} %iota.17.refs_2_, f32[192,128]{1,0:T(8,128)S(1)} %broadcast_in_dim.97.refs_3_), custom_call_target="tpu_custom_call" | custom-call | tf_op jit(solution)/shard_map/column_sums/pallas_call | solution.py:113
  47.3 16.6 %all_to_all.30 = f32[16,1,2048]{2,1,0:T(1,128)S(1)} all-to-all(f32[16,1,2048]{2,1,0:T(1,128)S(1)} %get-tuple-element.75), channel_id=1, replica_groups=mesh['dp'=16,'proto'=2] {'dp'}, dimensions={0} | all-to-all | bytes 262144 | tf_op jit(solution)/shard_map/all_to_all | solution.py:365
  64.1 13.0 %all_to_all.31.refs_2_ = f32[16,1,2048]{2,1,0:T(1,128)S(1)} all-to-all(f32[16,1,2048]{2,1,0:T(1,128)S(1)} %broadcast_in_dim.98), channel_id=1, replica_groups=mesh['dp'=16,'proto'=2] {'dp'}, dimensions={0} | all-to-all | bytes 262144 | tf_op jit(solution)/shard_map/all_to_all | solution.py:366
  77.0 4.9 %copy-done.5 = bf16[192,32768]{1,0:T(8,128)(2,1)S(1)} copy-done((bf16[192,32768]{1,0:T(8,128)(2,1)S(1)}, bf16[192,32768]{1,0:T(8,128)(2,1)}, u32[]{:S(2)}) %copy-start.5) | copy-done | bytes 12582936
  82.0 6.6 %row_sums.3 = (f32[192,128]{1,0:T(8,128)S(1)}, f32[1,32768]{1,0:T(1,128)}) custom-call(bf16[192,32768]{1,0:T(8,128)(2,1)S(1)} %copy-done.5, f32[192,128]{1,0:T(8,128)S(1)} %get-tuple-element.74.refs_1_, f32[16,1,2048]{2,1,0:T(1,128)S(1)} %all_to_all.31.refs_2_), custom_call_target="tpu_custom_call" | custom-call | tf_op jit(solution)/shard_map/row_sums/pallas_call | solution.py:159
  89.7 2.6 collective-permute-done.2.refs_3_
  92.4 8.0 %column_sums.4 = (f32[16,1,2048]{2,1,0:T(1,128)}, f32[192,128]{1,0:T(8,128)S(1)}) custom-call(bf16[192,32768]{1,0:T(8,128)(2,1)S(1)} %copy-done.5, f32[192,128]{1,0:T(8,128)S(1)} %get-tuple-element.74.refs_1_, f32[192,128]{1,0:T(8,128)S(1)} %get-tuple-element.76.refs_2_, f32[192,128]{1,0:T(8,128)S(1)} %collective-permute-done.2.refs_3_), custom_call_target="tpu_custom_call" | custom-call | tf_op jit(solution)/shard_map/column_sums/pallas_call | solution.py:113
  100.3 5.2 %all-to-all-start.2 = ((f32[16,1,2048]{2,1,0:T(1,128)}), f32[16,1,2048]{2,1,0:T(1,128)S(1)}, u32[]{:S(2)}, u32[]{:S(2)}) async-start(f32[16,1,2048]{2,1,0:T(1,128)} %get-tuple-element.78), calls=%async_computation.2 | async-start | bytes 262144 | tf_op jit(solution)/shard_map/all_to_all | solution.py:365
  105.6 9.2 %all-to-all-done.2 = f32[16,1,2048]{2,1,0:T(1,128)S(1)} async-done(((f32[16,1,2048]{2,1,0:T(1,128)}), f32[16,1,2048]{2,1,0:T(1,128)S(1)}, u32[]{:S(2)}, u32[]{:S(2)}) %all-to-all-start.2) | async-done | bytes 131104 | tf_op jit(solution)/shard_map/all_to_all | solution.py:365
  115.7 4.5 %all-to-all-start.3 = ((f32[16,1,2048]{2,1,0:T(1,128)}), f32[16,1,2048]{2,1,0:T(1,128)S(1)}, u32[]{:S(2)}, u32[]{:S(2)}) async-start(f32[16,1,2048]{2,1,0:T(1,128)} %broadcast_in_dim.99), calls=%async_computation.3 | async-start | bytes 262144 | tf_op jit(solution)/shard_map/all_to_all | solution.py:366
  121.9 7.7 %all-to-all-done.3.refs_2_ = f32[16,1,2048]{2,1,0:T(1,128)S(1)} async-done(((f32[16,1,2048]{2,1,0:T(1,128)}), f32[16,1,2048]{2,1,0:T(1,128)S(1)}, u32[]{:S(2)}, u32[]{:S(2)}) %all-to-all-start.3) | async-done | bytes 131104 | tf_op jit(solution)/shard_map/all_to_all | solution.py:366
  129.5 4.8 %copy-done.6 = bf16[192,32768]{1,0:T(8,128)(2,1)S(1)} copy-done((bf16[192,32768]{1,0:T(8,128)(2,1)S(1)}, bf16[192,32768]{1,0:T(8,128)(2,1)}, u32[]{:S(2)}) %copy-start.6) | copy-done | bytes 12582936
  134.4 6.6 %row_sums.4 = (f32[192,128]{1,0:T(8,128)S(1)}, f32[1,32768]{1,0:T(1,128)}) custom-call(bf16[192,32768]{1,0:T(8,128)(2,1)S(1)} %copy-done.6, f32[192,128]{1,0:T(8,128)S(1)} %get-tuple-element.77.refs_1_, f32[16,1,2048]{2,1,0:T(1,128)S(1)} %all-to-all-done.3.refs_2_), custom_call_target="tpu_custom_call" | custom-call | tf_op jit(solution)/shard_map/row_sums/pallas_call | solution.py:159
  142.1 2.6 collective-permute-done.3.refs_3_
  144.8 8.0 %column_sums.5 = (f32[16,1,2048]{2,1,0:T(1,128)}, f32[192,128]{1,0:T(8,128)S(1)}) custom-call(bf16[192,32768]{1,0:T(8,128)(2,1)S(1)} %copy-done.6, f32[192,128]{1,0:T(8,128)S(1)} %get-tuple-element.77.refs_1_, f32[192,128]{1,0:T(8,128)S(1)} %get-tuple-element.79.refs_2_, f32[192,128]{1,0:T(8,128)S(1)} %collective-permute-done.3.refs_3_), custom_call_target="tpu_custom_call" | custom-call | tf_op jit(solution)/shard_map/column_sums/pallas_call | solution.py:113
  152.7 5.3 %all-to-all-start.4 = ((f32[16,1,2048]{2,1,0:T(1,128)}), f32[16,1,2048]{2,1,0:T(1,128)S(1)}, u32[]{:S(2)}, u32[]{:S(2)}) async-start(f32[16,1,2048]{2,1,0:T(1,128)} %get-tuple-element.81), calls=%async_computation.4 | async-start | bytes 262144 | tf_op jit(solution)/shard_map/all_to_all | solution.py:365
  158.2 9.2 %all-to-all-done.4 = f32[16,1,2048]{2,1,0:T(1,128)S(1)} async-done(((f32[16,1,2048]{2,1,0:T(1,128)}), f32[16,1,2048]{2,1,0:T(1,128)S(1)}, u32[]{:S(2)}, u32[]{:S(2)}) %all-to-all-start.4) | async-done | bytes 131104 | tf_op jit(solution)/shard_map/all_to_all | solution.py:365
  168.2 4.8 %all-to-all-start.5 = ((f32[16,1,2048]{2,1,0:T(1,128)}), f32[16,1,2048]{2,1,0:T(1,128)S(1)}, u32[]{:S(2)}, u32[]{:S(2)}) async-start(f32[16,1,2048]{2,1,0:T(1,128)} %broadcast_in_dim.100), calls=%async_computation.5 | async-start | bytes 262144 | tf_op jit(solution)/shard_map/all_to_all | solution.py:366
  174.0 8.2 %all-to-all-done.5.refs_2_ = f32[16,1,2048]{2,1,0:T(1,128)S(1)} async-done(((f32[16,1,2048]{2,1,0:T(1,128)}), f32[16,1,2048]{2,1,0:T(1,128)S(1)}, u32[]{:S(2)}, u32[]{:S(2)}) %all-to-all-start.5) | async-done | bytes 131104 | tf_op jit(solution)/shard_map/all_to_all | solution.py:366
  182.2 4.6 %copy-done.7 = bf16[192,32768]{1,0:T(8,128)(2,1)S(1)} copy-done((bf16[192,32768]{1,0:T(8,128)(2,1)S(1)}, bf16[192,32768]{1,0:T(8,128)(2,1)}, u32[]{:S(2)}) %copy-start.7) | copy-done | bytes 12582936
  186.8 6.2 %row_sums.5 = (f32[192,128]{1,0:T(8,128)S(1)}, f32[1,32768]{1,0:T(1,128)S(1)}) custom-call(bf16[192,32768]{1,0:T(8,128)(2,1)S(1)} %copy-done.7, f32[192,128]{1,0:T(8,128)S(1)} %get-tuple-element.80.refs_1_, f32[16,1,2048]{2,1,0:T(1,128)S(1)} %all-to-all-done.5.refs_2_), custom_call_target="tpu_custom_call" | custom-call | tf_op jit(solution)/shard_map/row_sums/pallas_call | solution.py:159
  196.7 10.5 %copy-done.2 = f32[32768,256]{1,0:T(8,128)S(1)} copy-done((f32[32768,256]{1,0:T(8,128)S(1)}, f32[32768,256]{1,0:T(8,128)}, u32[]{:S(2)}) %copy-start.2) | copy-done | bytes 33554456
  207.3 20.8 %student_stats.1 = (f32[8,192]{1,0:T(8,128)S(1)}, f32[8,192]{1,0:T(8,128)S(1)}) custom-call(bf16[768,192]{1,0:T(8,128)(2,1)S(1)} %get-tuple-element.143.u_ref, f32[32768,256]{1,0:T(8,128)S(1)} %copy-done.2), custom_call_target="tpu_custom_call" | custom-call | tf_op jit(solution)/shard_map/student_stats/pallas_call | solution.py:212
  230.7 4.6 %copy-done.8 = bf16[192,32768]{1,0:T(8,128)(2,1)S(1)} copy-done((bf16[192,32768]{1,0:T(8,128)(2,1)S(1)}, bf16[192,32768]{1,0:T(8,128)(2,1)}, u32[]{:S(2)}) %copy-start.8) | copy-done | bytes 12582936
  235.3 3.7 grad_blocks.17
  239.0 3.6 collective-permute-start.5
  242.6 3.7 grad_blocks.18
  246.3 5.5 %grad_blocks.19 = (f32[256,1024]{1,0:T(8,128)S(1)}, f32[256,1024]{1,0:T(8,128)S(1)}, f32[192,256]{1,0:T(8,128)S(1)}) custom-call(s32[33]{0:T(128)S(1)} %dynamic-slice_bitcast_fusion.refs_0_, bf16[192,768]{1,0:T(8,128)(2,1)S(1)} %copy.104.refs_1_, bf16[256,576]{1,0:T(8,128)(2,1)S(1)} %pad_maximum_fusion.2.refs_2_, f32[192,128]{1,0:T(8,128)S(1)} %broadcast_in_dim.92.refs_3_, ...), custom_call_target="tpu_custom_call" | custom-call | tf_op jit(solution)/shard_map/grad_blocks/pallas_call | solution.py:285
  253.4 5.5 %grad_blocks.20 = (f32[256,1024]{1,0:T(8,128)S(1)}, f32[256,1024]{1,0:T(8,128)S(1)}, f32[192,256]{1,0:T(8,128)S(1)}) custom-call(s32[33]{0:T(128)S(1)} %dynamic-slice_bitcast_fusion.refs_0_, bf16[192,768]{1,0:T(8,128)(2,1)S(1)} %copy.104.refs_1_, bf16[256,576]{1,0:T(8,128)(2,1)S(1)} %pad_maximum_fusion.2.refs_2_, f32[192,128]{1,0:T(8,128)S(1)} %broadcast_in_dim.92.refs_3_, ...), custom_call_target="tpu_custom_call" | custom-call | tf_op jit(solution)/shard_map/grad_blocks/pallas_call | solution.py:285
  260.8 4.4 %collective-permute-done.7.refs_12_ = f32[256,1024]{1,0:T(8,128)S(1)} collective-permute-done((f32[256,1024]{1,0:T(8,128)S(1)}, f32[256,1024]{1,0:T(8,128)S(1)}, u32[]{:S(2)}, u32[]{:S(2)}) %collective-permute-start.7) | collective-permute-done | bytes 1048608 | tf_op jit(solution)/shard_map/ppermute | solution.py:482
  265.2 2.8 collective-permute-done.8.refs_13_
  267.9 5.5 %grad_blocks.21 = (f32[256,1024]{1,0:T(8,128)S(1)}, f32[256,1024]{1,0:T(8,128)S(1)}, f32[192,256]{1,0:T(8,128)S(1)}) custom-call(s32[33]{0:T(128)S(1)} %dynamic-slice_bitcast_fusion.refs_0_, bf16[192,768]{1,0:T(8,128)(2,1)S(1)} %copy.104.refs_1_, bf16[256,576]{1,0:T(8,128)(2,1)S(1)} %pad_maximum_fusion.2.refs_2_, f32[192,128]{1,0:T(8,128)S(1)} %broadcast_in_dim.92.refs_3_, ...), custom_call_target="tpu_custom_call" | custom-call | tf_op jit(solution)/shard_map/grad_blocks/pallas_call | solution.py:285
  274.0 5.2 %collective-permute-done.10.refs_13_ = f32[256,1024]{1,0:T(8,128)S(1)} collective-permute-done((f32[256,1024]{1,0:T(8,128)S(1)}, f32[256,1024]{1,0:T(8,128)S(1)}, u32[]{:S(2)}, u32[]{:S(2)}) %collective-permute-start.10) | collective-permute-done | bytes 1048608 | tf_op jit(solution)/shard_map/ppermute | solution.py:483
  279.2 6.5 %grad_blocks.22 = (f32[256,1024]{1,0:T(8,128)}, f32[256,1024]{1,0:T(8,128)}, f32[192,256]{1,0:T(8,128)S(1)}) custom-call(s32[33]{0:T(128)S(1)} %dynamic-slice_bitcast_fusion.refs_0_, bf16[192,768]{1,0:T(8,128)(2,1)S(1)} %copy.104.refs_1_, bf16[256,576]{1,0:T(8,128)(2,1)S(1)} %pad_maximum_fusion.2.refs_2_, f32[192,128]{1,0:T(8,128)S(1)} %broadcast_in_dim.92.refs_3_, ...), custom_call_target="tpu_custom_call" | custom-call | tf_op jit(solution)/shard_map/grad_blocks/pallas_call | solution.py:285
  287.6 2.8 collective-permute-done.12.refs_13_
  290.5 5.8 %grad_blocks.23 = (f32[256,1024]{1,0:T(8,128)S(1)}, f32[256,1024]{1,0:T(8,128)S(1)}, f32[192,256]{1,0:T(8,128)S(1)}) custom-call(s32[33]{0:T(128)S(1)} %dynamic-slice_bitcast_fusion.refs_0_, bf16[192,768]{1,0:T(8,128)(2,1)S(1)} %copy.104.refs_1_, bf16[256,576]{1,0:T(8,128)(2,1)S(1)} %pad_maximum_fusion.2.refs_2_, f32[192,128]{1,0:T(8,128)S(1)} %broadcast_in_dim.92.refs_3_, ...), custom_call_target="tpu_custom_call" | custom-call | tf_op jit(solution)/shard_map/grad_blocks/pallas_call | solution.py:285
  299.0 2.7 collective-permute-done.14.refs_13_
  301.7 5.8 %grad_blocks.24 = (f32[256,1024]{1,0:T(8,128)S(1)}, f32[256,1024]{1,0:T(8,128)S(1)}, f32[192,256]{1,0:T(8,128)S(1)}) custom-call(s32[33]{0:T(128)S(1)} %dynamic-slice_bitcast_fusion.refs_0_, bf16[192,768]{1,0:T(8,128)(2,1)S(1)} %copy.104.refs_1_, bf16[256,576]{1,0:T(8,128)(2,1)S(1)} %pad_maximum_fusion.2.refs_2_, f32[192,128]{1,0:T(8,128)S(1)} %broadcast_in_dim.92.refs_3_, ...), custom_call_target="tpu_custom_call" | custom-call | tf_op jit(solution)/shard_map/grad_blocks/pallas_call | solution.py:285
  310.1 2.8 collective-permute-done.16.refs_13_
  312.9 5.8 %grad_blocks.25 = (f32[256,1024]{1,0:T(8,128)S(1)}, f32[256,1024]{1,0:T(8,128)S(1)}, f32[192,256]{1,0:T(8,128)S(1)}) custom-call(s32[33]{0:T(128)S(1)} %dynamic-slice_bitcast_fusion.refs_0_, bf16[192,768]{1,0:T(8,128)(2,1)S(1)} %copy.104.refs_1_, bf16[256,576]{1,0:T(8,128)(2,1)S(1)} %pad_maximum_fusion.2.refs_2_, f32[192,128]{1,0:T(8,128)S(1)} %broadcast_in_dim.92.refs_3_, ...), custom_call_target="tpu_custom_call" | custom-call | tf_op jit(solution)/shard_map/grad_blocks/pallas_call | solution.py:285
  321.3 2.8 collective-permute-done.18.refs_13_
  324.2 5.8 %grad_blocks.26 = (f32[256,1024]{1,0:T(8,128)S(1)}, f32[256,1024]{1,0:T(8,128)S(1)}, f32[192,256]{1,0:T(8,128)S(1)}) custom-call(s32[33]{0:T(128)S(1)} %dynamic-slice_bitcast_fusion.refs_0_, bf16[192,768]{1,0:T(8,128)(2,1)S(1)} %copy.104.refs_1_, bf16[256,576]{1,0:T(8,128)(2,1)S(1)} %pad_maximum_fusion.2.refs_2_, f32[192,128]{1,0:T(8,128)S(1)} %broadcast_in_dim.92.refs_3_, ...), custom_call_target="tpu_custom_call" | custom-call | tf_op jit(solution)/shard_map/grad_blocks/pallas_call | solution.py:285
  332.6 2.8 collective-permute-done.20.refs_13_
  335.4 5.8 %grad_blocks.27 = (f32[256,1024]{1,0:T(8,128)S(1)}, f32[256,1024]{1,0:T(8,128)S(1)}, f32[192,256]{1,0:T(8,128)S(1)}) custom-call(s32[33]{0:T(128)S(1)} %dynamic-slice_bitcast_fusion.refs_0_, bf16[192,768]{1,0:T(8,128)(2,1)S(1)} %copy.104.refs_1_, bf16[256,576]{1,0:T(8,128)(2,1)S(1)} %pad_maximum_fusion.2.refs_2_, f32[192,128]{1,0:T(8,128)S(1)} %broadcast_in_dim.92.refs_3_, ...), custom_call_target="tpu_custom_call" | custom-call | tf_op jit(solution)/shard_map/grad_blocks/pallas_call | solution.py:285
  343.8 2.8 collective-permute-done.22.refs_13_
  346.6 5.8 %grad_blocks.28 = (f32[256,1024]{1,0:T(8,128)S(1)}, f32[256,1024]{1,0:T(8,128)S(1)}, f32[192,256]{1,0:T(8,128)S(1)}) custom-call(s32[33]{0:T(128)S(1)} %dynamic-slice_bitcast_fusion.refs_0_, bf16[192,768]{1,0:T(8,128)(2,1)S(1)} %copy.104.refs_1_, bf16[256,576]{1,0:T(8,128)(2,1)S(1)} %pad_maximum_fusion.2.refs_2_, f32[192,128]{1,0:T(8,128)S(1)} %broadcast_in_dim.92.refs_3_, ...), custom_call_target="tpu_custom_call" | custom-call | tf_op jit(solution)/shard_map/grad_blocks/pallas_call | solution.py:285
  355.1 2.8 collective-permute-done.24.refs_13_
  357.9 5.8 %grad_blocks.29 = (f32[256,1024]{1,0:T(8,128)S(1)}, f32[256,1024]{1,0:T(8,128)S(1)}, f32[192,256]{1,0:T(8,128)S(1)}) custom-call(s32[33]{0:T(128)S(1)} %dynamic-slice_bitcast_fusion.refs_0_, bf16[192,768]{1,0:T(8,128)(2,1)S(1)} %copy.104.refs_1_, bf16[256,576]{1,0:T(8,128)(2,1)S(1)} %pad_maximum_fusion.2.refs_2_, f32[192,128]{1,0:T(8,128)S(1)} %broadcast_in_dim.92.refs_3_, ...), custom_call_target="tpu_custom_call" | custom-call | tf_op jit(solution)/shard_map/grad_blocks/pallas_call | solution.py:285
  366.3 2.8 collective-permute-done.26.refs_13_
  369.1 5.8 %grad_blocks.30 = (f32[256,1024]{1,0:T(8,128)S(1)}, f32[256,1024]{1,0:T(8,128)S(1)}, f32[192,256]{1,0:T(8,128)S(1)}) custom-call(s32[33]{0:T(128)S(1)} %dynamic-slice_bitcast_fusion.refs_0_, bf16[192,768]{1,0:T(8,128)(2,1)S(1)} %copy.104.refs_1_, bf16[256,576]{1,0:T(8,128)(2,1)S(1)} %pad_maximum_fusion.2.refs_2_, f32[192,128]{1,0:T(8,128)S(1)} %broadcast_in_dim.92.refs_3_, ...), custom_call_target="tpu_custom_call" | custom-call | tf_op jit(solution)/shard_map/grad_blocks/pallas_call | solution.py:285
  377.5 2.8 collective-permute-done.28.refs_13_
  380.3 6.2 %grad_blocks.31 = (f32[256,1024]{1,0:T(8,128)}, f32[256,1024]{1,0:T(8,128)}, f32[192,256]{1,0:T(8,128)S(1)}) custom-call(s32[33]{0:T(128)S(1)} %dynamic-slice_bitcast_fusion.refs_0_, bf16[192,768]{1,0:T(8,128)(2,1)S(1)} %copy.104.refs_1_, bf16[256,576]{1,0:T(8,128)(2,1)S(1)} %pad_maximum_fusion.2.refs_2_, f32[192,128]{1,0:T(8,128)S(1)} %broadcast_in_dim.92.refs_3_, ...), custom_call_target="tpu_custom_call" | custom-call | tf_op jit(solution)/shard_map/grad_blocks/pallas_call | solution.py:285
  388.8 2.5 collective-permute-done.30.refs_13_
  391.2 6.3 %grad_blocks.32 = (f32[256,1024]{1,0:T(8,128)}, f32[256,1024]{1,0:T(8,128)}, f32[192,256]{1,0:T(8,128)S(1)}) custom-call(s32[33]{0:T(128)S(1)} %dynamic-slice_bitcast_fusion.refs_0_, bf16[192,768]{1,0:T(8,128)(2,1)S(1)} %copy.104.refs_1_, bf16[256,576]{1,0:T(8,128)(2,1)S(1)} %pad_maximum_fusion.2.refs_2_, f32[192,128]{1,0:T(8,128)S(1)} %broadcast_in_dim.92.refs_3_, ...), custom_call_target="tpu_custom_call" | custom-call | tf_op jit(solution)/shard_map/grad_blocks/pallas_call | solution.py:285
  399.3 5.5 %grad_blocks.33 = (f32[256,1024]{1,0:T(8,128)S(1)}, f32[256,1024]{1,0:T(8,128)S(1)}, f32[192,256]{1,0:T(8,128)S(1)}) custom-call(s32[33]{0:T(128)S(1)} %dynamic-slice_bitcast_fusion.refs_0_, bf16[192,768]{1,0:T(8,128)(2,1)S(1)} %copy.104.refs_1_, bf16[256,576]{1,0:T(8,128)(2,1)S(1)} %pad_maximum_fusion.2.refs_2_, f32[192,128]{1,0:T(8,128)S(1)} %broadcast_in_dim.92.refs_3_, ...), custom_call_target="tpu_custom_call" | custom-call | tf_op jit(solution)/shard_map/grad_blocks/pallas_call | solution.py:285
  410.0 4.1 collective-permute-done.31
  414.5 2.3 scatter_custom_fusion
  416.8 4.0 collective-permute-done.32.refs_1_
  420.8 2.5 collective-permute-done.33.refs_2_
  425.7 5.0 %proto_grads.1 = (f32[2,1024,256]{2,1,0:T(8,128)}, f32[2,1,1024]{2,1,0:T(1,128)}) custom-call(f32[256,2048]{1,0:T(8,128)S(1)} %bitcast.40, f32[256,2048]{1,0:T(8,128)S(1)} %bitcast.41, f32[1,2048]{1,0:T(1,128)S(1)} %bitcast.42, f32[1,2048]{1,0:T(1,128)S(1)} %bitcast.43, f32[256,1024]{1,0:T(8,128)S(1)} %copy-done.11, ...), custom_call_target="tpu_custom_call" | custom-call | tf_op jit(solution)/shard_map/proto_grads/pallas_call | solution.py:330
  (215 shorter events, 60.4 us)
Async XLA Ops:
  7.2 113.6 %copy-start = (f32[1024,256]{1,0:T(8,128)S(1)}, f32[1024,256]{1,0:T(8,128)}, u32[]{:S(2)}) copy-start(f32[1024,256]{1,0:T(8,128)} %param.7) | copy-start | bytes 3145732
  7.2 189.5 %all-gather.2.cloned.1.call-start = ((), (), s32[]{:S(2)}) async-start(), calls=%async_computation.6 | async-start | bytes 35651584 | tf_op jit(solution)/shard_map/all_gather | solution.py:427
  32.7 3.5 collective-permute-start.1
  88.5 17.0 %copy-start.25 = (s32[3]{0:T(128)S(1)}, s32[3]{0:T(128)}, u32[]{:S(2)}) copy-start(s32[3]{0:T(128)} %param.8) | copy-start | bytes 40
  88.5 31.7 %copy-start.24 = (s32[192]{0:T(256)S(1)}, s32[192]{0:T(256)}, u32[]{:S(2)}) copy-start(s32[192]{0:T(256)} %param.9) | copy-start | bytes 2308
  88.5 3.9 collective-permute-start.2
  100.3 14.5 %all-to-all-start.2 = ((f32[16,1,2048]{2,1,0:T(1,128)}), f32[16,1,2048]{2,1,0:T(1,128)S(1)}, u32[]{:S(2)}, u32[]{:S(2)}) async-start(f32[16,1,2048]{2,1,0:T(1,128)} %get-tuple-element.78), calls=%async_computation.2 | async-start | bytes 262144 | tf_op jit(solution)/shard_map/all_to_all | solution.py:365
  115.7 13.9 %all-to-all-start.3 = ((f32[16,1,2048]{2,1,0:T(1,128)}), f32[16,1,2048]{2,1,0:T(1,128)S(1)}, u32[]{:S(2)}, u32[]{:S(2)}) async-start(f32[16,1,2048]{2,1,0:T(1,128)} %broadcast_in_dim.99), calls=%async_computation.3 | async-start | bytes 262144 | tf_op jit(solution)/shard_map/all_to_all | solution.py:366
  120.2 37.9 %copy-start.21 = (pred[192]{0:T(512)(128)(4,1)}, pred[192]{0:T(512)(128)(4,1)S(1)}, u32[]{:S(2)}) copy-start(pred[192]{0:T(512)(128)(4,1)S(1)} %get-tuple-element.137) | copy-start | bytes 580
  121.8 36.3 %copy-start.17 = (f32[192,256]{0,1:T(8,128)}, f32[192,256]{0,1:T(8,128)S(1)}, u32[]{:S(2)}) copy-start(f32[192,256]{0,1:T(8,128)S(1)} %copy.83) | copy-start | bytes 589828
  140.9 3.9 collective-permute-start.3
  142.1 16.0 %copy-start.19 = (f32[192]{0:T(256)}, f32[192]{0:T(256)S(1)}, u32[]{:S(2)}) copy-start(f32[192]{0:T(256)S(1)} %add_rsqrt_fusion) | copy-start | bytes 2308
  152.7 14.6 %all-to-all-start.4 = ((f32[16,1,2048]{2,1,0:T(1,128)}), f32[16,1,2048]{2,1,0:T(1,128)S(1)}, u32[]{:S(2)}, u32[]{:S(2)}) async-start(f32[16,1,2048]{2,1,0:T(1,128)} %get-tuple-element.81), calls=%async_computation.4 | async-start | bytes 262144 | tf_op jit(solution)/shard_map/all_to_all | solution.py:365
  168.2 14.0 %all-to-all-start.5 = ((f32[16,1,2048]{2,1,0:T(1,128)}), f32[16,1,2048]{2,1,0:T(1,128)S(1)}, u32[]{:S(2)}, u32[]{:S(2)}) async-start(f32[16,1,2048]{2,1,0:T(1,128)} %broadcast_in_dim.100), calls=%async_computation.5 | async-start | bytes 262144 | tf_op jit(solution)/shard_map/all_to_all | solution.py:366
  193.0 3.5 collective-permute-start.4
  228.1 2.5 collective-permute-start
  239.0 7.3 %collective-permute-start.5 = (f32[256,1024]{1,0:T(8,128)S(1)}, f32[256,1024]{1,0:T(8,128)S(1)}, u32[]{:S(2)}, u32[]{:S(2)}) collective-permute-start(f32[256,1024]{1,0:T(8,128)S(1)} %get-tuple-element.86), channel_id=1, source_target_pairs={{0,2},{2,0},{4,6},{6,4},{8,10},{10,8},{12,14},{14,12},{16,18},{18,... | collective-permute-start | bytes 3145736 | tf_op jit(solution)/shard_map/ppermute | solution.py:354
  246.2 7.2 %collective-permute-start.6 = (f32[256,1024]{1,0:T(8,128)S(1)}, f32[256,1024]{1,0:T(8,128)S(1)}, u32[]{:S(2)}, u32[]{:S(2)}) collective-permute-start(f32[256,1024]{1,0:T(8,128)S(1)} %get-tuple-element.88), channel_id=1, source_target_pairs={{0,2},{2,0},{4,6},{6,4},{8,10},{10,8},{12,14},{14,12},{16,18},{18,... | collective-permute-start | bytes 3145736 | tf_op jit(solution)/shard_map/ppermute | solution.py:354
  251.8 13.3 %collective-permute-start.7 = (f32[256,1024]{1,0:T(8,128)S(1)}, f32[256,1024]{1,0:T(8,128)S(1)}, u32[]{:S(2)}, u32[]{:S(2)}) collective-permute-start(f32[256,1024]{1,0:T(8,128)S(1)} %get-tuple-element.90), channel_id=1, source_target_pairs={{0,2},{2,8},{4,6},{6,0},{8,10},{10,16},{12,14},{14,4},{16,18},{18,... | collective-permute-start | bytes 3145736 | tf_op jit(solution)/shard_map/ppermute | solution.py:482
  253.4 14.5 %collective-permute-start.8 = (f32[256,1024]{1,0:T(8,128)S(1)}, f32[256,1024]{1,0:T(8,128)S(1)}, u32[]{:S(2)}, u32[]{:S(2)}) collective-permute-start(f32[256,1024]{1,0:T(8,128)S(1)} %get-tuple-element.91), channel_id=1, source_target_pairs={{0,6},{2,0},{4,14},{6,4},{8,2},{10,8},{12,22},{14,12},{16,10},{18,... | collective-permute-start | bytes 3145736 | tf_op jit(solution)/shard_map/ppermute | solution.py:483
  258.9 20.3 %collective-permute-start.10 = (f32[256,1024]{1,0:T(8,128)S(1)}, f32[256,1024]{1,0:T(8,128)S(1)}, u32[]{:S(2)}, u32[]{:S(2)}) collective-permute-start(f32[256,1024]{1,0:T(8,128)S(1)} %get-tuple-element.94), channel_id=1, source_target_pairs={{0,6},{2,0},{4,14},{6,4},{8,2},{10,8},{12,22},{14,12},{16,10},{18,... | collective-permute-start | bytes 3145736 | tf_op jit(solution)/shard_map/ppermute | solution.py:483
  259.7 19.5 %collective-permute-start.9 = (f32[256,1024]{1,0:T(8,128)S(1)}, f32[256,1024]{1,0:T(8,128)S(1)}, u32[]{:S(2)}, u32[]{:S(2)}) collective-permute-start(f32[256,1024]{1,0:T(8,128)S(1)} %get-tuple-element.93), channel_id=1, source_target_pairs={{0,2},{2,8},{4,6},{6,0},{8,10},{10,16},{12,14},{14,4},{16,18},{18,... | collective-permute-start | bytes 3145736 | tf_op jit(solution)/shard_map/ppermute | solution.py:482
  273.5 14.2 %collective-permute-start.11 = (f32[256,1024]{1,0:T(8,128)S(1)}, f32[256,1024]{1,0:T(8,128)S(1)}, u32[]{:S(2)}, u32[]{:S(2)}) collective-permute-start(f32[256,1024]{1,0:T(8,128)S(1)} %get-tuple-element.96), channel_id=1, source_target_pairs={{0,2},{2,8},{4,6},{6,0},{8,10},{10,16},{12,14},{14,4},{16,18},{18,... | collective-permute-start | bytes 3145736 | tf_op jit(solution)/shard_map/ppermute | solution.py:482
  273.5 16.9 %collective-permute-start.12 = (f32[256,1024]{1,0:T(8,128)S(1)}, f32[256,1024]{1,0:T(8,128)S(1)}, u32[]{:S(2)}, u32[]{:S(2)}) collective-permute-start(f32[256,1024]{1,0:T(8,128)S(1)} %get-tuple-element.97), channel_id=1, source_target_pairs={{0,6},{2,0},{4,14},{6,4},{8,2},{10,8},{12,22},{14,12},{16,10},{18,... | collective-permute-start | bytes 3145736 | tf_op jit(solution)/shard_map/ppermute | solution.py:483
  279.2 11.2 %slice-start = ((s8[12582912]{0:T(1024)(128)(4,1)}), s8[4194304]{0:T(1024)(128)(4,1)S(1)}, s32[]{:S(2)}) async-start(s8[12582912]{0:T(1024)(128)(4,1)} %bitcast.22), calls=%async_computation.7 | async-start | bytes 8388608
  279.2 11.2 %slice-start.1 = ((s8[12582912]{0:T(1024)(128)(4,1)}), s8[4194304]{0:T(1024)(128)(4,1)S(1)}, s32[]{:S(2)}) async-start(s8[12582912]{0:T(1024)(128)(4,1)} %bitcast.22), calls=%async_computation.8 | async-start | bytes 8388608
  279.2 11.2 %slice-start.2 = ((s8[12582912]{0:T(1024)(128)(4,1)}), s8[4194304]{0:T(1024)(128)(4,1)S(1)}, s32[]{:S(2)}) async-start(s8[12582912]{0:T(1024)(128)(4,1)} %bitcast.22), calls=%async_computation.9 | async-start | bytes 8388608
  285.7 13.3 %collective-permute-start.13 = (f32[256,1024]{1,0:T(8,128)}, f32[256,1024]{1,0:T(8,128)S(1)}, u32[]{:S(2)}, u32[]{:S(2)}) collective-permute-start(f32[256,1024]{1,0:T(8,128)} %get-tuple-element.99), channel_id=1, source_target_pairs={{0,2},{2,8},{4,6},{6,0},{8,10},{10,16},{12,14},{14,4},{16,18},{18,... | collective-permute-start | bytes 3145736 | tf_op jit(solution)/shard_map/ppermute | solution.py:482
  285.7 16.0 %collective-permute-start.14 = (f32[256,1024]{1,0:T(8,128)}, f32[256,1024]{1,0:T(8,128)S(1)}, u32[]{:S(2)}, u32[]{:S(2)}) collective-permute-start(f32[256,1024]{1,0:T(8,128)} %get-tuple-element.100), channel_id=1, source_target_pairs={{0,6},{2,0},{4,14},{6,4},{8,2},{10,8},{12,22},{14,12},{16,10},{18,... | collective-permute-start | bytes 3145736 | tf_op jit(solution)/shard_map/ppermute | solution.py:483
  290.4 11.2 %slice-start.3 = ((s8[12582912]{0:T(1024)(128)(4,1)}), s8[4194304]{0:T(1024)(128)(4,1)S(1)}, s32[]{:S(2)}) async-start(s8[12582912]{0:T(1024)(128)(4,1)} %bitcast.24), calls=%async_computation.10 | async-start | bytes 8388608
  290.4 11.2 %slice-start.4 = ((s8[12582912]{0:T(1024)(128)(4,1)}), s8[4194304]{0:T(1024)(128)(4,1)S(1)}, s32[]{:S(2)}) async-start(s8[12582912]{0:T(1024)(128)(4,1)} %bitcast.24), calls=%async_computation.11 | async-start | bytes 8388608
  296.3 13.8 %collective-permute-start.15 = (f32[256,1024]{1,0:T(8,128)S(1)}, f32[256,1024]{1,0:T(8,128)S(1)}, u32[]{:S(2)}, u32[]{:S(2)}) collective-permute-start(f32[256,1024]{1,0:T(8,128)S(1)} %get-tuple-element.102), channel_id=1, source_target_pairs={{0,2},{2,8},{4,6},{6,0},{8,10},{10,16},{12,14},{14,4},{16,18},{18,... | collective-permute-start | bytes 3145736 | tf_op jit(solution)/shard_map/ppermute | solution.py:482
  296.4 16.5 %collective-permute-start.16 = (f32[256,1024]{1,0:T(8,128)S(1)}, f32[256,1024]{1,0:T(8,128)S(1)}, u32[]{:S(2)}, u32[]{:S(2)}) collective-permute-start(f32[256,1024]{1,0:T(8,128)S(1)} %get-tuple-element.103), channel_id=1, source_target_pairs={{0,6},{2,0},{4,14},{6,4},{8,2},{10,8},{12,22},{14,12},{16,10},{18,... | collective-permute-start | bytes 3145736 | tf_op jit(solution)/shard_map/ppermute | solution.py:483
  301.7 11.2 %slice-start.6 = ((s8[12582912]{0:T(1024)(128)(4,1)}), s8[4194304]{0:T(1024)(128)(4,1)S(1)}, s32[]{:S(2)}) async-start(s8[12582912]{0:T(1024)(128)(4,1)} %bitcast.26), calls=%async_computation.13 | async-start | bytes 8388608
  301.7 11.2 %slice-start.7 = ((s8[12582912]{0:T(1024)(128)(4,1)}), s8[4194304]{0:T(1024)(128)(4,1)S(1)}, s32[]{:S(2)}) async-start(s8[12582912]{0:T(1024)(128)(4,1)} %bitcast.26), calls=%async_computation.14 | async-start | bytes 8388608
  307.6 13.8 %collective-permute-start.17 = (f32[256,1024]{1,0:T(8,128)S(1)}, f32[256,1024]{1,0:T(8,128)S(1)}, u32[]{:S(2)}, u32[]{:S(2)}) collective-permute-start(f32[256,1024]{1,0:T(8,128)S(1)} %get-tuple-element.105), channel_id=1, source_target_pairs={{0,2},{2,8},{4,6},{6,0},{8,10},{10,16},{12,14},{14,4},{16,18},{18,... | collective-permute-start | bytes 3145736 | tf_op jit(solution)/shard_map/ppermute | solution.py:482
  307.6 16.5 %collective-permute-start.18 = (f32[256,1024]{1,0:T(8,128)S(1)}, f32[256,1024]{1,0:T(8,128)S(1)}, u32[]{:S(2)}, u32[]{:S(2)}) collective-permute-start(f32[256,1024]{1,0:T(8,128)S(1)} %get-tuple-element.106), channel_id=1, source_target_pairs={{0,6},{2,0},{4,14},{6,4},{8,2},{10,8},{12,22},{14,12},{16,10},{18,... | collective-permute-start | bytes 3145736 | tf_op jit(solution)/shard_map/ppermute | solution.py:483
  312.9 11.2 %slice-start.9 = ((s8[12582912]{0:T(1024)(128)(4,1)}), s8[4194304]{0:T(1024)(128)(4,1)S(1)}, s32[]{:S(2)}) async-start(s8[12582912]{0:T(1024)(128)(4,1)} %bitcast.28), calls=%async_computation.16 | async-start | bytes 8388608
  312.9 11.2 %slice-start.10 = ((s8[12582912]{0:T(1024)(128)(4,1)}), s8[4194304]{0:T(1024)(128)(4,1)S(1)}, s32[]{:S(2)}) async-start(s8[12582912]{0:T(1024)(128)(4,1)} %bitcast.28), calls=%async_computation.17 | async-start | bytes 8388608
  318.8 13.8 %collective-permute-start.19 = (f32[256,1024]{1,0:T(8,128)S(1)}, f32[256,1024]{1,0:T(8,128)S(1)}, u32[]{:S(2)}, u32[]{:S(2)}) collective-permute-start(f32[256,1024]{1,0:T(8,128)S(1)} %get-tuple-element.108), channel_id=1, source_target_pairs={{0,2},{2,8},{4,6},{6,0},{8,10},{10,16},{12,14},{14,4},{16,18},{18,... | collective-permute-start | bytes 3145736 | tf_op jit(solution)/shard_map/ppermute | solution.py:482
  318.8 16.5 %collective-permute-start.20 = (f32[256,1024]{1,0:T(8,128)S(1)}, f32[256,1024]{1,0:T(8,128)S(1)}, u32[]{:S(2)}, u32[]{:S(2)}) collective-permute-start(f32[256,1024]{1,0:T(8,128)S(1)} %get-tuple-element.109), channel_id=1, source_target_pairs={{0,6},{2,0},{4,14},{6,4},{8,2},{10,8},{12,22},{14,12},{16,10},{18,... | collective-permute-start | bytes 3145736 | tf_op jit(solution)/shard_map/ppermute | solution.py:483
  324.1 11.2 %slice-start.12 = ((s8[12582912]{0:T(1024)(128)(4,1)}), s8[4194304]{0:T(1024)(128)(4,1)S(1)}, s32[]{:S(2)}) async-start(s8[12582912]{0:T(1024)(128)(4,1)} %bitcast.30), calls=%async_computation.19 | async-start | bytes 8388608
  330.0 13.8 %collective-permute-start.21 = (f32[256,1024]{1,0:T(8,128)S(1)}, f32[256,1024]{1,0:T(8,128)S(1)}, u32[]{:S(2)}, u32[]{:S(2)}) collective-permute-start(f32[256,1024]{1,0:T(8,128)S(1)} %get-tuple-element.111), channel_id=1, source_target_pairs={{0,2},{2,8},{4,6},{6,0},{8,10},{10,16},{12,14},{14,4},{16,18},{18,... | collective-permute-start | bytes 3145736 | tf_op jit(solution)/shard_map/ppermute | solution.py:482
  330.1 16.5 %collective-permute-start.22 = (f32[256,1024]{1,0:T(8,128)S(1)}, f32[256,1024]{1,0:T(8,128)S(1)}, u32[]{:S(2)}, u32[]{:S(2)}) collective-permute-start(f32[256,1024]{1,0:T(8,128)S(1)} %get-tuple-element.112), channel_id=1, source_target_pairs={{0,6},{2,0},{4,14},{6,4},{8,2},{10,8},{12,22},{14,12},{16,10},{18,... | collective-permute-start | bytes 3145736 | tf_op jit(solution)/shard_map/ppermute | solution.py:483
  335.4 11.2 %slice-start.15 = ((s8[12582912]{0:T(1024)(128)(4,1)}), s8[4194304]{0:T(1024)(128)(4,1)S(1)}, s32[]{:S(2)}) async-start(s8[12582912]{0:T(1024)(128)(4,1)} %bitcast.32), calls=%async_computation.22 | async-start | bytes 8388608
  341.2 13.8 %collective-permute-start.23 = (f32[256,1024]{1,0:T(8,128)S(1)}, f32[256,1024]{1,0:T(8,128)S(1)}, u32[]{:S(2)}, u32[]{:S(2)}) collective-permute-start(f32[256,1024]{1,0:T(8,128)S(1)} %get-tuple-element.114), channel_id=1, source_target_pairs={{0,2},{2,8},{4,6},{6,0},{8,10},{10,16},{12,14},{14,4},{16,18},{18,... | collective-permute-start | bytes 3145736 | tf_op jit(solution)/shard_map/ppermute | solution.py:482
  341.3 16.5 %collective-permute-start.24 = (f32[256,1024]{1,0:T(8,128)S(1)}, f32[256,1024]{1,0:T(8,128)S(1)}, u32[]{:S(2)}, u32[]{:S(2)}) collective-permute-start(f32[256,1024]{1,0:T(8,128)S(1)} %get-tuple-element.115), channel_id=1, source_target_pairs={{0,6},{2,0},{4,14},{6,4},{8,2},{10,8},{12,22},{14,12},{16,10},{18,... | collective-permute-start | bytes 3145736 | tf_op jit(solution)/shard_map/ppermute | solution.py:483
  346.6 11.2 %slice-start.18 = ((s8[12582912]{0:T(1024)(128)(4,1)}), s8[4194304]{0:T(1024)(128)(4,1)S(1)}, s32[]{:S(2)}) async-start(s8[12582912]{0:T(1024)(128)(4,1)} %bitcast.34), calls=%async_computation.25 | async-start | bytes 8388608
  346.6 11.2 %slice-start.19 = ((s8[12582912]{0:T(1024)(128)(4,1)}), s8[4194304]{0:T(1024)(128)(4,1)S(1)}, s32[]{:S(2)}) async-start(s8[12582912]{0:T(1024)(128)(4,1)} %bitcast.34), calls=%async_computation.26 | async-start | bytes 8388608
  352.5 13.8 %collective-permute-start.25 = (f32[256,1024]{1,0:T(8,128)S(1)}, f32[256,1024]{1,0:T(8,128)S(1)}, u32[]{:S(2)}, u32[]{:S(2)}) collective-permute-start(f32[256,1024]{1,0:T(8,128)S(1)} %get-tuple-element.117), channel_id=1, source_target_pairs={{0,2},{2,8},{4,6},{6,0},{8,10},{10,16},{12,14},{14,4},{16,18},{18,... | collective-permute-start | bytes 3145736 | tf_op jit(solution)/shard_map/ppermute | solution.py:482
  352.5 16.5 %collective-permute-start.26 = (f32[256,1024]{1,0:T(8,128)S(1)}, f32[256,1024]{1,0:T(8,128)S(1)}, u32[]{:S(2)}, u32[]{:S(2)}) collective-permute-start(f32[256,1024]{1,0:T(8,128)S(1)} %get-tuple-element.118), channel_id=1, source_target_pairs={{0,6},{2,0},{4,14},{6,4},{8,2},{10,8},{12,22},{14,12},{16,10},{18,... | collective-permute-start | bytes 3145736 | tf_op jit(solution)/shard_map/ppermute | solution.py:483
  357.8 11.2 %slice-start.21 = ((s8[12582912]{0:T(1024)(128)(4,1)}), s8[4194304]{0:T(1024)(128)(4,1)S(1)}, s32[]{:S(2)}) async-start(s8[12582912]{0:T(1024)(128)(4,1)} %bitcast.36), calls=%async_computation.28 | async-start | bytes 8388608
  357.9 11.2 %slice-start.22 = ((s8[12582912]{0:T(1024)(128)(4,1)}), s8[4194304]{0:T(1024)(128)(4,1)S(1)}, s32[]{:S(2)}) async-start(s8[12582912]{0:T(1024)(128)(4,1)} %bitcast.36), calls=%async_computation.29 | async-start | bytes 8388608
  363.7 13.8 %collective-permute-start.27 = (f32[256,1024]{1,0:T(8,128)S(1)}, f32[256,1024]{1,0:T(8,128)S(1)}, u32[]{:S(2)}, u32[]{:S(2)}) collective-permute-start(f32[256,1024]{1,0:T(8,128)S(1)} %get-tuple-element.120), channel_id=1, source_target_pairs={{0,2},{2,8},{4,6},{6,0},{8,10},{10,16},{12,14},{14,4},{16,18},{18,... | collective-permute-start | bytes 3145736 | tf_op jit(solution)/shard_map/ppermute | solution.py:482
  363.8 16.5 %collective-permute-start.28 = (f32[256,1024]{1,0:T(8,128)S(1)}, f32[256,1024]{1,0:T(8,128)S(1)}, u32[]{:S(2)}, u32[]{:S(2)}) collective-permute-start(f32[256,1024]{1,0:T(8,128)S(1)} %get-tuple-element.121), channel_id=1, source_target_pairs={{0,6},{2,0},{4,14},{6,4},{8,2},{10,8},{12,22},{14,12},{16,10},{18,... | collective-permute-start | bytes 3145736 | tf_op jit(solution)/shard_map/ppermute | solution.py:483
  369.1 11.2 %slice-start.24 = ((s8[12582912]{0:T(1024)(128)(4,1)}), s8[4194304]{0:T(1024)(128)(4,1)S(1)}, s32[]{:S(2)}) async-start(s8[12582912]{0:T(1024)(128)(4,1)} %bitcast.38), calls=%async_computation.31 | async-start | bytes 8388608
  375.0 13.8 %collective-permute-start.29 = (f32[256,1024]{1,0:T(8,128)S(1)}, f32[256,1024]{1,0:T(8,128)S(1)}, u32[]{:S(2)}, u32[]{:S(2)}) collective-permute-start(f32[256,1024]{1,0:T(8,128)S(1)} %get-tuple-element.123), channel_id=1, source_target_pairs={{0,2},{2,8},{4,6},{6,0},{8,10},{10,16},{12,14},{14,4},{16,18},{18,... | collective-permute-start | bytes 3145736 | tf_op jit(solution)/shard_map/ppermute | solution.py:482
  375.0 16.2 %collective-permute-start.30 = (f32[256,1024]{1,0:T(8,128)S(1)}, f32[256,1024]{1,0:T(8,128)S(1)}, u32[]{:S(2)}, u32[]{:S(2)}) collective-permute-start(f32[256,1024]{1,0:T(8,128)S(1)} %get-tuple-element.124), channel_id=1, source_target_pairs={{0,6},{2,0},{4,14},{6,4},{8,2},{10,8},{12,22},{14,12},{16,10},{18,... | collective-permute-start | bytes 3145736 | tf_op jit(solution)/shard_map/ppermute | solution.py:483
  397.5 19.3 %collective-permute-start.34 = (f32[256,1024]{1,0:T(8,128)}, f32[256,1024]{1,0:T(8,128)}, u32[]{:S(2)}, u32[]{:S(2)}) collective-permute-start(f32[256,1024]{1,0:T(8,128)} %get-tuple-element.131), channel_id=1, source_target_pairs={{0,2},{2,8},{4,6},{6,0},{8,10},{10,16},{12,14},{14,4},{16,18},{18,... | collective-permute-start | bytes 3145736 | tf_op jit(solution)/shard_map/ppermute | solution.py:482
  397.5 19.3 %collective-permute-start.35 = (f32[256,1024]{1,0:T(8,128)}, f32[256,1024]{1,0:T(8,128)}, u32[]{:S(2)}, u32[]{:S(2)}) collective-permute-start(f32[256,1024]{1,0:T(8,128)} %get-tuple-element.132), channel_id=1, source_target_pairs={{0,6},{2,0},{4,14},{6,4},{8,2},{10,8},{12,22},{14,12},{16,10},{18,... | collective-permute-start | bytes 3145736 | tf_op jit(solution)/shard_map/ppermute | solution.py:483
  398.0 22.8 %collective-permute-start.32 = (f32[256,1024]{1,0:T(8,128)}, f32[256,1024]{1,0:T(8,128)}, u32[]{:S(2)}, u32[]{:S(2)}) collective-permute-start(f32[256,1024]{1,0:T(8,128)} %get-tuple-element.128), channel_id=1, source_target_pairs={{0,2},{2,8},{4,6},{6,0},{8,10},{10,16},{12,14},{14,4},{16,18},{18,... | collective-permute-start | bytes 3145736 | tf_op jit(solution)/shard_map/ppermute | solution.py:482
  399.3 24.0 %collective-permute-start.33 = (f32[256,1024]{1,0:T(8,128)}, f32[256,1024]{1,0:T(8,128)}, u32[]{:S(2)}, u32[]{:S(2)}) collective-permute-start(f32[256,1024]{1,0:T(8,128)} %get-tuple-element.129), channel_id=1, source_target_pairs={{0,6},{2,0},{4,14},{6,4},{8,2},{10,8},{12,22},{14,12},{16,10},{18,... | collective-permute-start | bytes 3145736 | tf_op jit(solution)/shard_map/ppermute | solution.py:483
  406.8 7.3 %collective-permute-start.31 = (f32[192,256]{0,1:T(8,128)S(1)}, f32[192,256]{0,1:T(8,128)S(1)}, u32[]{:S(2)}, u32[]{:S(2)}) collective-permute-start(f32[192,256]{0,1:T(8,128)S(1)} %copy.106), channel_id=1, source_target_pairs={{0,1},{1,0},{2,3},{3,2},{4,5},{5,4},{6,7},{7,6},{8,9},{9,8},{10,11... | collective-permute-start | bytes 589832 | tf_op jit(solution)/shard_map/ppermute | solution.py:354
  410.0 13.3 %copy-start.15 = (f32[2048]{0:T(1024)S(1)}, f32[2048]{0:T(1024)}, u32[]{:S(2)}) copy-start(f32[2048]{0:T(1024)} %param.12) | copy-start | bytes 24580
  (30 other events, 203.4 us)
Sparse Core Ops, SparseCore 0:
  11.3 183.1 all-gather.1
where the time goes:
time: 444 us; the launch traced here: 438 us
  Pallas kernels  174 us (39%)
  waiting for transfers between devices  114 us (26%)
  local copies, waits for them, and re-layouts  57.2 us (13%)
  starting transfers between devices  43 us (10%)
  blocking collectives  29.6 us (7%)
  between operations  15.4 us (3%)
  other arithmetic  5.41 us (1%)
    pallas_call x17, Pallas kernels, grad_step(): pl.pallas_call(lambda *refs: grad_kernel(*refs, blocks=blocks, arrivals=l...  94.9 us
    unnamed x107, local copies, waits for them, and re-layouts  50.6 us
    ppermute x14, waiting for transfers between devices, body(): lax.ppermute(second, 'dp', behind)  37.8 us
    ppermute x14, waiting for transfers between devices, body(): lax.ppermute(first, 'dp', ahead)  27.8 us
    pallas_call x3, Pallas kernels, column_pass(): pl.pallas_call(lambda *refs: column_kernel(*refs, unroll=min(16, shard //...  21.6 us
    pallas_call x1, Pallas kernels, student_pass(): pl.pallas_call(student_kernel, grid=(rows // block,), in_specs=[pl.BlockS...  20.8 us
    pallas_call x3, Pallas kernels, row_pass(): pl.pallas_call(lambda *refs: row_kernel(*refs, unroll=min(16, block // LA...  19.3 us
    all_to_all x2, waiting for transfers between devices, column_total(): lax.all_to_all(x, 'dp', 0, 0, tiled=True)  18.4 us
  transfers between devices with their start and end apart: 41, of which 35 were waited for; matrix products, arithmetic and copies ran while one was open for 2% of the time, Pallas kernels for 32%

commit v1 on v0

--- a/solution.py
+++ b/solution.py
@@ -17,12 +17,13 @@
 LANES = 128
 GROUP = 16
 VMEM_LIMIT = 20 * 1024 * 1024
+STUDENT_LIMIT = 44 * 1024 * 1024
 F32 = jnp.float32
 BF16 = jnp.bfloat16
 
 
-def params():
-    return pltpu.CompilerParams(vmem_limit_bytes=VMEM_LIMIT)
+def params(limit=VMEM_LIMIT):
+    return pltpu.CompilerParams(vmem_limit_bytes=limit)
 
 
 def split(x):
@@ -71,7 +72,7 @@
         grid=(tokens // rows,),
         in_specs=[pl.BlockSpec((rows, width), lambda i: (i, 0))],
         out_specs=[spec, spec, pl.BlockSpec((rows, width), lambda i: (i, 0))],
-        out_shape=[shape, shape, jax.ShapeDtypeStruct(teacher.shape, teacher.dtype)],
+        out_shape=[shape, shape, pltpu.VMEM(teacher.shape, teacher.dtype)],
         compiler_params=params(),
         name="teacher_stats",
     )(teacher)
@@ -178,35 +179,41 @@
     return jnp.concatenate([hi, hi, lo], axis=axis)
 
 
-def student_kernel(u_ref, w_ref, m_ref, s_ref):
-    tokens = u_ref.shape[1]
-
-    @pl.when(pl.program_id(0) == 0)
+def student_kernel(u_ref, w_ref, m_ref, s_ref, score_a, score_b):
+    rows, tokens = score_a.shape
+    step = pl.program_id(0)
+
+    def scores(start):
+        w_hi, w_lo = split(w_ref[start : start + rows, :])
+        return dot(parts_of_left(w_hi, w_lo, 1), u_ref[...])
+
+    def merge(logits, largest, total):
+        logits = logits.reshape(rows // 8, 8, tokens)
+        best = jnp.maximum(largest, jnp.max(logits, axis=0))
+        fresh = jnp.sum(jnp.exp2(logits - best[None]), axis=0)
+        return best, total * jnp.exp2(largest - best) + fresh
+
+    @pl.when(step == 0)
     def _():
         m_ref[...] = jnp.full_like(m_ref, -1e30)
         s_ref[...] = jnp.zeros_like(s_ref)
-
-    rows = w_ref.shape[0]
-    chunk = min(rows, 512)
-    largest, total = m_ref[...], s_ref[...]
-    scores = []
-    for r in range(0, rows, chunk):
-        w_hi, w_lo = split(w_ref[r : r + chunk, :])
-        logits = dot(parts_of_left(w_hi, w_lo, 1), u_ref[...])
-        scores.append(logits.reshape(chunk // 8, 8, tokens))
-    for logits in scores:
-        best = jnp.maximum(largest, jnp.max(logits, axis=0))
-        fresh = jnp.sum(jnp.exp2(logits - best[None]), axis=0)
-        total = total * jnp.exp2(largest - best) + fresh
-        largest = best
-    m_ref[...] = largest
-    s_ref[...] = total
+        score_b[...] = jnp.full_like(score_b, -1e30)
+
+    score_a[...] = scores(0)
+    stats = merge(score_b[...], m_ref[...], s_ref[...])
+    score_b[...] = scores(rows)
+    stats = merge(score_a[...], *stats)
+    m_ref[...], s_ref[...] = stats
+
+    @pl.when(step == pl.num_programs(0) - 1)
+    def _():
+        m_ref[...], s_ref[...] = merge(score_b[...], m_ref[...], s_ref[...])
 
 
 def student_pass(u_turned, protos):
     tokens = u_turned.shape[1]
     rows, depth = protos.shape
-    block = min(rows, 2048)
+    block = min(rows // 2, 4096)
     stat = pl.BlockSpec((8, tokens), lambda i: (0, 0))
     shape = jax.ShapeDtypeStruct((8, tokens), F32)
     return pl.pallas_call(
@@ -218,7 +225,8 @@
         ],
         out_specs=[stat, stat],
         out_shape=[shape, shape],
-        compiler_params=params(),
+        scratch_shapes=[pltpu.VMEM((block // 2, tokens), F32)] * 2,
+        compiler_params=params(STUDENT_LIMIT),
         name="student_stats",
     )(u_turned, protos)
 
@@ -303,47 +311,43 @@
     return parts, tok
 
 
-def proto_kernel(turned_a, turned_b, gain_a, gain_b, *refs):
-    grad_ref, gains_ref = refs[6:]
-    for i, (turned, gain) in enumerate(((turned_a, gain_a), (turned_b, gain_b))):
-        a, b, c = refs[3 * i : 3 * i + 3]
-        summed = a[...] + (b[...] + c[...])
-        protos = turned[...]
-        norm = jnp.sqrt(jnp.sum(protos * protos, axis=0, keepdims=True) + EPS)
-        unit = protos / norm
-        gain_dot = jnp.sum(unit * summed, axis=0, keepdims=True)
-        grad = gain[...] / (TEMP_S * norm) * (summed - unit * gain_dot)
-        grad_ref[i] = grad.T
-        gains_ref[i] = gain_dot / TEMP_S
-
-
-def proto_grads(prototypes, gain, parts):
+def proto_kernel(turned, gain, a, b, c, *refs):
+    grad_ref, gains_ref = refs[-2:]
+    summed = a[...] + (b[...] + c[...])
+    protos = turned[...]
+    norm = jnp.sqrt(jnp.sum(protos * protos, axis=0, keepdims=True) + EPS)
+    unit = protos / norm
+    gain_dot = jnp.sum(unit * summed, axis=0, keepdims=True)
+    grad = gain[...] / (TEMP_S * norm) * (summed - unit * gain_dot)
+    grad_ref[...] = grad.T
+    gains_ref[...] = gain_dot / TEMP_S
+
+
+def proto_grads(turned, gain_row, parts, half, done):
     depth, width = parts[0].shape
     block = min(width, 256)
     count = width // block
-    turned = prototypes.T
-    gain_row = gain[None, :]
-
-    def at(shape, sub):
-        return pl.BlockSpec(shape, lambda i: (0, sub * count + i))
-
-    grad, gains = pl.pallas_call(
+    return pl.pallas_call(
         proto_kernel,
         grid=(count,),
-        in_specs=[at((depth, block), 0), at((depth, block), 1), at((1, block), 0), at((1, block), 1)]
-        + [pl.BlockSpec((depth, block), lambda i: (0, i))] * 6,
+        in_specs=[
+            pl.BlockSpec((depth, block), lambda i: (0, half * count + i)),
+            pl.BlockSpec((1, block), lambda i: (0, half * count + i)),
+        ]
+        + [pl.BlockSpec((depth, block), lambda i: (0, i))] * 3
+        + [pl.BlockSpec(memory_space=pl.ANY)] * len(done),
         out_specs=[
-            pl.BlockSpec((2, block, depth), lambda i: (0, i, 0)),
-            pl.BlockSpec((2, 1, block), lambda i: (0, 0, i)),
+            pl.BlockSpec((block, depth), lambda i: (half * count + i, 0)),
+            pl.BlockSpec((1, block), lambda i: (0, half * count + i)),
         ],
         out_shape=[
-            jax.ShapeDtypeStruct((2, width, depth), F32),
-            jax.ShapeDtypeStruct((2, 1, width), F32),
+            jax.ShapeDtypeStruct((2 * width, depth), F32),
+            jax.ShapeDtypeStruct((1, 2 * width), F32),
         ],
+        input_output_aliases={5 + i: i for i in range(len(done))},
         compiler_params=params(),
         name="proto_grads",
-    )(turned, turned, gain_row, gain_row, *parts)
-    return grad.reshape(2 * width, depth), gains.reshape(2 * width)
+    )(turned, gain_row, *parts, *done)
 
 
 def halves(count):
@@ -475,17 +479,22 @@
         (part,), token_part = blocks_of((slot(half, sub),), [])
         crossed[sub] = swap(part, "dp", dp_count, 1)
     waiting = [[crossed[0]], [crossed[1]]]
+    mine = []
     for far in range(half - 1, 0, -1):
+        if len(mine) < 2 and far <= half // 2 + 1:
+            (part,), token_part = blocks_of((slot(0, len(mine)),), [])
+            mine.append(part)
         for sub in range(2):
             (first, second), token_part = blocks_of((slot(far, sub), slot(-far, sub)), waiting[sub])
             waiting[sub] = [
                 lax.ppermute(first, "dp", ahead),
                 lax.ppermute(second, "dp", behind),
             ]
-    mine, token_part = blocks_of((slot(0, 0), slot(0, 1)), [])
-    grad_proto, grad_gain = proto_grads(
-        prototypes, gain, [x for sub in range(2) for x in (mine[sub], *waiting[sub])]
-    )
+    turned, gain_row = prototypes.T, gain[None, :]
+    grads = ()
+    for sub in range(2):
+        grads = proto_grads(turned, gain_row, [mine[sub], *waiting[sub]], sub, grads)
+    grad_proto, grad_gain = grads[0], grads[1].reshape(shard)
 
     for distance in halves(proto_count):
         token_part = token_part + swap(token_part, "proto", proto_count, distance)

time: 444 us -> 427 us (0.962)
  waiting for transfers between devices: 114 us -> 97.2 us
  local copies, waits for them, and re-layouts: 57.2 us -> 48.6 us
  Pallas kernels: 174 us -> 180 us
    unnamed x107 -> x101, local copies, waits for them, and re-layouts: 50.6 us -> 40.3 us
    ppermute x14, waiting for transfers between devices: 27.8 us -> 18 us  [body(): lax.ppermute(first, 'dp', ahead)]
    ppermute x14, waiting for transfers between devices: 37.8 us -> 30.3 us  [body(): lax.ppermute(second, 'dp', behind)]
    pallas_call x17 -> x18, Pallas kernels: 94.9 us -> 96.2 us  [grad_step(): pl.pallas_call(lambda *refs: grad_kernel(*refs, blocks=blocks, arrivals=l...]
  transfers between devices with their start and end apart: 41 -> 41, of which waited for: 35 -> 30; matrix products, arithmetic and copies ran while one was open for 2% -> 3% of each run, Pallas kernels for 32% -> 36%
where the time goes in v1:
time: 427 us; the launch traced here: 420 us
  Pallas kernels  180 us (42%)
  waiting for transfers between devices  97.2 us (23%)
  local copies, waits for them, and re-layouts  48.6 us (11%)
  starting transfers between devices  42.1 us (10%)
  blocking collectives  29.6 us (7%)
  between operations  15.4 us (4%)
  other arithmetic  7.13 us (2%)
    pallas_call x18, Pallas kernels, grad_step(): pl.pallas_call(lambda *refs: grad_kernel(*refs, blocks=blocks, arrivals=l...  96.2 us
    unnamed x101, local copies, waits for them, and re-layouts  40.3 us
    ppermute x14, waiting for transfers between devices, body(): lax.ppermute(second, 'dp', behind)  30.3 us
    pallas_call x1, Pallas kernels, student_pass(): pl.pallas_call(student_kernel, grid=(rows // block,), in_specs=[pl.BlockS...  22.5 us
    pallas_call x3, Pallas kernels, column_pass(): pl.pallas_call(lambda *refs: column_kernel(*refs, unroll=min(16, shard //...  21.6 us
    pallas_call x3, Pallas kernels, row_pass(): pl.pallas_call(lambda *refs: row_kernel(*refs, unroll=min(16, block // LA...  19.3 us
    all_to_all x2, waiting for transfers between devices, column_total(): lax.all_to_all(x, 'dp', 0, 0, tiled=True)  18.4 us
    ppermute x14, waiting for transfers between devices, body(): lax.ppermute(first, 'dp', ahead)  18 us
  transfers between devices with their start and end apart: 41, of which 30 were waited for; matrix products, arithmetic and copies ran while one was open for 3% of the time, Pallas kernels for 36%

profile of v1, /device:TPU:1, one launch (start us, length us, event | category | flops | bytes accessed | tf_op | source)
XLA Modules:
  0.0 420.2 jit_solution(5507687067204741745)
XLA Ops:
  11.2 4.6 %copy-done.8 = bf16[192,32768]{1,0:T(8,128)(2,1)S(1)} copy-done((bf16[192,32768]{1,0:T(8,128)(2,1)S(1)}, bf16[192,32768]{1,0:T(8,128)(2,1)}, u32[]{:S(2)}) %copy-start.8) | copy-done | bytes 12582936
  15.8 12.1 %teacher_stats.1 = (f32[192,128]{1,0:T(8,128)S(1)}, f32[192,128]{1,0:T(8,128)S(1)}, bf16[192,32768]{1,0:T(8,128)(2,1)S(1)}) custom-call(bf16[192,32768]{1,0:T(8,128)(2,1)S(1)} %copy-done.8), custom_call_target="tpu_custom_call" | custom-call | tf_op jit(solution)/shard_map/teacher_stats/pallas_call | solution.py:70
  27.9 4.6 %copy-done.2 = bf16[192,32768]{1,0:T(8,128)(2,1)} copy-done((bf16[192,32768]{1,0:T(8,128)(2,1)}, bf16[192,32768]{1,0:T(8,128)(2,1)S(1)}, u32[]{:S(2)}) %copy-start.2) | copy-done | bytes 12582936
  32.7 2.1 collective-permute-start.1
  36.8 4.8 %copy-done.3 = bf16[192,32768]{1,0:T(8,128)(2,1)S(1)} copy-done((bf16[192,32768]{1,0:T(8,128)(2,1)S(1)}, bf16[192,32768]{1,0:T(8,128)(2,1)}, u32[]{:S(2)}) %copy-start.3) | copy-done | bytes 12582936
  41.6 5.7 %column_sums.3 = (f32[16,1,2048]{2,1,0:T(1,128)S(1)}, f32[192,128]{1,0:T(8,128)S(1)}) custom-call(bf16[192,32768]{1,0:T(8,128)(2,1)S(1)} %copy-done.3, f32[192,128]{1,0:T(8,128)S(1)} %broadcast_in_dim.94.refs_1_, f32[192,128]{1,0:T(8,128)S(1)} %iota.17.refs_2_, f32[192,128]{1,0:T(8,128)S(1)} %broadcast_in_dim.97.refs_3_), custom_call_target="tpu_custom_call" | custom-call | tf_op jit(solution)/shard_map/column_sums/pallas_call | solution.py:114
  47.3 16.6 %all_to_all.30 = f32[16,1,2048]{2,1,0:T(1,128)S(1)} all-to-all(f32[16,1,2048]{2,1,0:T(1,128)S(1)} %get-tuple-element.78), channel_id=1, replica_groups=mesh['dp'=16,'proto'=2] {'dp'}, dimensions={0} | all-to-all | bytes 262144 | tf_op jit(solution)/shard_map/all_to_all | solution.py:369
  64.1 13.0 %all_to_all.31.refs_2_ = f32[16,1,2048]{2,1,0:T(1,128)S(1)} all-to-all(f32[16,1,2048]{2,1,0:T(1,128)S(1)} %broadcast_in_dim.98), channel_id=1, replica_groups=mesh['dp'=16,'proto'=2] {'dp'}, dimensions={0} | all-to-all | bytes 262144 | tf_op jit(solution)/shard_map/all_to_all | solution.py:370
  77.0 4.9 %copy-done.4 = bf16[192,32768]{1,0:T(8,128)(2,1)S(1)} copy-done((bf16[192,32768]{1,0:T(8,128)(2,1)S(1)}, bf16[192,32768]{1,0:T(8,128)(2,1)}, u32[]{:S(2)}) %copy-start.4) | copy-done | bytes 12582936
  81.9 6.6 %row_sums.3 = (f32[192,128]{1,0:T(8,128)S(1)}, f32[1,32768]{1,0:T(1,128)}) custom-call(bf16[192,32768]{1,0:T(8,128)(2,1)S(1)} %copy-done.4, f32[192,128]{1,0:T(8,128)S(1)} %get-tuple-element.77.refs_1_, f32[16,1,2048]{2,1,0:T(1,128)S(1)} %all_to_all.31.refs_2_), custom_call_target="tpu_custom_call" | custom-call | tf_op jit(solution)/shard_map/row_sums/pallas_call | solution.py:160
  89.7 2.6 collective-permute-done.2.refs_3_
  92.4 8.0 %column_sums.4 = (f32[16,1,2048]{2,1,0:T(1,128)}, f32[192,128]{1,0:T(8,128)S(1)}) custom-call(bf16[192,32768]{1,0:T(8,128)(2,1)S(1)} %copy-done.4, f32[192,128]{1,0:T(8,128)S(1)} %get-tuple-element.77.refs_1_, f32[192,128]{1,0:T(8,128)S(1)} %get-tuple-element.79.refs_2_, f32[192,128]{1,0:T(8,128)S(1)} %collective-permute-done.2.refs_3_), custom_call_target="tpu_custom_call" | custom-call | tf_op jit(solution)/shard_map/column_sums/pallas_call | solution.py:114
  100.3 5.2 %all-to-all-start.2 = ((f32[16,1,2048]{2,1,0:T(1,128)}), f32[16,1,2048]{2,1,0:T(1,128)S(1)}, u32[]{:S(2)}, u32[]{:S(2)}) async-start(f32[16,1,2048]{2,1,0:T(1,128)} %get-tuple-element.81), calls=%async_computation.2 | async-start | bytes 262144 | tf_op jit(solution)/shard_map/all_to_all | solution.py:369
  105.6 9.2 %all-to-all-done.2 = f32[16,1,2048]{2,1,0:T(1,128)S(1)} async-done(((f32[16,1,2048]{2,1,0:T(1,128)}), f32[16,1,2048]{2,1,0:T(1,128)S(1)}, u32[]{:S(2)}, u32[]{:S(2)}) %all-to-all-start.2) | async-done | bytes 131104 | tf_op jit(solution)/shard_map/all_to_all | solution.py:369
  115.7 4.5 %all-to-all-start.3 = ((f32[16,1,2048]{2,1,0:T(1,128)}), f32[16,1,2048]{2,1,0:T(1,128)S(1)}, u32[]{:S(2)}, u32[]{:S(2)}) async-start(f32[16,1,2048]{2,1,0:T(1,128)} %broadcast_in_dim.99), calls=%async_computation.3 | async-start | bytes 262144 | tf_op jit(solution)/shard_map/all_to_all | solution.py:370
  121.9 7.7 %all-to-all-done.3.refs_2_ = f32[16,1,2048]{2,1,0:T(1,128)S(1)} async-done(((f32[16,1,2048]{2,1,0:T(1,128)}), f32[16,1,2048]{2,1,0:T(1,128)S(1)}, u32[]{:S(2)}, u32[]{:S(2)}) %all-to-all-start.3) | async-done | bytes 131104 | tf_op jit(solution)/shard_map/all_to_all | solution.py:370
  129.5 4.8 %copy-done.5 = bf16[192,32768]{1,0:T(8,128)(2,1)S(1)} copy-done((bf16[192,32768]{1,0:T(8,128)(2,1)S(1)}, bf16[192,32768]{1,0:T(8,128)(2,1)}, u32[]{:S(2)}) %copy-start.5) | copy-done | bytes 12582936
  134.3 6.6 %row_sums.4 = (f32[192,128]{1,0:T(8,128)S(1)}, f32[1,32768]{1,0:T(1,128)}) custom-call(bf16[192,32768]{1,0:T(8,128)(2,1)S(1)} %copy-done.5, f32[192,128]{1,0:T(8,128)S(1)} %get-tuple-element.80.refs_1_, f32[16,1,2048]{2,1,0:T(1,128)S(1)} %all-to-all-done.3.refs_2_), custom_call_target="tpu_custom_call" | custom-call | tf_op jit(solution)/shard_map/row_sums/pallas_call | solution.py:160
  142.1 2.6 collective-permute-done.3.refs_3_
  144.8 8.0 %column_sums.5 = (f32[16,1,2048]{2,1,0:T(1,128)}, f32[192,128]{1,0:T(8,128)S(1)}) custom-call(bf16[192,32768]{1,0:T(8,128)(2,1)S(1)} %copy-done.5, f32[192,128]{1,0:T(8,128)S(1)} %get-tuple-element.80.refs_1_, f32[192,128]{1,0:T(8,128)S(1)} %get-tuple-element.82.refs_2_, f32[192,128]{1,0:T(8,128)S(1)} %collective-permute-done.3.refs_3_), custom_call_target="tpu_custom_call" | custom-call | tf_op jit(solution)/shard_map/column_sums/pallas_call | solution.py:114
  152.7 5.3 %all-to-all-start.4 = ((f32[16,1,2048]{2,1,0:T(1,128)}), f32[16,1,2048]{2,1,0:T(1,128)S(1)}, u32[]{:S(2)}, u32[]{:S(2)}) async-start(f32[16,1,2048]{2,1,0:T(1,128)} %get-tuple-element.84), calls=%async_computation.4 | async-start | bytes 262144 | tf_op jit(solution)/shard_map/all_to_all | solution.py:369
  158.2 9.2 %all-to-all-done.4 = f32[16,1,2048]{2,1,0:T(1,128)S(1)} async-done(((f32[16,1,2048]{2,1,0:T(1,128)}), f32[16,1,2048]{2,1,0:T(1,128)S(1)}, u32[]{:S(2)}, u32[]{:S(2)}) %all-to-all-start.4) | async-done | bytes 131104 | tf_op jit(solution)/shard_map/all_to_all | solution.py:369
  168.2 4.8 %all-to-all-start.5 = ((f32[16,1,2048]{2,1,0:T(1,128)}), f32[16,1,2048]{2,1,0:T(1,128)S(1)}, u32[]{:S(2)}, u32[]{:S(2)}) async-start(f32[16,1,2048]{2,1,0:T(1,128)} %broadcast_in_dim.100), calls=%async_computation.5 | async-start | bytes 262144 | tf_op jit(solution)/shard_map/all_to_all | solution.py:370
  174.0 8.2 %all-to-all-done.5.refs_2_ = f32[16,1,2048]{2,1,0:T(1,128)S(1)} async-done(((f32[16,1,2048]{2,1,0:T(1,128)}), f32[16,1,2048]{2,1,0:T(1,128)S(1)}, u32[]{:S(2)}, u32[]{:S(2)}) %all-to-all-start.5) | async-done | bytes 131104 | tf_op jit(solution)/shard_map/all_to_all | solution.py:370
  182.2 4.6 %copy-done.6 = bf16[192,32768]{1,0:T(8,128)(2,1)S(1)} copy-done((bf16[192,32768]{1,0:T(8,128)(2,1)S(1)}, bf16[192,32768]{1,0:T(8,128)(2,1)}, u32[]{:S(2)}) %copy-start.6) | copy-done | bytes 12582936
  186.8 6.2 %row_sums.5 = (f32[192,128]{1,0:T(8,128)S(1)}, f32[1,32768]{1,0:T(1,128)S(1)}) custom-call(bf16[192,32768]{1,0:T(8,128)(2,1)S(1)} %copy-done.6, f32[192,128]{1,0:T(8,128)S(1)} %get-tuple-element.83.refs_1_, f32[16,1,2048]{2,1,0:T(1,128)S(1)} %all-to-all-done.5.refs_2_), custom_call_target="tpu_custom_call" | custom-call | tf_op jit(solution)/shard_map/row_sums/pallas_call | solution.py:160
  196.7 22.5 %student_stats.1 = (f32[8,192]{1,0:T(8,128)S(1)}, f32[8,192]{1,0:T(8,128)S(1)}) custom-call(bf16[768,192]{1,0:T(8,128)(2,1)S(1)} %get-tuple-element.149.u_ref, f32[32768,256]{1,0:T(8,128)} %all-gather.2.cloned.1.call-done.w_ref.refs_8_.refs_10_.refs_11_), custom_call_target="tpu_custom_call" | custom-call | tf_op jit(solution)/shard_map/student_stats/pallas_call | solution.py:219
  221.9 4.6 %copy-done.7 = bf16[192,32768]{1,0:T(8,128)(2,1)S(1)} copy-done((bf16[192,32768]{1,0:T(8,128)(2,1)S(1)}, bf16[192,32768]{1,0:T(8,128)(2,1)}, u32[]{:S(2)}) %copy-start.7) | copy-done | bytes 12582936
  226.5 3.7 grad_blocks.18
  230.2 3.6 collective-permute-start.5
  233.7 3.7 grad_blocks.19
  237.5 5.5 %grad_blocks.20 = (f32[256,1024]{1,0:T(8,128)S(1)}, f32[256,1024]{1,0:T(8,128)S(1)}, f32[192,256]{1,0:T(8,128)S(1)}) custom-call(s32[33]{0:T(128)S(1)} %dynamic-slice_bitcast_fusion.refs_0_, bf16[192,768]{1,0:T(8,128)(2,1)S(1)} %copy.110.refs_1_, bf16[256,576]{1,0:T(8,128)(2,1)S(1)} %pad_maximum_fusion.2.refs_2_, f32[192,128]{1,0:T(8,128)S(1)} %broadcast_in_dim.92.refs_3_, ...), custom_call_target="tpu_custom_call" | custom-call | tf_op jit(solution)/shard_map/grad_blocks/pallas_call | solution.py:293
  244.6 5.5 %grad_blocks.21 = (f32[256,1024]{1,0:T(8,128)S(1)}, f32[256,1024]{1,0:T(8,128)S(1)}, f32[192,256]{1,0:T(8,128)S(1)}) custom-call(s32[33]{0:T(128)S(1)} %dynamic-slice_bitcast_fusion.refs_0_, bf16[192,768]{1,0:T(8,128)(2,1)S(1)} %copy.110.refs_1_, bf16[256,576]{1,0:T(8,128)(2,1)S(1)} %pad_maximum_fusion.2.refs_2_, f32[192,128]{1,0:T(8,128)S(1)} %broadcast_in_dim.92.refs_3_, ...), custom_call_target="tpu_custom_call" | custom-call | tf_op jit(solution)/shard_map/grad_blocks/pallas_call | solution.py:293
  251.9 4.4 %collective-permute-done.7.refs_12_ = f32[256,1024]{1,0:T(8,128)S(1)} collective-permute-done((f32[256,1024]{1,0:T(8,128)S(1)}, f32[256,1024]{1,0:T(8,128)S(1)}, u32[]{:S(2)}, u32[]{:S(2)}) %collective-permute-start.7) | collective-permute-done | bytes 1048608 | tf_op jit(solution)/shard_map/ppermute | solution.py:490
  256.4 2.8 collective-permute-done.8.refs_13_
  259.1 5.5 %grad_blocks.22 = (f32[256,1024]{1,0:T(8,128)S(1)}, f32[256,1024]{1,0:T(8,128)S(1)}, f32[192,256]{1,0:T(8,128)S(1)}) custom-call(s32[33]{0:T(128)S(1)} %dynamic-slice_bitcast_fusion.refs_0_, bf16[192,768]{1,0:T(8,128)(2,1)S(1)} %copy.110.refs_1_, bf16[256,576]{1,0:T(8,128)(2,1)S(1)} %pad_maximum_fusion.2.refs_2_, f32[192,128]{1,0:T(8,128)S(1)} %broadcast_in_dim.92.refs_3_, ...), custom_call_target="tpu_custom_call" | custom-call | tf_op jit(solution)/shard_map/grad_blocks/pallas_call | solution.py:293
  265.4 2.2 collective-permute-done.9.refs_12_
  267.6 2.8 collective-permute-done.10.refs_13_
  270.4 5.5 %grad_blocks.23 = (f32[256,1024]{1,0:T(8,128)S(1)}, f32[256,1024]{1,0:T(8,128)S(1)}, f32[192,256]{1,0:T(8,128)S(1)}) custom-call(s32[33]{0:T(128)S(1)} %dynamic-slice_bitcast_fusion.refs_0_, bf16[192,768]{1,0:T(8,128)(2,1)S(1)} %copy.110.refs_1_, bf16[256,576]{1,0:T(8,128)(2,1)S(1)} %pad_maximum_fusion.2.refs_2_, f32[192,128]{1,0:T(8,128)S(1)} %broadcast_in_dim.92.refs_3_, ...), custom_call_target="tpu_custom_call" | custom-call | tf_op jit(solution)/shard_map/grad_blocks/pallas_call | solution.py:293
  276.4 3.7 grad_blocks.24
  281.6 5.5 %grad_blocks.25 = (f32[256,1024]{1,0:T(8,128)S(1)}, f32[256,1024]{1,0:T(8,128)S(1)}, f32[192,256]{1,0:T(8,128)S(1)}) custom-call(s32[33]{0:T(128)S(1)} %dynamic-slice_bitcast_fusion.refs_0_, bf16[192,768]{1,0:T(8,128)(2,1)S(1)} %copy.110.refs_1_, bf16[256,576]{1,0:T(8,128)(2,1)S(1)} %pad_maximum_fusion.2.refs_2_, f32[192,128]{1,0:T(8,128)S(1)} %broadcast_in_dim.92.refs_3_, ...), custom_call_target="tpu_custom_call" | custom-call | tf_op jit(solution)/shard_map/grad_blocks/pallas_call | solution.py:293
  287.7 2.4 collective-permute-done.13.refs_12_
  290.1 2.8 collective-permute-done.14.refs_13_
  292.8 5.5 %grad_blocks.26 = (f32[256,1024]{1,0:T(8,128)S(1)}, f32[256,1024]{1,0:T(8,128)S(1)}, f32[192,256]{1,0:T(8,128)S(1)}) custom-call(s32[33]{0:T(128)S(1)} %dynamic-slice_bitcast_fusion.refs_0_, bf16[192,768]{1,0:T(8,128)(2,1)S(1)} %copy.110.refs_1_, bf16[256,576]{1,0:T(8,128)(2,1)S(1)} %pad_maximum_fusion.2.refs_2_, f32[192,128]{1,0:T(8,128)S(1)} %broadcast_in_dim.92.refs_3_, ...), custom_call_target="tpu_custom_call" | custom-call | tf_op jit(solution)/shard_map/grad_blocks/pallas_call | solution.py:293
  298.9 3.7 grad_blocks.27
  304.1 5.8 %grad_blocks.28 = (f32[256,1024]{1,0:T(8,128)S(1)}, f32[256,1024]{1,0:T(8,128)S(1)}, f32[192,256]{1,0:T(8,128)S(1)}) custom-call(s32[33]{0:T(128)S(1)} %dynamic-slice_bitcast_fusion.refs_0_, bf16[192,768]{1,0:T(8,128)(2,1)S(1)} %copy.110.refs_1_, bf16[256,576]{1,0:T(8,128)(2,1)S(1)} %pad_maximum_fusion.2.refs_2_, f32[192,128]{1,0:T(8,128)S(1)} %broadcast_in_dim.92.refs_3_, ...), custom_call_target="tpu_custom_call" | custom-call | tf_op jit(solution)/shard_map/grad_blocks/pallas_call | solution.py:293
  312.5 2.8 collective-permute-done.18.refs_13_
  317.7 5.9 %grad_blocks.29 = (f32[256,1024]{1,0:T(8,128)S(1)}, f32[256,1024]{1,0:T(8,128)S(1)}, f32[192,256]{1,0:T(8,128)S(1)}) custom-call(s32[33]{0:T(128)S(1)} %dynamic-slice_bitcast_fusion.refs_0_, bf16[192,768]{1,0:T(8,128)(2,1)S(1)} %copy.110.refs_1_, bf16[256,576]{1,0:T(8,128)(2,1)S(1)} %pad_maximum_fusion.2.refs_2_, f32[192,128]{1,0:T(8,128)S(1)} %broadcast_in_dim.92.refs_3_, ...), custom_call_target="tpu_custom_call" | custom-call | tf_op jit(solution)/shard_map/grad_blocks/pallas_call | solution.py:293
  324.4 2.1 collective-permute-done.20.refs_13_
  326.6 5.8 %grad_blocks.30 = (f32[256,1024]{1,0:T(8,128)S(1)}, f32[256,1024]{1,0:T(8,128)S(1)}, f32[192,256]{1,0:T(8,128)S(1)}) custom-call(s32[33]{0:T(128)S(1)} %dynamic-slice_bitcast_fusion.refs_0_, bf16[192,768]{1,0:T(8,128)(2,1)S(1)} %copy.110.refs_1_, bf16[256,576]{1,0:T(8,128)(2,1)S(1)} %pad_maximum_fusion.2.refs_2_, f32[192,128]{1,0:T(8,128)S(1)} %broadcast_in_dim.92.refs_3_, ...), custom_call_target="tpu_custom_call" | custom-call | tf_op jit(solution)/shard_map/grad_blocks/pallas_call | solution.py:293
  333.0 2.4 collective-permute-done.21.refs_12_
  335.4 3.1 collective-permute-done.22.refs_13_
  338.5 5.8 %grad_blocks.31 = (f32[256,1024]{1,0:T(8,128)S(1)}, f32[256,1024]{1,0:T(8,128)S(1)}, f32[192,256]{1,0:T(8,128)S(1)}) custom-call(s32[33]{0:T(128)S(1)} %dynamic-slice_bitcast_fusion.refs_0_, bf16[192,768]{1,0:T(8,128)(2,1)S(1)} %copy.110.refs_1_, bf16[256,576]{1,0:T(8,128)(2,1)S(1)} %pad_maximum_fusion.2.refs_2_, f32[192,128]{1,0:T(8,128)S(1)} %broadcast_in_dim.92.refs_3_, ...), custom_call_target="tpu_custom_call" | custom-call | tf_op jit(solution)/shard_map/grad_blocks/pallas_call | solution.py:293
  346.6 3.1 collective-permute-done.24.refs_13_
  349.8 5.8 %grad_blocks.32 = (f32[256,1024]{1,0:T(8,128)S(1)}, f32[256,1024]{1,0:T(8,128)S(1)}, f32[192,256]{1,0:T(8,128)S(1)}) custom-call(s32[33]{0:T(128)S(1)} %dynamic-slice_bitcast_fusion.refs_0_, bf16[192,768]{1,0:T(8,128)(2,1)S(1)} %copy.110.refs_1_, bf16[256,576]{1,0:T(8,128)(2,1)S(1)} %pad_maximum_fusion.2.refs_2_, f32[192,128]{1,0:T(8,128)S(1)} %broadcast_in_dim.92.refs_3_, ...), custom_call_target="tpu_custom_call" | custom-call | tf_op jit(solution)/shard_map/grad_blocks/pallas_call | solution.py:293
  357.9 3.1 collective-permute-done.26.refs_13_
  361.0 6.5 %grad_blocks.33 = (f32[256,1024]{1,0:T(8,128)}, f32[256,1024]{1,0:T(8,128)}, f32[192,256]{1,0:T(8,128)S(1)}) custom-call(s32[33]{0:T(128)S(1)} %dynamic-slice_bitcast_fusion.refs_0_, bf16[192,768]{1,0:T(8,128)(2,1)S(1)} %copy.110.refs_1_, bf16[256,576]{1,0:T(8,128)(2,1)S(1)} %pad_maximum_fusion.2.refs_2_, f32[192,128]{1,0:T(8,128)S(1)} %broadcast_in_dim.92.refs_3_, ...), custom_call_target="tpu_custom_call" | custom-call | tf_op jit(solution)/shard_map/grad_blocks/pallas_call | solution.py:293
  369.1 3.1 collective-permute-done.28.refs_13_
  374.6 6.6 %grad_blocks.34 = (f32[256,1024]{1,0:T(8,128)}, f32[256,1024]{1,0:T(8,128)}, f32[192,256]{1,0:T(8,128)S(1)}) custom-call(s32[33]{0:T(128)S(1)} %dynamic-slice_bitcast_fusion.refs_0_, bf16[192,768]{1,0:T(8,128)(2,1)S(1)} %copy.110.refs_1_, bf16[256,576]{1,0:T(8,128)(2,1)S(1)} %pad_maximum_fusion.2.refs_2_, f32[192,128]{1,0:T(8,128)S(1)} %broadcast_in_dim.92.refs_3_, ...), custom_call_target="tpu_custom_call" | custom-call | tf_op jit(solution)/shard_map/grad_blocks/pallas_call | solution.py:293
  383.6 6.2 %grad_blocks.35 = (f32[256,1024]{1,0:T(8,128)}, f32[256,1024]{1,0:T(8,128)}, f32[192,256]{1,0:T(8,128)S(1)}) custom-call(s32[33]{0:T(128)S(1)} %dynamic-slice_bitcast_fusion.refs_0_, bf16[192,768]{1,0:T(8,128)(2,1)S(1)} %copy.110.refs_1_, bf16[256,576]{1,0:T(8,128)(2,1)S(1)} %pad_maximum_fusion.2.refs_2_, f32[192,128]{1,0:T(8,128)S(1)} %broadcast_in_dim.92.refs_3_, ...), custom_call_target="tpu_custom_call" | custom-call | tf_op jit(solution)/shard_map/grad_blocks/pallas_call | solution.py:293
  394.3 4.9 %collective-permute-done.31 = f32[192,256]{0,1:T(8,128)} collective-permute-done((f32[192,256]{0,1:T(8,128)}, f32[192,256]{0,1:T(8,128)}, u32[]{:S(2)}, u32[]{:S(2)}) %collective-permute-start.31) | collective-permute-done | bytes 196640 | tf_op jit(solution)/shard_map/ppermute | solution.py:358
  402.1 2.3 scatter_custom_fusion
  404.5 4.2 proto_grads.2
  408.7 4.2 proto_grads.3
  (209 shorter events, 53.0 us)
Async XLA Ops:
  7.2 113.6 %copy-start = (f32[1024,256]{1,0:T(8,128)S(1)}, f32[1024,256]{1,0:T(8,128)}, u32[]{:S(2)}) copy-start(f32[1024,256]{1,0:T(8,128)} %param.7) | copy-start | bytes 3145732
  7.2 189.5 %all-gather.2.cloned.1.call-start = ((), (), s32[]{:S(2)}) async-start(), calls=%async_computation.6 | async-start | bytes 35651584 | tf_op jit(solution)/shard_map/all_gather | solution.py:431
  32.7 3.5 collective-permute-start.1
  88.5 17.0 %copy-start.28 = (s32[3]{0:T(128)S(1)}, s32[3]{0:T(128)}, u32[]{:S(2)}) copy-start(s32[3]{0:T(128)} %param.8) | copy-start | bytes 40
  88.5 31.7 %copy-start.27 = (s32[192]{0:T(256)S(1)}, s32[192]{0:T(256)}, u32[]{:S(2)}) copy-start(s32[192]{0:T(256)} %param.9) | copy-start | bytes 2308
  88.5 3.9 collective-permute-start.2
  100.3 14.5 %all-to-all-start.2 = ((f32[16,1,2048]{2,1,0:T(1,128)}), f32[16,1,2048]{2,1,0:T(1,128)S(1)}, u32[]{:S(2)}, u32[]{:S(2)}) async-start(f32[16,1,2048]{2,1,0:T(1,128)} %get-tuple-element.81), calls=%async_computation.2 | async-start | bytes 262144 | tf_op jit(solution)/shard_map/all_to_all | solution.py:369
  115.7 13.9 %all-to-all-start.3 = ((f32[16,1,2048]{2,1,0:T(1,128)}), f32[16,1,2048]{2,1,0:T(1,128)S(1)}, u32[]{:S(2)}, u32[]{:S(2)}) async-start(f32[16,1,2048]{2,1,0:T(1,128)} %broadcast_in_dim.99), calls=%async_computation.3 | async-start | bytes 262144 | tf_op jit(solution)/shard_map/all_to_all | solution.py:370
  120.2 37.9 %copy-start.24 = (pred[192]{0:T(512)(128)(4,1)}, pred[192]{0:T(512)(128)(4,1)S(1)}, u32[]{:S(2)}) copy-start(pred[192]{0:T(512)(128)(4,1)S(1)} %get-tuple-element.143) | copy-start | bytes 580
  121.8 36.3 %copy-start.20 = (f32[192,256]{0,1:T(8,128)}, f32[192,256]{0,1:T(8,128)S(1)}, u32[]{:S(2)}) copy-start(f32[192,256]{0,1:T(8,128)S(1)} %copy.88) | copy-start | bytes 589828
  140.9 3.9 collective-permute-start.3
  142.1 16.0 %copy-start.22 = (f32[192]{0:T(256)}, f32[192]{0:T(256)S(1)}, u32[]{:S(2)}) copy-start(f32[192]{0:T(256)S(1)} %add_rsqrt_fusion) | copy-start | bytes 2308
  152.7 14.6 %all-to-all-start.4 = ((f32[16,1,2048]{2,1,0:T(1,128)}), f32[16,1,2048]{2,1,0:T(1,128)S(1)}, u32[]{:S(2)}, u32[]{:S(2)}) async-start(f32[16,1,2048]{2,1,0:T(1,128)} %get-tuple-element.84), calls=%async_computation.4 | async-start | bytes 262144 | tf_op jit(solution)/shard_map/all_to_all | solution.py:369
  168.2 14.0 %all-to-all-start.5 = ((f32[16,1,2048]{2,1,0:T(1,128)}), f32[16,1,2048]{2,1,0:T(1,128)S(1)}, u32[]{:S(2)}, u32[]{:S(2)}) async-start(f32[16,1,2048]{2,1,0:T(1,128)} %broadcast_in_dim.100), calls=%async_computation.5 | async-start | bytes 262144 | tf_op jit(solution)/shard_map/all_to_all | solution.py:370
  193.0 3.5 collective-permute-start.4
  219.2 2.5 collective-permute-start
  230.2 7.4 %collective-permute-start.5 = (f32[256,1024]{1,0:T(8,128)S(1)}, f32[256,1024]{1,0:T(8,128)S(1)}, u32[]{:S(2)}, u32[]{:S(2)}) collective-permute-start(f32[256,1024]{1,0:T(8,128)S(1)} %get-tuple-element.89), channel_id=1, source_target_pairs={{0,2},{2,0},{4,6},{6,4},{8,10},{10,8},{12,14},{14,12},{16,18},{18,... | collective-permute-start | bytes 3145736 | tf_op jit(solution)/shard_map/ppermute | solution.py:358
  237.4 7.2 %collective-permute-start.6 = (f32[256,1024]{1,0:T(8,128)S(1)}, f32[256,1024]{1,0:T(8,128)S(1)}, u32[]{:S(2)}, u32[]{:S(2)}) collective-permute-start(f32[256,1024]{1,0:T(8,128)S(1)} %get-tuple-element.91), channel_id=1, source_target_pairs={{0,2},{2,0},{4,6},{6,4},{8,10},{10,8},{12,14},{14,12},{16,18},{18,... | collective-permute-start | bytes 3145736 | tf_op jit(solution)/shard_map/ppermute | solution.py:358
  243.0 13.3 %collective-permute-start.7 = (f32[256,1024]{1,0:T(8,128)S(1)}, f32[256,1024]{1,0:T(8,128)S(1)}, u32[]{:S(2)}, u32[]{:S(2)}) collective-permute-start(f32[256,1024]{1,0:T(8,128)S(1)} %get-tuple-element.93), channel_id=1, source_target_pairs={{0,2},{2,8},{4,6},{6,0},{8,10},{10,16},{12,14},{14,4},{16,18},{18,... | collective-permute-start | bytes 3145736 | tf_op jit(solution)/shard_map/ppermute | solution.py:490
  244.6 14.5 %collective-permute-start.8 = (f32[256,1024]{1,0:T(8,128)S(1)}, f32[256,1024]{1,0:T(8,128)S(1)}, u32[]{:S(2)}, u32[]{:S(2)}) collective-permute-start(f32[256,1024]{1,0:T(8,128)S(1)} %get-tuple-element.94), channel_id=1, source_target_pairs={{0,6},{2,0},{4,14},{6,4},{8,2},{10,8},{12,22},{14,12},{16,10},{18,... | collective-permute-start | bytes 3145736 | tf_op jit(solution)/shard_map/ppermute | solution.py:491
  250.1 17.5 %collective-permute-start.9 = (f32[256,1024]{1,0:T(8,128)S(1)}, f32[256,1024]{1,0:T(8,128)S(1)}, u32[]{:S(2)}, u32[]{:S(2)}) collective-permute-start(f32[256,1024]{1,0:T(8,128)S(1)} %get-tuple-element.96), channel_id=1, source_target_pairs={{0,2},{2,8},{4,6},{6,0},{8,10},{10,16},{12,14},{14,4},{16,18},{18,... | collective-permute-start | bytes 3145736 | tf_op jit(solution)/shard_map/ppermute | solution.py:490
  251.9 18.5 %collective-permute-start.10 = (f32[256,1024]{1,0:T(8,128)S(1)}, f32[256,1024]{1,0:T(8,128)S(1)}, u32[]{:S(2)}, u32[]{:S(2)}) collective-permute-start(f32[256,1024]{1,0:T(8,128)S(1)} %get-tuple-element.97), channel_id=1, source_target_pairs={{0,6},{2,0},{4,14},{6,4},{8,2},{10,8},{12,22},{14,12},{16,10},{18,... | collective-permute-start | bytes 3145736 | tf_op jit(solution)/shard_map/ppermute | solution.py:491
  264.6 15.5 %collective-permute-start.11 = (f32[256,1024]{1,0:T(8,128)S(1)}, f32[256,1024]{1,0:T(8,128)S(1)}, u32[]{:S(2)}, u32[]{:S(2)}) collective-permute-start(f32[256,1024]{1,0:T(8,128)S(1)} %get-tuple-element.100), channel_id=1, source_target_pairs={{0,2},{2,8},{4,6},{6,0},{8,10},{10,16},{12,14},{14,4},{16,18},{18,... | collective-permute-start | bytes 3145736 | tf_op jit(solution)/shard_map/ppermute | solution.py:490
  264.7 16.9 %collective-permute-start.12 = (f32[256,1024]{1,0:T(8,128)S(1)}, f32[256,1024]{1,0:T(8,128)S(1)}, u32[]{:S(2)}, u32[]{:S(2)}) collective-permute-start(f32[256,1024]{1,0:T(8,128)S(1)} %get-tuple-element.101), channel_id=1, source_target_pairs={{0,6},{2,0},{4,14},{6,4},{8,2},{10,8},{12,22},{14,12},{16,10},{18,... | collective-permute-start | bytes 3145736 | tf_op jit(solution)/shard_map/ppermute | solution.py:491
  275.9 14.2 %collective-permute-start.13 = (f32[256,1024]{1,0:T(8,128)S(1)}, f32[256,1024]{1,0:T(8,128)S(1)}, u32[]{:S(2)}, u32[]{:S(2)}) collective-permute-start(f32[256,1024]{1,0:T(8,128)S(1)} %get-tuple-element.103), channel_id=1, source_target_pairs={{0,2},{2,8},{4,6},{6,0},{8,10},{10,16},{12,14},{14,4},{16,18},{18,... | collective-permute-start | bytes 3145736 | tf_op jit(solution)/shard_map/ppermute | solution.py:490
  275.9 16.9 %collective-permute-start.14 = (f32[256,1024]{1,0:T(8,128)S(1)}, f32[256,1024]{1,0:T(8,128)S(1)}, u32[]{:S(2)}, u32[]{:S(2)}) collective-permute-start(f32[256,1024]{1,0:T(8,128)S(1)} %get-tuple-element.104), channel_id=1, source_target_pairs={{0,6},{2,0},{4,14},{6,4},{8,2},{10,8},{12,22},{14,12},{16,10},{18,... | collective-permute-start | bytes 3145736 | tf_op jit(solution)/shard_map/ppermute | solution.py:491
  287.1 15.5 %collective-permute-start.15 = (f32[256,1024]{1,0:T(8,128)S(1)}, f32[256,1024]{1,0:T(8,128)S(1)}, u32[]{:S(2)}, u32[]{:S(2)}) collective-permute-start(f32[256,1024]{1,0:T(8,128)S(1)} %get-tuple-element.107), channel_id=1, source_target_pairs={{0,2},{2,8},{4,6},{6,0},{8,10},{10,16},{12,14},{14,4},{16,18},{18,... | collective-permute-start | bytes 3145736 | tf_op jit(solution)/shard_map/ppermute | solution.py:490
  287.2 16.9 %collective-permute-start.16 = (f32[256,1024]{1,0:T(8,128)S(1)}, f32[256,1024]{1,0:T(8,128)S(1)}, u32[]{:S(2)}, u32[]{:S(2)}) collective-permute-start(f32[256,1024]{1,0:T(8,128)S(1)} %get-tuple-element.108), channel_id=1, source_target_pairs={{0,6},{2,0},{4,14},{6,4},{8,2},{10,8},{12,22},{14,12},{16,10},{18,... | collective-permute-start | bytes 3145736 | tf_op jit(solution)/shard_map/ppermute | solution.py:491
  298.4 14.2 %collective-permute-start.17 = (f32[256,1024]{1,0:T(8,128)S(1)}, f32[256,1024]{1,0:T(8,128)S(1)}, u32[]{:S(2)}, u32[]{:S(2)}) collective-permute-start(f32[256,1024]{1,0:T(8,128)S(1)} %get-tuple-element.110), channel_id=1, source_target_pairs={{0,2},{2,8},{4,6},{6,0},{8,10},{10,16},{12,14},{14,4},{16,18},{18,... | collective-permute-start | bytes 3145736 | tf_op jit(solution)/shard_map/ppermute | solution.py:490
  298.4 16.9 %collective-permute-start.18 = (f32[256,1024]{1,0:T(8,128)S(1)}, f32[256,1024]{1,0:T(8,128)S(1)}, u32[]{:S(2)}, u32[]{:S(2)}) collective-permute-start(f32[256,1024]{1,0:T(8,128)S(1)} %get-tuple-element.111), channel_id=1, source_target_pairs={{0,6},{2,0},{4,14},{6,4},{8,2},{10,8},{12,22},{14,12},{16,10},{18,... | collective-permute-start | bytes 3145736 | tf_op jit(solution)/shard_map/ppermute | solution.py:491
  304.1 12.2 %slice-start = ((s8[12582912]{0:T(1024)(128)(4,1)}), s8[4194304]{0:T(1024)(128)(4,1)S(1)}, s32[]{:S(2)}) async-start(s8[12582912]{0:T(1024)(128)(4,1)} %bitcast.21), calls=%async_computation.7 | async-start | bytes 8388608
  304.1 12.2 %slice-start.1 = ((s8[12582912]{0:T(1024)(128)(4,1)}), s8[4194304]{0:T(1024)(128)(4,1)S(1)}, s32[]{:S(2)}) async-start(s8[12582912]{0:T(1024)(128)(4,1)} %bitcast.21), calls=%async_computation.8 | async-start | bytes 8388608
  304.1 12.2 %slice-start.2 = ((s8[12582912]{0:T(1024)(128)(4,1)}), s8[4194304]{0:T(1024)(128)(4,1)S(1)}, s32[]{:S(2)}) async-start(s8[12582912]{0:T(1024)(128)(4,1)} %bitcast.21), calls=%async_computation.9 | async-start | bytes 8388608
  309.9 14.5 %collective-permute-start.19 = (f32[256,1024]{1,0:T(8,128)S(1)}, f32[256,1024]{1,0:T(8,128)S(1)}, u32[]{:S(2)}, u32[]{:S(2)}) collective-permute-start(f32[256,1024]{1,0:T(8,128)S(1)} %get-tuple-element.113), channel_id=1, source_target_pairs={{0,2},{2,8},{4,6},{6,0},{8,10},{10,16},{12,14},{14,4},{16,18},{18,... | collective-permute-start | bytes 3145736 | tf_op jit(solution)/shard_map/ppermute | solution.py:490
  310.2 16.3 %collective-permute-start.20 = (f32[256,1024]{1,0:T(8,128)S(1)}, f32[256,1024]{1,0:T(8,128)S(1)}, u32[]{:S(2)}, u32[]{:S(2)}) collective-permute-start(f32[256,1024]{1,0:T(8,128)S(1)} %get-tuple-element.114), channel_id=1, source_target_pairs={{0,6},{2,0},{4,14},{6,4},{8,2},{10,8},{12,22},{14,12},{16,10},{18,... | collective-permute-start | bytes 3145736 | tf_op jit(solution)/shard_map/ppermute | solution.py:491
  316.3 10.3 %slice-start.3 = ((s8[12582912]{0:T(1024)(128)(4,1)}), s8[4194304]{0:T(1024)(128)(4,1)S(1)}, s32[]{:S(2)}) async-start(s8[12582912]{0:T(1024)(128)(4,1)} %bitcast.23), calls=%async_computation.10 | async-start | bytes 8388608
  323.6 11.8 %collective-permute-start.21 = (f32[256,1024]{1,0:T(8,128)S(1)}, f32[256,1024]{1,0:T(8,128)S(1)}, u32[]{:S(2)}, u32[]{:S(2)}) collective-permute-start(f32[256,1024]{1,0:T(8,128)S(1)} %get-tuple-element.116), channel_id=1, source_target_pairs={{0,2},{2,8},{4,6},{6,0},{8,10},{10,16},{12,14},{14,4},{16,18},{18,... | collective-permute-start | bytes 3145736 | tf_op jit(solution)/shard_map/ppermute | solution.py:490
  323.7 14.8 %collective-permute-start.22 = (f32[256,1024]{1,0:T(8,128)S(1)}, f32[256,1024]{1,0:T(8,128)S(1)}, u32[]{:S(2)}, u32[]{:S(2)}) collective-permute-start(f32[256,1024]{1,0:T(8,128)S(1)} %get-tuple-element.117), channel_id=1, source_target_pairs={{0,6},{2,0},{4,14},{6,4},{8,2},{10,8},{12,22},{14,12},{16,10},{18,... | collective-permute-start | bytes 3145736 | tf_op jit(solution)/shard_map/ppermute | solution.py:491
  326.5 12.0 %slice-start.6 = ((s8[12582912]{0:T(1024)(128)(4,1)}), s8[4194304]{0:T(1024)(128)(4,1)S(1)}, s32[]{:S(2)}) async-start(s8[12582912]{0:T(1024)(128)(4,1)} %bitcast.25), calls=%async_computation.13 | async-start | bytes 8388608
  326.6 11.9 %slice-start.7 = ((s8[12582912]{0:T(1024)(128)(4,1)}), s8[4194304]{0:T(1024)(128)(4,1)S(1)}, s32[]{:S(2)}) async-start(s8[12582912]{0:T(1024)(128)(4,1)} %bitcast.25), calls=%async_computation.14 | async-start | bytes 8388608
  326.6 11.9 %slice-start.8 = ((s8[12582912]{0:T(1024)(128)(4,1)}), s8[4194304]{0:T(1024)(128)(4,1)S(1)}, s32[]{:S(2)}) async-start(s8[12582912]{0:T(1024)(128)(4,1)} %bitcast.25), calls=%async_computation.15 | async-start | bytes 8388608
  332.4 14.2 %collective-permute-start.23 = (f32[256,1024]{1,0:T(8,128)S(1)}, f32[256,1024]{1,0:T(8,128)S(1)}, u32[]{:S(2)}, u32[]{:S(2)}) collective-permute-start(f32[256,1024]{1,0:T(8,128)S(1)} %get-tuple-element.119), channel_id=1, source_target_pairs={{0,2},{2,8},{4,6},{6,0},{8,10},{10,16},{12,14},{14,4},{16,18},{18,... | collective-permute-start | bytes 3145736 | tf_op jit(solution)/shard_map/ppermute | solution.py:490
  332.5 17.2 %collective-permute-start.24 = (f32[256,1024]{1,0:T(8,128)S(1)}, f32[256,1024]{1,0:T(8,128)S(1)}, u32[]{:S(2)}, u32[]{:S(2)}) collective-permute-start(f32[256,1024]{1,0:T(8,128)S(1)} %get-tuple-element.120), channel_id=1, source_target_pairs={{0,6},{2,0},{4,14},{6,4},{8,2},{10,8},{12,22},{14,12},{16,10},{18,... | collective-permute-start | bytes 3145736 | tf_op jit(solution)/shard_map/ppermute | solution.py:491
  338.5 11.2 %slice-start.9 = ((s8[12582912]{0:T(1024)(128)(4,1)}), s8[4194304]{0:T(1024)(128)(4,1)S(1)}, s32[]{:S(2)}) async-start(s8[12582912]{0:T(1024)(128)(4,1)} %bitcast.27), calls=%async_computation.16 | async-start | bytes 8388608
  338.5 11.2 %slice-start.10 = ((s8[12582912]{0:T(1024)(128)(4,1)}), s8[4194304]{0:T(1024)(128)(4,1)S(1)}, s32[]{:S(2)}) async-start(s8[12582912]{0:T(1024)(128)(4,1)} %bitcast.27), calls=%async_computation.17 | async-start | bytes 8388608
  338.5 11.2 %slice-start.11 = ((s8[12582912]{0:T(1024)(128)(4,1)}), s8[4194304]{0:T(1024)(128)(4,1)S(1)}, s32[]{:S(2)}) async-start(s8[12582912]{0:T(1024)(128)(4,1)} %bitcast.27), calls=%async_computation.18 | async-start | bytes 8388608
  344.4 13.5 %collective-permute-start.25 = (f32[256,1024]{1,0:T(8,128)S(1)}, f32[256,1024]{1,0:T(8,128)S(1)}, u32[]{:S(2)}, u32[]{:S(2)}) collective-permute-start(f32[256,1024]{1,0:T(8,128)S(1)} %get-tuple-element.122), channel_id=1, source_target_pairs={{0,2},{2,8},{4,6},{6,0},{8,10},{10,16},{12,14},{14,4},{16,18},{18,... | collective-permute-start | bytes 3145736 | tf_op jit(solution)/shard_map/ppermute | solution.py:490
  344.5 16.5 %collective-permute-start.26 = (f32[256,1024]{1,0:T(8,128)S(1)}, f32[256,1024]{1,0:T(8,128)S(1)}, u32[]{:S(2)}, u32[]{:S(2)}) collective-permute-start(f32[256,1024]{1,0:T(8,128)S(1)} %get-tuple-element.123), channel_id=1, source_target_pairs={{0,6},{2,0},{4,14},{6,4},{8,2},{10,8},{12,22},{14,12},{16,10},{18,... | collective-permute-start | bytes 3145736 | tf_op jit(solution)/shard_map/ppermute | solution.py:491
  349.7 11.2 %slice-start.12 = ((s8[12582912]{0:T(1024)(128)(4,1)}), s8[4194304]{0:T(1024)(128)(4,1)S(1)}, s32[]{:S(2)}) async-start(s8[12582912]{0:T(1024)(128)(4,1)} %bitcast.29), calls=%async_computation.19 | async-start | bytes 8388608
  349.7 11.2 %slice-start.13 = ((s8[12582912]{0:T(1024)(128)(4,1)}), s8[4194304]{0:T(1024)(128)(4,1)S(1)}, s32[]{:S(2)}) async-start(s8[12582912]{0:T(1024)(128)(4,1)} %bitcast.29), calls=%async_computation.20 | async-start | bytes 8388608
  349.8 11.2 %slice-start.14 = ((s8[12582912]{0:T(1024)(128)(4,1)}), s8[4194304]{0:T(1024)(128)(4,1)S(1)}, s32[]{:S(2)}) async-start(s8[12582912]{0:T(1024)(128)(4,1)} %bitcast.29), calls=%async_computation.21 | async-start | bytes 8388608
  355.6 13.5 %collective-permute-start.27 = (f32[256,1024]{1,0:T(8,128)S(1)}, f32[256,1024]{1,0:T(8,128)S(1)}, u32[]{:S(2)}, u32[]{:S(2)}) collective-permute-start(f32[256,1024]{1,0:T(8,128)S(1)} %get-tuple-element.125), channel_id=1, source_target_pairs={{0,2},{2,8},{4,6},{6,0},{8,10},{10,16},{12,14},{14,4},{16,18},{18,... | collective-permute-start | bytes 3145736 | tf_op jit(solution)/shard_map/ppermute | solution.py:490
  355.7 16.5 %collective-permute-start.28 = (f32[256,1024]{1,0:T(8,128)S(1)}, f32[256,1024]{1,0:T(8,128)S(1)}, u32[]{:S(2)}, u32[]{:S(2)}) collective-permute-start(f32[256,1024]{1,0:T(8,128)S(1)} %get-tuple-element.126), channel_id=1, source_target_pairs={{0,6},{2,0},{4,14},{6,4},{8,2},{10,8},{12,22},{14,12},{16,10},{18,... | collective-permute-start | bytes 3145736 | tf_op jit(solution)/shard_map/ppermute | solution.py:491
  361.0 12.2 %slice-start.15 = ((s8[12582912]{0:T(1024)(128)(4,1)}), s8[4194304]{0:T(1024)(128)(4,1)S(1)}, s32[]{:S(2)}) async-start(s8[12582912]{0:T(1024)(128)(4,1)} %bitcast.31), calls=%async_computation.22 | async-start | bytes 8388608
  361.0 12.2 %slice-start.16 = ((s8[12582912]{0:T(1024)(128)(4,1)}), s8[4194304]{0:T(1024)(128)(4,1)S(1)}, s32[]{:S(2)}) async-start(s8[12582912]{0:T(1024)(128)(4,1)} %bitcast.31), calls=%async_computation.23 | async-start | bytes 8388608
  361.0 12.2 %slice-start.17 = ((s8[12582912]{0:T(1024)(128)(4,1)}), s8[4194304]{0:T(1024)(128)(4,1)S(1)}, s32[]{:S(2)}) async-start(s8[12582912]{0:T(1024)(128)(4,1)} %bitcast.31), calls=%async_computation.24 | async-start | bytes 8388608
  367.5 14.2 %collective-permute-start.29 = (f32[256,1024]{1,0:T(8,128)}, f32[256,1024]{1,0:T(8,128)S(1)}, u32[]{:S(2)}, u32[]{:S(2)}) collective-permute-start(f32[256,1024]{1,0:T(8,128)} %get-tuple-element.128), channel_id=1, source_target_pairs={{0,2},{2,8},{4,6},{6,0},{8,10},{10,16},{12,14},{14,4},{16,18},{18,... | collective-permute-start | bytes 3145736 | tf_op jit(solution)/shard_map/ppermute | solution.py:490
  367.5 16.0 %collective-permute-start.30 = (f32[256,1024]{1,0:T(8,128)}, f32[256,1024]{1,0:T(8,128)S(1)}, u32[]{:S(2)}, u32[]{:S(2)}) collective-permute-start(f32[256,1024]{1,0:T(8,128)} %get-tuple-element.129), channel_id=1, source_target_pairs={{0,6},{2,0},{4,14},{6,4},{8,2},{10,8},{12,22},{14,12},{16,10},{18,... | collective-permute-start | bytes 3145736 | tf_op jit(solution)/shard_map/ppermute | solution.py:491
  373.2 10.4 %slice-start.18 = ((s8[12582912]{0:T(1024)(128)(4,1)}), s8[4194304]{0:T(1024)(128)(4,1)S(1)}, s32[]{:S(2)}) async-start(s8[12582912]{0:T(1024)(128)(4,1)} %bitcast.33), calls=%async_computation.25 | async-start | bytes 8388608
  381.2 23.3 %collective-permute-start.34 = (f32[256,1024]{1,0:T(8,128)}, f32[256,1024]{1,0:T(8,128)}, u32[]{:S(2)}, u32[]{:S(2)}) collective-permute-start(f32[256,1024]{1,0:T(8,128)} %get-tuple-element.135), channel_id=1, source_target_pairs={{0,2},{2,8},{4,6},{6,0},{8,10},{10,16},{12,14},{14,4},{16,18},{18,... | collective-permute-start | bytes 3145736 | tf_op jit(solution)/shard_map/ppermute | solution.py:490
  381.2 23.3 %collective-permute-start.35 = (f32[256,1024]{1,0:T(8,128)}, f32[256,1024]{1,0:T(8,128)}, u32[]{:S(2)}, u32[]{:S(2)}) collective-permute-start(f32[256,1024]{1,0:T(8,128)} %get-tuple-element.136), channel_id=1, source_target_pairs={{0,6},{2,0},{4,14},{6,4},{8,2},{10,8},{12,22},{14,12},{16,10},{18,... | collective-permute-start | bytes 3145736 | tf_op jit(solution)/shard_map/ppermute | solution.py:491
  389.8 18.9 %collective-permute-start.32 = (f32[256,1024]{1,0:T(8,128)}, f32[256,1024]{1,0:T(8,128)}, u32[]{:S(2)}, u32[]{:S(2)}) collective-permute-start(f32[256,1024]{1,0:T(8,128)} %get-tuple-element.132), channel_id=1, source_target_pairs={{0,2},{2,8},{4,6},{6,0},{8,10},{10,16},{12,14},{14,4},{16,18},{18,... | collective-permute-start | bytes 3145736 | tf_op jit(solution)/shard_map/ppermute | solution.py:490
  389.8 18.9 %collective-permute-start.33 = (f32[256,1024]{1,0:T(8,128)}, f32[256,1024]{1,0:T(8,128)}, u32[]{:S(2)}, u32[]{:S(2)}) collective-permute-start(f32[256,1024]{1,0:T(8,128)} %get-tuple-element.133), channel_id=1, source_target_pairs={{0,6},{2,0},{4,14},{6,4},{8,2},{10,8},{12,22},{14,12},{16,10},{18,... | collective-permute-start | bytes 3145736 | tf_op jit(solution)/shard_map/ppermute | solution.py:491
  391.1 8.0 %collective-permute-start.31 = (f32[192,256]{0,1:T(8,128)}, f32[192,256]{0,1:T(8,128)}, u32[]{:S(2)}, u32[]{:S(2)}) collective-permute-start(f32[192,256]{0,1:T(8,128)} %copy.112), channel_id=1, source_target_pairs={{0,1},{1,0},{2,3},{3,2},{4,5},{5,4},{6,7},{7,6},{8,9},{9,8},{10,11... | collective-permute-start | bytes 589832 | tf_op jit(solution)/shard_map/ppermute | solution.py:358
  (27 other events, 145.7 us)
Sparse Core Ops, SparseCore 0:
  11.3 183.1 all-gather.1

commit v2 on v1

--- a/solution.py
+++ b/solution.py
@@ -17,7 +17,7 @@
 LANES = 128
 GROUP = 16
 VMEM_LIMIT = 20 * 1024 * 1024
-STUDENT_LIMIT = 44 * 1024 * 1024
+STREAM_LIMIT = 52 * 1024 * 1024
 F32 = jnp.float32
 BF16 = jnp.bfloat16
 
@@ -35,8 +35,7 @@
     return lax.dot_general(a, b, (dims, ((), ())), preferred_element_type=F32)
 
 
-def teacher_kernel(t_ref, m_ref, s_ref, copy_ref, *, width, unroll):
-    copy_ref[...] = t_ref[...]
+def teacher_kernel(t_ref, m_ref, s_ref, *, width, unroll):
     span = LANES * unroll
     for r in range(0, t_ref.shape[0], GROUP):
 
@@ -71,9 +70,9 @@
         lambda *refs: teacher_kernel(*refs, width=width, unroll=16),
         grid=(tokens // rows,),
         in_specs=[pl.BlockSpec((rows, width), lambda i: (i, 0))],
-        out_specs=[spec, spec, pl.BlockSpec((rows, width), lambda i: (i, 0))],
-        out_shape=[shape, shape, pltpu.VMEM(teacher.shape, teacher.dtype)],
-        compiler_params=params(),
+        out_specs=[spec, spec],
+        out_shape=[shape, shape],
+        compiler_params=params(STREAM_LIMIT),
         name="teacher_stats",
     )(teacher)
 
@@ -120,7 +119,7 @@
             jax.ShapeDtypeStruct((owners, 1, shard), F32),
             jax.ShapeDtypeStruct((tokens, LANES), F32),
         ],
-        compiler_params=params(),
+        compiler_params=params(STREAM_LIMIT),
         name="column_sums",
     )(teacher, offset, row_here, row_there)
 
@@ -166,7 +165,7 @@
             jax.ShapeDtypeStruct((tokens, LANES), F32),
             jax.ShapeDtypeStruct((1, width), F32),
         ],
-        compiler_params=params(),
+        compiler_params=params(STREAM_LIMIT),
         name="row_sums",
     )(teacher, offset, sums)
 
@@ -181,6 +180,7 @@
 
 def student_kernel(u_ref, w_ref, m_ref, s_ref, score_a, score_b):
     rows, tokens = score_a.shape
+    held = (score_b, score_a)
     step = pl.program_id(0)
 
     def scores(start):
@@ -199,10 +199,11 @@
         s_ref[...] = jnp.zeros_like(s_ref)
         score_b[...] = jnp.full_like(score_b, -1e30)
 
-    score_a[...] = scores(0)
-    stats = merge(score_b[...], m_ref[...], s_ref[...])
-    score_b[...] = scores(rows)
-    stats = merge(score_a[...], *stats)
+    stats = m_ref[...], s_ref[...]
+    pieces = w_ref.shape[0] // rows
+    for i in range(pieces):
+        held[(i + 1) % 2][...] = scores(i * rows)
+        stats = merge(held[i % 2][...], *stats)
     m_ref[...], s_ref[...] = stats
 
     @pl.when(step == pl.num_programs(0) - 1)
@@ -225,8 +226,8 @@
         ],
         out_specs=[stat, stat],
         out_shape=[shape, shape],
-        scratch_shapes=[pltpu.VMEM((block // 2, tokens), F32)] * 2,
-        compiler_params=params(STUDENT_LIMIT),
+        scratch_shapes=[pltpu.VMEM((min(block // 2, 512), tokens), F32)] * 2,
+        compiler_params=params(STREAM_LIMIT),
         name="student_stats",
     )(u_turned, protos)
 
@@ -261,7 +262,7 @@
     tok_out[...] = token_part
 
 
-def grad_step(own, slots, consts, tok, teacher, cols, protos, arrived, width):
+def grad_step(own, slots, consts, tok, teacher, cols, protos, arrived, width, limit):
     tokens, depth = tok.shape
     block = min(width, 512)
     count = width // block
@@ -297,7 +298,7 @@
         grid_spec=grid,
         out_shape=[jax.ShapeDtypeStruct((depth, width), F32) for slot in slots]
         + [jax.ShapeDtypeStruct(tok.shape, F32)],
-        compiler_params=params(),
+        compiler_params=params(limit),
         name="grad_blocks",
     )(
         own,
@@ -325,7 +326,7 @@
 
 def proto_grads(turned, gain_row, parts, half, done):
     depth, width = parts[0].shape
-    block = min(width, 256)
+    block = min(width, 512)
     count = width // block
     return pl.pallas_call(
         proto_kernel,
@@ -350,6 +351,24 @@
     )(turned, gain_row, *parts, *done)
 
 
+def token_kernel(here, there, unit, inverse, after, out):
+    token_sum = here[...] + there[...]
+    inner = jnp.sum(unit[...] * token_sum, axis=1, keepdims=True)
+    out[...] = (token_sum - unit[...] * inner) * inverse[...][:, :1]
+
+
+def token_grads(here, there, unit, inverse, after):
+    vmem = pl.BlockSpec(memory_space=pltpu.VMEM)
+    return pl.pallas_call(
+        token_kernel,
+        in_specs=[vmem] * 4 + [pl.BlockSpec(memory_space=pl.ANY)],
+        out_specs=vmem,
+        out_shape=jax.ShapeDtypeStruct(unit.shape, F32),
+        compiler_params=params(),
+        name="token_grads",
+    )(here, there, unit, inverse, after)
+
+
 def halves(count):
     return [1 << bit for bit in range(count.bit_length() - 1)]
 
@@ -447,7 +466,7 @@
     u_turned = parts_of_right(u_hi, u_lo, 1).T
     t_parts = parts_of_left(*pieces(unit_tok.T), 1)
 
-    top, total, teacher_logits = teacher_stats(teacher_logits)
+    top, total = teacher_stats(teacher_logits)
     base = log_total(top[:, 0], jnp.sum(total, axis=1), "proto", proto_count)
     offset = jnp.broadcast_to(base[:, None], (tokens_here, LANES))
     lane = lax.broadcasted_iota(jnp.int32, (tokens_here, LANES), 1)
@@ -469,14 +488,14 @@
     token_part = jnp.zeros(unit_tok.shape, F32)
     consts = (u_parts, t_parts, lse, offset)
 
-    def blocks_of(slots, arrived):
+    def blocks_of(slots, arrived, limit=VMEM_LIMIT):
         return grad_step(
-            own, slots, consts, token_part, teacher_logits, cols, gathered, arrived, width
+            own, slots, consts, token_part, teacher_logits, cols, gathered, arrived, width, limit
         )
 
     crossed = [None, None]
     for sub in range(2):
-        (part,), token_part = blocks_of((slot(half, sub),), [])
+        (part,), token_part = blocks_of((slot(half, sub),), [], STREAM_LIMIT)
         crossed[sub] = swap(part, "dp", dp_count, 1)
     waiting = [[crossed[0]], [crossed[1]]]
     mine = []
@@ -485,21 +504,27 @@
             (part,), token_part = blocks_of((slot(0, len(mine)),), [])
             mine.append(part)
         for sub in range(2):
-            (first, second), token_part = blocks_of((slot(far, sub), slot(-far, sub)), waiting[sub])
+            (first, second), token_part = blocks_of(
+                (slot(far, sub), slot(-far, sub)),
+                waiting[sub],
+                STREAM_LIMIT if far == half - 1 else VMEM_LIMIT,
+            )
             waiting[sub] = [
                 lax.ppermute(first, "dp", ahead),
                 lax.ppermute(second, "dp", behind),
             ]
+    token_here, token_there = sum_pair(token_part, "proto", proto_count)
     turned, gain_row = prototypes.T, gain[None, :]
-    grads = ()
-    for sub in range(2):
-        grads = proto_grads(turned, gain_row, [mine[sub], *waiting[sub]], sub, grads)
+    grads = proto_grads(turned, gain_row, [mine[0], *waiting[0]], 0, ())
+    input_grad = token_grads(
+        token_here,
+        token_there,
+        unit_tok,
+        jnp.broadcast_to(inverse, (tokens_here, LANES)),
+        grads[1],
+    )
+    grads = proto_grads(turned, gain_row, [mine[1], *waiting[1]], 1, grads)
     grad_proto, grad_gain = grads[0], grads[1].reshape(shard)
-
-    for distance in halves(proto_count):
-        token_part = token_part + swap(token_part, "proto", proto_count, distance)
-    inner_dot = jnp.sum(unit_tok * token_part, axis=1, keepdims=True)
-    input_grad = (token_part - unit_tok * inner_dot) * inverse
     grad_packed = jnp.zeros(packed.shape, F32).at[row_index].set(input_grad)
     return (grad_packed, grad_proto, grad_gain)
 

time: 427 us -> 433 us (1.014)
  Pallas kernels: 180 us -> 216 us
  local copies, waits for them, and re-layouts: 48.6 us -> 23.2 us
  blocking collectives: 29.6 us -> 16.7 us
  waiting for transfers between devices: 97.2 us -> 103 us
  starting transfers between devices: 42.1 us -> 46.6 us
    unnamed x101 -> x91, local copies, waits for them, and re-layouts: 40.3 us -> 16 us
    pallas_call x3, Pallas kernels: 19.3 us -> 38.3 us  [row_pass(): pl.pallas_call(lambda *refs: row_kernel(*refs, unroll=min(16, block // LA...]
    pallas_call x3, Pallas kernels: 21.6 us -> 38.8 us  [column_pass(): pl.pallas_call(lambda *refs: column_kernel(*refs, unroll=min(16, shard //...]
    all_to_all x1 -> x0, blocking collectives: 13 us -> none  [column_total(): lax.all_to_all(jnp.broadcast_to(mine, x.shape), 'dp', 0, 0, tiled=True)]
    all_to_all x2 -> x3, waiting for transfers between devices: 15.8 us -> 26.5 us  [column_total(): lax.all_to_all(jnp.broadcast_to(mine, x.shape), 'dp', 0, 0, tiled=True)]
    ppermute x8, waiting for transfers between devices: 14.6 us -> 9.71 us  [swap(): return lax.ppermute(x, axis, [(i, i ^ distance) for i in range(count)])]
    all_to_all x2 -> x3, starting transfers between devices: 9.3 us -> 13.8 us  [column_total(): lax.all_to_all(jnp.broadcast_to(mine, x.shape), 'dp', 0, 0, tiled=True)]
  transfers between devices with their start and end apart: 41 -> 42, of which waited for: 30 -> 33; matrix products, arithmetic and copies ran while one was open for 3% -> 2% of each run, Pallas kernels for 36% -> 45%
where the time goes in v2:
time: 433 us; the launch traced here: 425 us
  Pallas kernels  216 us (50%)
  waiting for transfers between devices  103 us (24%)
  starting transfers between devices  46.6 us (11%)
  local copies, waits for them, and re-layouts  23.2 us (5%)
  blocking collectives  16.7 us (4%)
  between operations  15.2 us (4%)
  other arithmetic  5.33 us (1%)
    pallas_call x18, Pallas kernels, grad_step(): pl.pallas_call(lambda *refs: grad_kernel(*refs, blocks=blocks, arrivals=l...  100 us
    pallas_call x3, Pallas kernels, column_pass(): pl.pallas_call(lambda *refs: column_kernel(*refs, unroll=min(16, shard //...  38.8 us
    pallas_call x3, Pallas kernels, row_pass(): pl.pallas_call(lambda *refs: row_kernel(*refs, unroll=min(16, block // LA...  38.3 us
    ppermute x14, waiting for transfers between devices, body(): lax.ppermute(second, 'dp', behind)  33.1 us
    all_to_all x3, waiting for transfers between devices, column_total(): lax.all_to_all(jnp.broadcast_to(mine, x.shape), 'dp', 0, 0, tiled=True)  26.5 us
    pallas_call x1, Pallas kernels, student_pass(): pl.pallas_call(student_kernel, grid=(rows // block,), in_specs=[pl.BlockS...  18.9 us
    all_to_all x2, waiting for transfers between devices, column_total(): lax.all_to_all(x, 'dp', 0, 0, tiled=True)  17.1 us
    all_to_all x1, blocking collectives, column_total(): lax.all_to_all(x, 'dp', 0, 0, tiled=True)  16.7 us
  transfers between devices with their start and end apart: 42, of which 33 were waited for; matrix products, arithmetic and copies ran while one was open for 2% of the time, Pallas kernels for 45%

profile of v2, /device:TPU:1, one launch (start us, length us, event | category | flops | bytes accessed | tf_op | source)
XLA Modules:
  0.0 425.2 jit_solution(14303737448429627716)
XLA Ops:
  7.2 2.1 multiply_reduce_fusion
  11.2 13.0 %teacher_stats.1 = (f32[192,128]{1,0:T(8,128)S(1)}, f32[192,128]{1,0:T(8,128)S(1)}) custom-call(bf16[192,32768]{1,0:T(8,128)(2,1)} %refs_7_.27), custom_call_target="tpu_custom_call" | custom-call | tf_op jit(solution)/shard_map/teacher_stats/pallas_call | solution.py:69
  24.4 2.1 collective-permute-start.1
  28.4 12.4 %column_sums.3 = (f32[16,1,2048]{2,1,0:T(1,128)S(1)}, f32[192,128]{1,0:T(8,128)S(1)}) custom-call(bf16[192,32768]{1,0:T(8,128)(2,1)} %refs_7_.27, f32[192,128]{1,0:T(8,128)S(1)} %broadcast_in_dim.98.refs_1_, f32[192,128]{1,0:T(8,128)S(1)} %iota.17.refs_2_, f32[192,128]{1,0:T(8,128)S(1)} %broadcast_in_dim.101.refs_3_), custom_call_target="tpu_custom_call" | custom-call | tf_op jit(solution)/shard_map/column_sums/pallas_call | solution.py:113
  40.8 16.7 %all_to_all.30 = f32[16,1,2048]{2,1,0:T(1,128)S(1)} all-to-all(f32[16,1,2048]{2,1,0:T(1,128)S(1)} %get-tuple-element.76), channel_id=1, replica_groups=mesh['dp'=16,'proto'=2] {'dp'}, dimensions={0} | all-to-all | bytes 262144 | tf_op jit(solution)/shard_map/all_to_all | solution.py:388
  58.4 4.5 %all-to-all-start.1 = ((f32[16,1,2048]{2,1,0:T(1,128)}), f32[16,1,2048]{2,1,0:T(1,128)S(1)}, u32[]{:S(2)}, u32[]{:S(2)}) async-start(f32[16,1,2048]{2,1,0:T(1,128)} %broadcast_in_dim.102), calls=%async_computation.1 | async-start | bytes 262144 | tf_op jit(solution)/shard_map/all_to_all | solution.py:389
  62.9 9.3 %all-to-all-done.1.refs_2_ = f32[16,1,2048]{2,1,0:T(1,128)S(1)} async-done(((f32[16,1,2048]{2,1,0:T(1,128)}), f32[16,1,2048]{2,1,0:T(1,128)S(1)}, u32[]{:S(2)}, u32[]{:S(2)}) %all-to-all-start.1) | async-done | bytes 131104 | tf_op jit(solution)/shard_map/all_to_all | solution.py:389
  72.3 13.0 %row_sums.3 = (f32[192,128]{1,0:T(8,128)S(1)}, f32[1,32768]{1,0:T(1,128)}) custom-call(bf16[192,32768]{1,0:T(8,128)(2,1)} %refs_7_.27, f32[192,128]{1,0:T(8,128)S(1)} %get-tuple-element.75.refs_1_, f32[16,1,2048]{2,1,0:T(1,128)S(1)} %all-to-all-done.1.refs_2_), custom_call_target="tpu_custom_call" | custom-call | tf_op jit(solution)/shard_map/row_sums/pallas_call | solution.py:159
  86.5 2.6 collective-permute-done.2.refs_3_
  89.2 13.2 %column_sums.4 = (f32[16,1,2048]{2,1,0:T(1,128)}, f32[192,128]{1,0:T(8,128)S(1)}) custom-call(bf16[192,32768]{1,0:T(8,128)(2,1)} %refs_7_.27, f32[192,128]{1,0:T(8,128)S(1)} %get-tuple-element.75.refs_1_, f32[192,128]{1,0:T(8,128)S(1)} %get-tuple-element.77.refs_2_, f32[192,128]{1,0:T(8,128)S(1)} %collective-permute-done.2.refs_3_), custom_call_target="tpu_custom_call" | custom-call | tf_op jit(solution)/shard_map/column_sums/pallas_call | solution.py:113
  102.4 5.2 %all-to-all-start.2 = ((f32[16,1,2048]{2,1,0:T(1,128)}), f32[16,1,2048]{2,1,0:T(1,128)S(1)}, u32[]{:S(2)}, u32[]{:S(2)}) async-start(f32[16,1,2048]{2,1,0:T(1,128)} %get-tuple-element.79), calls=%async_computation.2 | async-start | bytes 262144 | tf_op jit(solution)/shard_map/all_to_all | solution.py:388
  109.1 7.8 %all-to-all-done.2 = f32[16,1,2048]{2,1,0:T(1,128)S(1)} async-done(((f32[16,1,2048]{2,1,0:T(1,128)}), f32[16,1,2048]{2,1,0:T(1,128)S(1)}, u32[]{:S(2)}, u32[]{:S(2)}) %all-to-all-start.2) | async-done | bytes 131104 | tf_op jit(solution)/shard_map/all_to_all | solution.py:388
  117.8 4.5 %all-to-all-start.3 = ((f32[16,1,2048]{2,1,0:T(1,128)}), f32[16,1,2048]{2,1,0:T(1,128)S(1)}, u32[]{:S(2)}, u32[]{:S(2)}) async-start(f32[16,1,2048]{2,1,0:T(1,128)} %broadcast_in_dim.103), calls=%async_computation.3 | async-start | bytes 262144 | tf_op jit(solution)/shard_map/all_to_all | solution.py:389
  122.5 9.1 %all-to-all-done.3.refs_2_ = f32[16,1,2048]{2,1,0:T(1,128)S(1)} async-done(((f32[16,1,2048]{2,1,0:T(1,128)}), f32[16,1,2048]{2,1,0:T(1,128)S(1)}, u32[]{:S(2)}, u32[]{:S(2)}) %all-to-all-start.3) | async-done | bytes 131104 | tf_op jit(solution)/shard_map/all_to_all | solution.py:389
  131.6 12.9 %row_sums.4 = (f32[192,128]{1,0:T(8,128)S(1)}, f32[1,32768]{1,0:T(1,128)}) custom-call(bf16[192,32768]{1,0:T(8,128)(2,1)} %refs_7_.27, f32[192,128]{1,0:T(8,128)S(1)} %get-tuple-element.78.refs_1_, f32[16,1,2048]{2,1,0:T(1,128)S(1)} %all-to-all-done.3.refs_2_), custom_call_target="tpu_custom_call" | custom-call | tf_op jit(solution)/shard_map/row_sums/pallas_call | solution.py:159
  145.8 2.6 collective-permute-done.3.refs_3_
  148.4 13.2 %column_sums.5 = (f32[16,1,2048]{2,1,0:T(1,128)}, f32[192,128]{1,0:T(8,128)S(1)}) custom-call(bf16[192,32768]{1,0:T(8,128)(2,1)} %refs_7_.27, f32[192,128]{1,0:T(8,128)S(1)} %get-tuple-element.78.refs_1_, f32[192,128]{1,0:T(8,128)S(1)} %get-tuple-element.80.refs_2_, f32[192,128]{1,0:T(8,128)S(1)} %collective-permute-done.3.refs_3_), custom_call_target="tpu_custom_call" | custom-call | tf_op jit(solution)/shard_map/column_sums/pallas_call | solution.py:113
  161.6 5.6 %all-to-all-start.4 = ((f32[16,1,2048]{2,1,0:T(1,128)}), f32[16,1,2048]{2,1,0:T(1,128)S(1)}, u32[]{:S(2)}, u32[]{:S(2)}) async-start(f32[16,1,2048]{2,1,0:T(1,128)} %get-tuple-element.82), calls=%async_computation.4 | async-start | bytes 262144 | tf_op jit(solution)/shard_map/all_to_all | solution.py:388
  167.2 9.3 %all-to-all-done.4 = f32[16,1,2048]{2,1,0:T(1,128)S(1)} async-done(((f32[16,1,2048]{2,1,0:T(1,128)}), f32[16,1,2048]{2,1,0:T(1,128)S(1)}, u32[]{:S(2)}, u32[]{:S(2)}) %all-to-all-start.4) | async-done | bytes 131104 | tf_op jit(solution)/shard_map/all_to_all | solution.py:388
  177.3 4.8 %all-to-all-start.5 = ((f32[16,1,2048]{2,1,0:T(1,128)}), f32[16,1,2048]{2,1,0:T(1,128)S(1)}, u32[]{:S(2)}, u32[]{:S(2)}) async-start(f32[16,1,2048]{2,1,0:T(1,128)} %broadcast_in_dim.104), calls=%async_computation.5 | async-start | bytes 262144 | tf_op jit(solution)/shard_map/all_to_all | solution.py:389
  183.2 8.1 %all-to-all-done.5.refs_2_ = f32[16,1,2048]{2,1,0:T(1,128)S(1)} async-done(((f32[16,1,2048]{2,1,0:T(1,128)}), f32[16,1,2048]{2,1,0:T(1,128)S(1)}, u32[]{:S(2)}, u32[]{:S(2)}) %all-to-all-start.5) | async-done | bytes 131104 | tf_op jit(solution)/shard_map/all_to_all | solution.py:389
  191.3 12.5 %row_sums.5 = (f32[192,128]{1,0:T(8,128)S(1)}, f32[1,32768]{1,0:T(1,128)S(1)}) custom-call(bf16[192,32768]{1,0:T(8,128)(2,1)} %refs_7_.27, f32[192,128]{1,0:T(8,128)S(1)} %get-tuple-element.81.refs_1_, f32[16,1,2048]{2,1,0:T(1,128)S(1)} %all-to-all-done.5.refs_2_), custom_call_target="tpu_custom_call" | custom-call | tf_op jit(solution)/shard_map/row_sums/pallas_call | solution.py:159
  205.2 2.1 collective-permute-done.4
  207.4 18.9 %student_stats.1 = (f32[8,192]{1,0:T(8,128)S(1)}, f32[8,192]{1,0:T(8,128)S(1)}) custom-call(bf16[768,192]{1,0:T(8,128)(2,1)S(1)} %copy.80.u_ref, f32[32768,256]{1,0:T(8,128)} %all-gather.2.cloned.1.call-done.w_ref.refs_8_.refs_10_.refs_11_), custom_call_target="tpu_custom_call" | custom-call | tf_op jit(solution)/shard_map/student_stats/pallas_call | solution.py:220
  229.1 4.4 %grad_blocks.18 = (f32[256,1024]{1,0:T(8,128)}, f32[192,256]{1,0:T(8,128)S(1)}) custom-call(s32[33]{0:T(128)S(1)} %dynamic-slice_bitcast_fusion.refs_0_, bf16[192,768]{1,0:T(8,128)(2,1)S(1)} %get-tuple-element.144.refs_1_, bf16[256,576]{1,0:T(8,128)(2,1)S(1)} %copy.102.refs_2_, f32[192,128]{1,0:T(8,128)S(1)} %broadcast_in_dim.96.refs_3_, ...), custom_call_target="tpu_custom_call" | custom-call | tf_op jit(solution)/shard_map/grad_blocks/pallas_call | solution.py:294
  233.5 3.5 collective-permute-start.5
  237.0 4.4 %grad_blocks.19 = (f32[256,1024]{1,0:T(8,128)}, f32[192,256]{1,0:T(8,128)S(1)}) custom-call(s32[33]{0:T(128)S(1)} %dynamic-slice_bitcast_fusion.refs_0_, bf16[192,768]{1,0:T(8,128)(2,1)S(1)} %get-tuple-element.144.refs_1_, bf16[256,576]{1,0:T(8,128)(2,1)S(1)} %copy.102.refs_2_, f32[192,128]{1,0:T(8,128)S(1)} %broadcast_in_dim.96.refs_3_, ...), custom_call_target="tpu_custom_call" | custom-call | tf_op jit(solution)/shard_map/grad_blocks/pallas_call | solution.py:294
  242.4 6.5 %grad_blocks.20 = (f32[256,1024]{1,0:T(8,128)}, f32[256,1024]{1,0:T(8,128)}, f32[192,256]{1,0:T(8,128)S(1)}) custom-call(s32[33]{0:T(128)S(1)} %dynamic-slice_bitcast_fusion.refs_0_, bf16[192,768]{1,0:T(8,128)(2,1)S(1)} %get-tuple-element.144.refs_1_, bf16[256,576]{1,0:T(8,128)(2,1)S(1)} %copy.102.refs_2_, f32[192,128]{1,0:T(8,128)S(1)} %broadcast_in_dim.96.refs_3_, ...), custom_call_target="tpu_custom_call" | custom-call | tf_op jit(solution)/shard_map/grad_blocks/pallas_call | solution.py:294
  250.4 6.5 %grad_blocks.21 = (f32[256,1024]{1,0:T(8,128)}, f32[256,1024]{1,0:T(8,128)}, f32[192,256]{1,0:T(8,128)S(1)}) custom-call(s32[33]{0:T(128)S(1)} %dynamic-slice_bitcast_fusion.refs_0_, bf16[192,768]{1,0:T(8,128)(2,1)S(1)} %get-tuple-element.144.refs_1_, bf16[256,576]{1,0:T(8,128)(2,1)S(1)} %copy.102.refs_2_, f32[192,128]{1,0:T(8,128)S(1)} %broadcast_in_dim.96.refs_3_, ...), custom_call_target="tpu_custom_call" | custom-call | tf_op jit(solution)/shard_map/grad_blocks/pallas_call | solution.py:294
  258.7 2.3 collective-permute-done.7.refs_12_
  261.0 2.7 collective-permute-done.8.refs_13_
  263.7 4.6 %copy-done.2 = bf16[192,32768]{1,0:T(8,128)(2,1)S(1)} copy-done((bf16[192,32768]{1,0:T(8,128)(2,1)S(1)}, bf16[192,32768]{1,0:T(8,128)(2,1)}, u32[]{:S(2)}) %copy-start.2) | copy-done | bytes 12582936
  268.3 5.5 %grad_blocks.22 = (f32[256,1024]{1,0:T(8,128)S(1)}, f32[256,1024]{1,0:T(8,128)S(1)}, f32[192,256]{1,0:T(8,128)S(1)}) custom-call(s32[33]{0:T(128)S(1)} %dynamic-slice_bitcast_fusion.refs_0_, bf16[192,768]{1,0:T(8,128)(2,1)S(1)} %get-tuple-element.144.refs_1_, bf16[256,576]{1,0:T(8,128)(2,1)S(1)} %copy.102.refs_2_, f32[192,128]{1,0:T(8,128)S(1)} %broadcast_in_dim.96.refs_3_, ...), custom_call_target="tpu_custom_call" | custom-call | tf_op jit(solution)/shard_map/grad_blocks/pallas_call | solution.py:294
  274.7 5.5 %grad_blocks.23 = (f32[256,1024]{1,0:T(8,128)S(1)}, f32[256,1024]{1,0:T(8,128)S(1)}, f32[192,256]{1,0:T(8,128)S(1)}) custom-call(s32[33]{0:T(128)S(1)} %dynamic-slice_bitcast_fusion.refs_0_, bf16[192,768]{1,0:T(8,128)(2,1)S(1)} %get-tuple-element.144.refs_1_, bf16[256,576]{1,0:T(8,128)(2,1)S(1)} %copy.102.refs_2_, f32[192,128]{1,0:T(8,128)S(1)} %broadcast_in_dim.96.refs_3_, ...), custom_call_target="tpu_custom_call" | custom-call | tf_op jit(solution)/shard_map/grad_blocks/pallas_call | solution.py:294
  281.9 3.7 grad_blocks.24
  285.6 2.8 collective-permute-done.12.refs_13_
  288.4 5.5 %grad_blocks.25 = (f32[256,1024]{1,0:T(8,128)S(1)}, f32[256,1024]{1,0:T(8,128)S(1)}, f32[192,256]{1,0:T(8,128)S(1)}) custom-call(s32[33]{0:T(128)S(1)} %dynamic-slice_bitcast_fusion.refs_0_, bf16[192,768]{1,0:T(8,128)(2,1)S(1)} %get-tuple-element.144.refs_1_, bf16[256,576]{1,0:T(8,128)(2,1)S(1)} %copy.102.refs_2_, f32[192,128]{1,0:T(8,128)S(1)} %broadcast_in_dim.96.refs_3_, ...), custom_call_target="tpu_custom_call" | custom-call | tf_op jit(solution)/shard_map/grad_blocks/pallas_call | solution.py:294
  294.5 2.3 collective-permute-done.13.refs_12_
  296.8 2.8 collective-permute-done.14.refs_13_
  299.6 5.5 %grad_blocks.26 = (f32[256,1024]{1,0:T(8,128)S(1)}, f32[256,1024]{1,0:T(8,128)S(1)}, f32[192,256]{1,0:T(8,128)S(1)}) custom-call(s32[33]{0:T(128)S(1)} %dynamic-slice_bitcast_fusion.refs_0_, bf16[192,768]{1,0:T(8,128)(2,1)S(1)} %get-tuple-element.144.refs_1_, bf16[256,576]{1,0:T(8,128)(2,1)S(1)} %copy.102.refs_2_, f32[192,128]{1,0:T(8,128)S(1)} %broadcast_in_dim.96.refs_3_, ...), custom_call_target="tpu_custom_call" | custom-call | tf_op jit(solution)/shard_map/grad_blocks/pallas_call | solution.py:294
  305.7 3.7 grad_blocks.27
  310.9 6.5 %grad_blocks.28 = (f32[256,1024]{1,0:T(8,128)}, f32[256,1024]{1,0:T(8,128)}, f32[192,256]{1,0:T(8,128)S(1)}) custom-call(s32[33]{0:T(128)S(1)} %dynamic-slice_bitcast_fusion.refs_0_, bf16[192,768]{1,0:T(8,128)(2,1)S(1)} %get-tuple-element.144.refs_1_, bf16[256,576]{1,0:T(8,128)(2,1)S(1)} %copy.102.refs_2_, f32[192,128]{1,0:T(8,128)S(1)} %broadcast_in_dim.96.refs_3_, ...), custom_call_target="tpu_custom_call" | custom-call | tf_op jit(solution)/shard_map/grad_blocks/pallas_call | solution.py:294
  319.3 2.8 collective-permute-done.18.refs_13_
  324.5 5.9 %grad_blocks.29 = (f32[256,1024]{1,0:T(8,128)S(1)}, f32[256,1024]{1,0:T(8,128)S(1)}, f32[192,256]{1,0:T(8,128)S(1)}) custom-call(s32[33]{0:T(128)S(1)} %dynamic-slice_bitcast_fusion.refs_0_, bf16[192,768]{1,0:T(8,128)(2,1)S(1)} %get-tuple-element.144.refs_1_, bf16[256,576]{1,0:T(8,128)(2,1)S(1)} %copy.102.refs_2_, f32[192,128]{1,0:T(8,128)S(1)} %broadcast_in_dim.96.refs_3_, ...), custom_call_target="tpu_custom_call" | custom-call | tf_op jit(solution)/shard_map/grad_blocks/pallas_call | solution.py:294
  331.0 2.1 collective-permute-done.20.refs_13_
  333.1 5.8 %grad_blocks.30 = (f32[256,1024]{1,0:T(8,128)S(1)}, f32[256,1024]{1,0:T(8,128)S(1)}, f32[192,256]{1,0:T(8,128)S(1)}) custom-call(s32[33]{0:T(128)S(1)} %dynamic-slice_bitcast_fusion.refs_0_, bf16[192,768]{1,0:T(8,128)(2,1)S(1)} %get-tuple-element.144.refs_1_, bf16[256,576]{1,0:T(8,128)(2,1)S(1)} %copy.102.refs_2_, f32[192,128]{1,0:T(8,128)S(1)} %broadcast_in_dim.96.refs_3_, ...), custom_call_target="tpu_custom_call" | custom-call | tf_op jit(solution)/shard_map/grad_blocks/pallas_call | solution.py:294
  339.7 2.5 collective-permute-done.21.refs_12_
  342.2 2.8 collective-permute-done.22.refs_13_
  345.1 5.8 %grad_blocks.31 = (f32[256,1024]{1,0:T(8,128)S(1)}, f32[256,1024]{1,0:T(8,128)S(1)}, f32[192,256]{1,0:T(8,128)S(1)}) custom-call(s32[33]{0:T(128)S(1)} %dynamic-slice_bitcast_fusion.refs_0_, bf16[192,768]{1,0:T(8,128)(2,1)S(1)} %get-tuple-element.144.refs_1_, bf16[256,576]{1,0:T(8,128)(2,1)S(1)} %copy.102.refs_2_, f32[192,128]{1,0:T(8,128)S(1)} %broadcast_in_dim.96.refs_3_, ...), custom_call_target="tpu_custom_call" | custom-call | tf_op jit(solution)/shard_map/grad_blocks/pallas_call | solution.py:294
  351.5 1.9 collective-permute-done.23.refs_12_
  353.4 2.8 collective-permute-done.24.refs_13_
  356.3 5.8 %grad_blocks.32 = (f32[256,1024]{1,0:T(8,128)S(1)}, f32[256,1024]{1,0:T(8,128)S(1)}, f32[192,256]{1,0:T(8,128)S(1)}) custom-call(s32[33]{0:T(128)S(1)} %dynamic-slice_bitcast_fusion.refs_0_, bf16[192,768]{1,0:T(8,128)(2,1)S(1)} %get-tuple-element.144.refs_1_, bf16[256,576]{1,0:T(8,128)(2,1)S(1)} %copy.102.refs_2_, f32[192,128]{1,0:T(8,128)S(1)} %broadcast_in_dim.96.refs_3_, ...), custom_call_target="tpu_custom_call" | custom-call | tf_op jit(solution)/shard_map/grad_blocks/pallas_call | solution.py:294
  362.7 1.9 collective-permute-done.25.refs_12_
  364.7 2.8 collective-permute-done.26.refs_13_
  367.6 6.4 %grad_blocks.33 = (f32[256,1024]{1,0:T(8,128)}, f32[256,1024]{1,0:T(8,128)S(1)}, f32[192,256]{1,0:T(8,128)S(1)}) custom-call(s32[33]{0:T(128)S(1)} %dynamic-slice_bitcast_fusion.refs_0_, bf16[192,768]{1,0:T(8,128)(2,1)S(1)} %get-tuple-element.144.refs_1_, bf16[256,576]{1,0:T(8,128)(2,1)S(1)} %copy.102.refs_2_, f32[192,128]{1,0:T(8,128)S(1)} %broadcast_in_dim.96.refs_3_, ...), custom_call_target="tpu_custom_call" | custom-call | tf_op jit(solution)/shard_map/grad_blocks/pallas_call | solution.py:294
  375.9 2.8 collective-permute-done.28.refs_13_
  381.1 6.7 %grad_blocks.34 = (f32[256,1024]{1,0:T(8,128)}, f32[256,1024]{1,0:T(8,128)}, f32[192,256]{1,0:T(8,128)S(1)}) custom-call(s32[33]{0:T(128)S(1)} %dynamic-slice_bitcast_fusion.refs_0_, bf16[192,768]{1,0:T(8,128)(2,1)S(1)} %get-tuple-element.144.refs_1_, bf16[256,576]{1,0:T(8,128)(2,1)S(1)} %copy.102.refs_2_, f32[192,128]{1,0:T(8,128)S(1)} %broadcast_in_dim.96.refs_3_, ...), custom_call_target="tpu_custom_call" | custom-call | tf_op jit(solution)/shard_map/grad_blocks/pallas_call | solution.py:294
  389.7 6.3 %grad_blocks.35 = (f32[256,1024]{1,0:T(8,128)}, f32[256,1024]{1,0:T(8,128)}, f32[192,256]{1,0:T(8,128)S(1)}) custom-call(s32[33]{0:T(128)S(1)} %dynamic-slice_bitcast_fusion.refs_0_, bf16[192,768]{1,0:T(8,128)(2,1)S(1)} %get-tuple-element.144.refs_1_, bf16[256,576]{1,0:T(8,128)(2,1)S(1)} %copy.102.refs_2_, f32[192,128]{1,0:T(8,128)S(1)} %broadcast_in_dim.96.refs_3_, ...), custom_call_target="tpu_custom_call" | custom-call | tf_op jit(solution)/shard_map/grad_blocks/pallas_call | solution.py:294
  399.8 2.8 collective-permute-done.33.c
  402.6 3.0 proto_grads.2
  406.6 2.3 scatter_custom_fusion
  408.9 2.2 collective-permute-done.34.b
  411.1 2.5 collective-permute-done.35.c
  414.9 2.9 proto_grads.3
  (199 shorter events, 44.6 us)
Async XLA Ops:
  7.2 101.1 %copy-start = (f32[1024,256]{1,0:T(8,128)S(1)}, f32[1024,256]{1,0:T(8,128)}, u32[]{:S(2)}) copy-start(f32[1024,256]{1,0:T(8,128)} %param.7) | copy-start | bytes 3145732
  7.2 200.2 %all-gather.2.cloned.1.call-start = ((), (), s32[]{:S(2)}) async-start(), calls=%async_computation.6 | async-start | bytes 35651584 | tf_op jit(solution)/shard_map/all_gather | solution.py:450
  24.4 3.5 collective-permute-start.1
  58.4 13.9 %all-to-all-start.1 = ((f32[16,1,2048]{2,1,0:T(1,128)}), f32[16,1,2048]{2,1,0:T(1,128)S(1)}, u32[]{:S(2)}, u32[]{:S(2)}) async-start(f32[16,1,2048]{2,1,0:T(1,128)} %broadcast_in_dim.102), calls=%async_computation.1 | async-start | bytes 262144 | tf_op jit(solution)/shard_map/all_to_all | solution.py:389
  72.3 14.2 %copy-start.23 = (s32[3]{0:T(128)S(1)}, s32[3]{0:T(128)}, u32[]{:S(2)}) copy-start(s32[3]{0:T(128)} %param.8) | copy-start | bytes 40
  85.3 3.9 collective-permute-start.2
  86.5 21.1 %copy-start.22 = (s32[192]{0:T(256)S(1)}, s32[192]{0:T(256)}, u32[]{:S(2)}) copy-start(s32[192]{0:T(256)} %param.9) | copy-start | bytes 2308
  102.4 14.6 %all-to-all-start.2 = ((f32[16,1,2048]{2,1,0:T(1,128)}), f32[16,1,2048]{2,1,0:T(1,128)S(1)}, u32[]{:S(2)}, u32[]{:S(2)}) async-start(f32[16,1,2048]{2,1,0:T(1,128)} %get-tuple-element.79), calls=%async_computation.2 | async-start | bytes 262144 | tf_op jit(solution)/shard_map/all_to_all | solution.py:388
  117.8 13.9 %all-to-all-start.3 = ((f32[16,1,2048]{2,1,0:T(1,128)}), f32[16,1,2048]{2,1,0:T(1,128)S(1)}, u32[]{:S(2)}, u32[]{:S(2)}) async-start(f32[16,1,2048]{2,1,0:T(1,128)} %broadcast_in_dim.103), calls=%async_computation.3 | async-start | bytes 262144 | tf_op jit(solution)/shard_map/all_to_all | solution.py:389
  122.5 23.1 %copy-start.19 = (f32[192]{0:T(256)}, f32[192]{0:T(256)S(1)}, u32[]{:S(2)}) copy-start(f32[192]{0:T(256)S(1)} %add_rsqrt_fusion) | copy-start | bytes 2308
  144.5 3.9 collective-permute-start.3
  145.8 21.4 %copy-start.3 = (f32[192,256]{1,0:T(8,128)}, f32[192,256]{1,0:T(8,128)S(1)}, u32[]{:S(2)}) copy-start(f32[192,256]{1,0:T(8,128)S(1)} %get-tuple-element.140.unit) | copy-start | bytes 589828
  161.6 14.9 %all-to-all-start.4 = ((f32[16,1,2048]{2,1,0:T(1,128)}), f32[16,1,2048]{2,1,0:T(1,128)S(1)}, u32[]{:S(2)}, u32[]{:S(2)}) async-start(f32[16,1,2048]{2,1,0:T(1,128)} %get-tuple-element.82), calls=%async_computation.4 | async-start | bytes 262144 | tf_op jit(solution)/shard_map/all_to_all | solution.py:388
  177.3 14.0 %all-to-all-start.5 = ((f32[16,1,2048]{2,1,0:T(1,128)}), f32[16,1,2048]{2,1,0:T(1,128)S(1)}, u32[]{:S(2)}, u32[]{:S(2)}) async-start(f32[16,1,2048]{2,1,0:T(1,128)} %broadcast_in_dim.104), calls=%async_computation.5 | async-start | bytes 262144 | tf_op jit(solution)/shard_map/all_to_all | solution.py:389
  203.8 3.5 collective-permute-start.4
  226.4 2.5 collective-permute-start
  233.5 7.9 %collective-permute-start.5 = (f32[256,1024]{1,0:T(8,128)}, f32[256,1024]{1,0:T(8,128)S(1)}, u32[]{:S(2)}, u32[]{:S(2)}) collective-permute-start(f32[256,1024]{1,0:T(8,128)} %get-tuple-element.87), channel_id=1, source_target_pairs={{0,2},{2,0},{4,6},{6,4},{8,10},{10,8},{12,14},{14,12},{16,18},{18,... | collective-permute-start | bytes 3145736 | tf_op jit(solution)/shard_map/ppermute | solution.py:377
  241.4 8.1 %collective-permute-start.6 = (f32[256,1024]{1,0:T(8,128)}, f32[256,1024]{1,0:T(8,128)S(1)}, u32[]{:S(2)}, u32[]{:S(2)}) collective-permute-start(f32[256,1024]{1,0:T(8,128)} %get-tuple-element.89), channel_id=1, source_target_pairs={{0,2},{2,0},{4,6},{6,4},{8,10},{10,8},{12,14},{14,12},{16,18},{18,... | collective-permute-start | bytes 3145736 | tf_op jit(solution)/shard_map/ppermute | solution.py:377
  248.9 12.1 %collective-permute-start.7 = (f32[256,1024]{1,0:T(8,128)}, f32[256,1024]{1,0:T(8,128)S(1)}, u32[]{:S(2)}, u32[]{:S(2)}) collective-permute-start(f32[256,1024]{1,0:T(8,128)} %get-tuple-element.91), channel_id=1, source_target_pairs={{0,2},{2,8},{4,6},{6,0},{8,10},{10,16},{12,14},{14,4},{16,18},{18,... | collective-permute-start | bytes 3145736 | tf_op jit(solution)/shard_map/ppermute | solution.py:513
  248.9 14.8 %collective-permute-start.8 = (f32[256,1024]{1,0:T(8,128)}, f32[256,1024]{1,0:T(8,128)S(1)}, u32[]{:S(2)}, u32[]{:S(2)}) collective-permute-start(f32[256,1024]{1,0:T(8,128)} %get-tuple-element.92), channel_id=1, source_target_pairs={{0,6},{2,0},{4,14},{6,4},{8,2},{10,8},{12,22},{14,12},{16,10},{18,... | collective-permute-start | bytes 3145736 | tf_op jit(solution)/shard_map/ppermute | solution.py:514
  257.0 17.4 %collective-permute-start.9 = (f32[256,1024]{1,0:T(8,128)}, f32[256,1024]{1,0:T(8,128)S(1)}, u32[]{:S(2)}, u32[]{:S(2)}) collective-permute-start(f32[256,1024]{1,0:T(8,128)} %get-tuple-element.94), channel_id=1, source_target_pairs={{0,2},{2,8},{4,6},{6,0},{8,10},{10,16},{12,14},{14,4},{16,18},{18,... | collective-permute-start | bytes 3145736 | tf_op jit(solution)/shard_map/ppermute | solution.py:513
  258.2 16.5 %collective-permute-start.10 = (f32[256,1024]{1,0:T(8,128)}, f32[256,1024]{1,0:T(8,128)S(1)}, u32[]{:S(2)}, u32[]{:S(2)}) collective-permute-start(f32[256,1024]{1,0:T(8,128)} %get-tuple-element.95), channel_id=1, source_target_pairs={{0,6},{2,0},{4,14},{6,4},{8,2},{10,8},{12,22},{14,12},{16,10},{18,... | collective-permute-start | bytes 3145736 | tf_op jit(solution)/shard_map/ppermute | solution.py:514
  273.8 11.8 %collective-permute-start.11 = (f32[256,1024]{1,0:T(8,128)S(1)}, f32[256,1024]{1,0:T(8,128)S(1)}, u32[]{:S(2)}, u32[]{:S(2)}) collective-permute-start(f32[256,1024]{1,0:T(8,128)S(1)} %get-tuple-element.98), channel_id=1, source_target_pairs={{0,2},{2,8},{4,6},{6,0},{8,10},{10,16},{12,14},{14,4},{16,18},{18,... | collective-permute-start | bytes 3145736 | tf_op jit(solution)/shard_map/ppermute | solution.py:513
  273.8 14.6 %collective-permute-start.12 = (f32[256,1024]{1,0:T(8,128)S(1)}, f32[256,1024]{1,0:T(8,128)S(1)}, u32[]{:S(2)}, u32[]{:S(2)}) collective-permute-start(f32[256,1024]{1,0:T(8,128)S(1)} %get-tuple-element.99), channel_id=1, source_target_pairs={{0,6},{2,0},{4,14},{6,4},{8,2},{10,8},{12,22},{14,12},{16,10},{18,... | collective-permute-start | bytes 3145736 | tf_op jit(solution)/shard_map/ppermute | solution.py:514
  280.2 16.6 %collective-permute-start.13 = (f32[256,1024]{1,0:T(8,128)S(1)}, f32[256,1024]{1,0:T(8,128)S(1)}, u32[]{:S(2)}, u32[]{:S(2)}) collective-permute-start(f32[256,1024]{1,0:T(8,128)S(1)} %get-tuple-element.101), channel_id=1, source_target_pairs={{0,2},{2,8},{4,6},{6,0},{8,10},{10,16},{12,14},{14,4},{16,18},{18,... | collective-permute-start | bytes 3145736 | tf_op jit(solution)/shard_map/ppermute | solution.py:513
  281.2 18.4 %collective-permute-start.14 = (f32[256,1024]{1,0:T(8,128)S(1)}, f32[256,1024]{1,0:T(8,128)S(1)}, u32[]{:S(2)}, u32[]{:S(2)}) collective-permute-start(f32[256,1024]{1,0:T(8,128)S(1)} %get-tuple-element.102), channel_id=1, source_target_pairs={{0,6},{2,0},{4,14},{6,4},{8,2},{10,8},{12,22},{14,12},{16,10},{18,... | collective-permute-start | bytes 3145736 | tf_op jit(solution)/shard_map/ppermute | solution.py:514
  293.9 15.5 %collective-permute-start.15 = (f32[256,1024]{1,0:T(8,128)S(1)}, f32[256,1024]{1,0:T(8,128)S(1)}, u32[]{:S(2)}, u32[]{:S(2)}) collective-permute-start(f32[256,1024]{1,0:T(8,128)S(1)} %get-tuple-element.105), channel_id=1, source_target_pairs={{0,2},{2,8},{4,6},{6,0},{8,10},{10,16},{12,14},{14,4},{16,18},{18,... | collective-permute-start | bytes 3145736 | tf_op jit(solution)/shard_map/ppermute | solution.py:513
  294.0 16.9 %collective-permute-start.16 = (f32[256,1024]{1,0:T(8,128)S(1)}, f32[256,1024]{1,0:T(8,128)S(1)}, u32[]{:S(2)}, u32[]{:S(2)}) collective-permute-start(f32[256,1024]{1,0:T(8,128)S(1)} %get-tuple-element.106), channel_id=1, source_target_pairs={{0,6},{2,0},{4,14},{6,4},{8,2},{10,8},{12,22},{14,12},{16,10},{18,... | collective-permute-start | bytes 3145736 | tf_op jit(solution)/shard_map/ppermute | solution.py:514
  305.1 14.1 %collective-permute-start.17 = (f32[256,1024]{1,0:T(8,128)S(1)}, f32[256,1024]{1,0:T(8,128)S(1)}, u32[]{:S(2)}, u32[]{:S(2)}) collective-permute-start(f32[256,1024]{1,0:T(8,128)S(1)} %get-tuple-element.108), channel_id=1, source_target_pairs={{0,2},{2,8},{4,6},{6,0},{8,10},{10,16},{12,14},{14,4},{16,18},{18,... | collective-permute-start | bytes 3145736 | tf_op jit(solution)/shard_map/ppermute | solution.py:513
  305.2 16.9 %collective-permute-start.18 = (f32[256,1024]{1,0:T(8,128)S(1)}, f32[256,1024]{1,0:T(8,128)S(1)}, u32[]{:S(2)}, u32[]{:S(2)}) collective-permute-start(f32[256,1024]{1,0:T(8,128)S(1)} %get-tuple-element.109), channel_id=1, source_target_pairs={{0,6},{2,0},{4,14},{6,4},{8,2},{10,8},{12,22},{14,12},{16,10},{18,... | collective-permute-start | bytes 3145736 | tf_op jit(solution)/shard_map/ppermute | solution.py:514
  310.9 12.2 %slice-start = ((s8[12582912]{0:T(1024)(128)(4,1)}), s8[4194304]{0:T(1024)(128)(4,1)S(1)}, s32[]{:S(2)}) async-start(s8[12582912]{0:T(1024)(128)(4,1)} %bitcast.21), calls=%async_computation.7 | async-start | bytes 8388608
  310.9 12.2 %slice-start.1 = ((s8[12582912]{0:T(1024)(128)(4,1)}), s8[4194304]{0:T(1024)(128)(4,1)S(1)}, s32[]{:S(2)}) async-start(s8[12582912]{0:T(1024)(128)(4,1)} %bitcast.21), calls=%async_computation.8 | async-start | bytes 8388608
  310.9 12.2 %slice-start.2 = ((s8[12582912]{0:T(1024)(128)(4,1)}), s8[4194304]{0:T(1024)(128)(4,1)S(1)}, s32[]{:S(2)}) async-start(s8[12582912]{0:T(1024)(128)(4,1)} %bitcast.21), calls=%async_computation.9 | async-start | bytes 8388608
  317.3 13.6 %collective-permute-start.19 = (f32[256,1024]{1,0:T(8,128)}, f32[256,1024]{1,0:T(8,128)S(1)}, u32[]{:S(2)}, u32[]{:S(2)}) collective-permute-start(f32[256,1024]{1,0:T(8,128)} %get-tuple-element.111), channel_id=1, source_target_pairs={{0,2},{2,8},{4,6},{6,0},{8,10},{10,16},{12,14},{14,4},{16,18},{18,... | collective-permute-start | bytes 3145736 | tf_op jit(solution)/shard_map/ppermute | solution.py:513
  317.6 15.4 %collective-permute-start.20 = (f32[256,1024]{1,0:T(8,128)}, f32[256,1024]{1,0:T(8,128)S(1)}, u32[]{:S(2)}, u32[]{:S(2)}) collective-permute-start(f32[256,1024]{1,0:T(8,128)} %get-tuple-element.112), channel_id=1, source_target_pairs={{0,6},{2,0},{4,14},{6,4},{8,2},{10,8},{12,22},{14,12},{16,10},{18,... | collective-permute-start | bytes 3145736 | tf_op jit(solution)/shard_map/ppermute | solution.py:514
  323.1 10.0 %slice-start.3 = ((s8[12582912]{0:T(1024)(128)(4,1)}), s8[4194304]{0:T(1024)(128)(4,1)S(1)}, s32[]{:S(2)}) async-start(s8[12582912]{0:T(1024)(128)(4,1)} %bitcast.23), calls=%async_computation.10 | async-start | bytes 8388608
  330.4 11.8 %collective-permute-start.21 = (f32[256,1024]{1,0:T(8,128)S(1)}, f32[256,1024]{1,0:T(8,128)S(1)}, u32[]{:S(2)}, u32[]{:S(2)}) collective-permute-start(f32[256,1024]{1,0:T(8,128)S(1)} %get-tuple-element.114), channel_id=1, source_target_pairs={{0,2},{2,8},{4,6},{6,0},{8,10},{10,16},{12,14},{14,4},{16,18},{18,... | collective-permute-start | bytes 3145736 | tf_op jit(solution)/shard_map/ppermute | solution.py:513
  330.5 14.6 %collective-permute-start.22 = (f32[256,1024]{1,0:T(8,128)S(1)}, f32[256,1024]{1,0:T(8,128)S(1)}, u32[]{:S(2)}, u32[]{:S(2)}) collective-permute-start(f32[256,1024]{1,0:T(8,128)S(1)} %get-tuple-element.115), channel_id=1, source_target_pairs={{0,6},{2,0},{4,14},{6,4},{8,2},{10,8},{12,22},{14,12},{16,10},{18,... | collective-permute-start | bytes 3145736 | tf_op jit(solution)/shard_map/ppermute | solution.py:514
  333.1 12.0 %slice-start.6 = ((s8[12582912]{0:T(1024)(128)(4,1)}), s8[4194304]{0:T(1024)(128)(4,1)S(1)}, s32[]{:S(2)}) async-start(s8[12582912]{0:T(1024)(128)(4,1)} %bitcast.25), calls=%async_computation.13 | async-start | bytes 8388608
  333.1 12.0 %slice-start.7 = ((s8[12582912]{0:T(1024)(128)(4,1)}), s8[4194304]{0:T(1024)(128)(4,1)S(1)}, s32[]{:S(2)}) async-start(s8[12582912]{0:T(1024)(128)(4,1)} %bitcast.25), calls=%async_computation.14 | async-start | bytes 8388608
  333.1 12.0 %slice-start.8 = ((s8[12582912]{0:T(1024)(128)(4,1)}), s8[4194304]{0:T(1024)(128)(4,1)S(1)}, s32[]{:S(2)}) async-start(s8[12582912]{0:T(1024)(128)(4,1)} %bitcast.25), calls=%async_computation.15 | async-start | bytes 8388608
  338.9 14.5 %collective-permute-start.23 = (f32[256,1024]{1,0:T(8,128)S(1)}, f32[256,1024]{1,0:T(8,128)S(1)}, u32[]{:S(2)}, u32[]{:S(2)}) collective-permute-start(f32[256,1024]{1,0:T(8,128)S(1)} %get-tuple-element.117), channel_id=1, source_target_pairs={{0,2},{2,8},{4,6},{6,0},{8,10},{10,16},{12,14},{14,4},{16,18},{18,... | collective-permute-start | bytes 3145736 | tf_op jit(solution)/shard_map/ppermute | solution.py:513
  339.0 17.3 %collective-permute-start.24 = (f32[256,1024]{1,0:T(8,128)S(1)}, f32[256,1024]{1,0:T(8,128)S(1)}, u32[]{:S(2)}, u32[]{:S(2)}) collective-permute-start(f32[256,1024]{1,0:T(8,128)S(1)} %get-tuple-element.118), channel_id=1, source_target_pairs={{0,6},{2,0},{4,14},{6,4},{8,2},{10,8},{12,22},{14,12},{16,10},{18,... | collective-permute-start | bytes 3145736 | tf_op jit(solution)/shard_map/ppermute | solution.py:514
  345.0 11.2 %slice-start.9 = ((s8[12582912]{0:T(1024)(128)(4,1)}), s8[4194304]{0:T(1024)(128)(4,1)S(1)}, s32[]{:S(2)}) async-start(s8[12582912]{0:T(1024)(128)(4,1)} %bitcast.27), calls=%async_computation.16 | async-start | bytes 8388608
  345.1 11.2 %slice-start.10 = ((s8[12582912]{0:T(1024)(128)(4,1)}), s8[4194304]{0:T(1024)(128)(4,1)S(1)}, s32[]{:S(2)}) async-start(s8[12582912]{0:T(1024)(128)(4,1)} %bitcast.27), calls=%async_computation.17 | async-start | bytes 8388608
  345.1 11.2 %slice-start.11 = ((s8[12582912]{0:T(1024)(128)(4,1)}), s8[4194304]{0:T(1024)(128)(4,1)S(1)}, s32[]{:S(2)}) async-start(s8[12582912]{0:T(1024)(128)(4,1)} %bitcast.27), calls=%async_computation.18 | async-start | bytes 8388608
  350.9 13.7 %collective-permute-start.25 = (f32[256,1024]{1,0:T(8,128)S(1)}, f32[256,1024]{1,0:T(8,128)S(1)}, u32[]{:S(2)}, u32[]{:S(2)}) collective-permute-start(f32[256,1024]{1,0:T(8,128)S(1)} %get-tuple-element.120), channel_id=1, source_target_pairs={{0,2},{2,8},{4,6},{6,0},{8,10},{10,16},{12,14},{14,4},{16,18},{18,... | collective-permute-start | bytes 3145736 | tf_op jit(solution)/shard_map/ppermute | solution.py:513
  351.0 16.5 %collective-permute-start.26 = (f32[256,1024]{1,0:T(8,128)S(1)}, f32[256,1024]{1,0:T(8,128)S(1)}, u32[]{:S(2)}, u32[]{:S(2)}) collective-permute-start(f32[256,1024]{1,0:T(8,128)S(1)} %get-tuple-element.121), channel_id=1, source_target_pairs={{0,6},{2,0},{4,14},{6,4},{8,2},{10,8},{12,22},{14,12},{16,10},{18,... | collective-permute-start | bytes 3145736 | tf_op jit(solution)/shard_map/ppermute | solution.py:514
  356.3 11.2 %slice-start.12 = ((s8[12582912]{0:T(1024)(128)(4,1)}), s8[4194304]{0:T(1024)(128)(4,1)S(1)}, s32[]{:S(2)}) async-start(s8[12582912]{0:T(1024)(128)(4,1)} %bitcast.29), calls=%async_computation.19 | async-start | bytes 8388608
  356.3 11.2 %slice-start.13 = ((s8[12582912]{0:T(1024)(128)(4,1)}), s8[4194304]{0:T(1024)(128)(4,1)S(1)}, s32[]{:S(2)}) async-start(s8[12582912]{0:T(1024)(128)(4,1)} %bitcast.29), calls=%async_computation.20 | async-start | bytes 8388608
  356.3 11.2 %slice-start.14 = ((s8[12582912]{0:T(1024)(128)(4,1)}), s8[4194304]{0:T(1024)(128)(4,1)S(1)}, s32[]{:S(2)}) async-start(s8[12582912]{0:T(1024)(128)(4,1)} %bitcast.29), calls=%async_computation.21 | async-start | bytes 8388608
  362.2 13.7 %collective-permute-start.27 = (f32[256,1024]{1,0:T(8,128)S(1)}, f32[256,1024]{1,0:T(8,128)S(1)}, u32[]{:S(2)}, u32[]{:S(2)}) collective-permute-start(f32[256,1024]{1,0:T(8,128)S(1)} %get-tuple-element.123), channel_id=1, source_target_pairs={{0,2},{2,8},{4,6},{6,0},{8,10},{10,16},{12,14},{14,4},{16,18},{18,... | collective-permute-start | bytes 3145736 | tf_op jit(solution)/shard_map/ppermute | solution.py:513
  362.2 16.5 %collective-permute-start.28 = (f32[256,1024]{1,0:T(8,128)S(1)}, f32[256,1024]{1,0:T(8,128)S(1)}, u32[]{:S(2)}, u32[]{:S(2)}) collective-permute-start(f32[256,1024]{1,0:T(8,128)S(1)} %get-tuple-element.124), channel_id=1, source_target_pairs={{0,6},{2,0},{4,14},{6,4},{8,2},{10,8},{12,22},{14,12},{16,10},{18,... | collective-permute-start | bytes 3145736 | tf_op jit(solution)/shard_map/ppermute | solution.py:514
  367.5 12.2 %slice-start.15 = ((s8[12582912]{0:T(1024)(128)(4,1)}), s8[4194304]{0:T(1024)(128)(4,1)S(1)}, s32[]{:S(2)}) async-start(s8[12582912]{0:T(1024)(128)(4,1)} %bitcast.31), calls=%async_computation.22 | async-start | bytes 8388608
  367.5 12.2 %slice-start.16 = ((s8[12582912]{0:T(1024)(128)(4,1)}), s8[4194304]{0:T(1024)(128)(4,1)S(1)}, s32[]{:S(2)}) async-start(s8[12582912]{0:T(1024)(128)(4,1)} %bitcast.31), calls=%async_computation.23 | async-start | bytes 8388608
  367.5 12.2 %slice-start.17 = ((s8[12582912]{0:T(1024)(128)(4,1)}), s8[4194304]{0:T(1024)(128)(4,1)S(1)}, s32[]{:S(2)}) async-start(s8[12582912]{0:T(1024)(128)(4,1)} %bitcast.31), calls=%async_computation.24 | async-start | bytes 8388608
  373.9 14.4 %collective-permute-start.29 = (f32[256,1024]{1,0:T(8,128)}, f32[256,1024]{1,0:T(8,128)S(1)}, u32[]{:S(2)}, u32[]{:S(2)}) collective-permute-start(f32[256,1024]{1,0:T(8,128)} %get-tuple-element.126), channel_id=1, source_target_pairs={{0,2},{2,8},{4,6},{6,0},{8,10},{10,16},{12,14},{14,4},{16,18},{18,... | collective-permute-start | bytes 3145736 | tf_op jit(solution)/shard_map/ppermute | solution.py:513
  373.9 15.8 %collective-permute-start.30 = (f32[256,1024]{1,0:T(8,128)S(1)}, f32[256,1024]{1,0:T(8,128)S(1)}, u32[]{:S(2)}, u32[]{:S(2)}) collective-permute-start(f32[256,1024]{1,0:T(8,128)S(1)} %get-tuple-element.127), channel_id=1, source_target_pairs={{0,6},{2,0},{4,14},{6,4},{8,2},{10,8},{12,22},{14,12},{16,10},{18,... | collective-permute-start | bytes 3145736 | tf_op jit(solution)/shard_map/ppermute | solution.py:514
  379.7 10.0 %slice-start.18 = ((s8[12582912]{0:T(1024)(128)(4,1)}), s8[4194304]{0:T(1024)(128)(4,1)S(1)}, s32[]{:S(2)}) async-start(s8[12582912]{0:T(1024)(128)(4,1)} %bitcast.33), calls=%async_computation.25 | async-start | bytes 8388608
  387.8 12.1 %collective-permute-start.32 = (f32[256,1024]{1,0:T(8,128)}, f32[256,1024]{1,0:T(8,128)}, u32[]{:S(2)}, u32[]{:S(2)}) collective-permute-start(f32[256,1024]{1,0:T(8,128)} %get-tuple-element.130), channel_id=1, source_target_pairs={{0,2},{2,8},{4,6},{6,0},{8,10},{10,16},{12,14},{14,4},{16,18},{18,... | collective-permute-start | bytes 3145736 | tf_op jit(solution)/shard_map/ppermute | solution.py:513
  387.8 14.8 %collective-permute-start.33 = (f32[256,1024]{1,0:T(8,128)}, f32[256,1024]{1,0:T(8,128)}, u32[]{:S(2)}, u32[]{:S(2)}) collective-permute-start(f32[256,1024]{1,0:T(8,128)} %get-tuple-element.131), channel_id=1, source_target_pairs={{0,6},{2,0},{4,14},{6,4},{8,2},{10,8},{12,22},{14,12},{16,10},{18,... | collective-permute-start | bytes 3145736 | tf_op jit(solution)/shard_map/ppermute | solution.py:514
  396.0 15.1 %collective-permute-start.34 = (f32[256,1024]{1,0:T(8,128)}, f32[256,1024]{1,0:T(8,128)}, u32[]{:S(2)}, u32[]{:S(2)}) collective-permute-start(f32[256,1024]{1,0:T(8,128)} %get-tuple-element.134), channel_id=1, source_target_pairs={{0,2},{2,8},{4,6},{6,0},{8,10},{10,16},{12,14},{14,4},{16,18},{18,... | collective-permute-start | bytes 3145736 | tf_op jit(solution)/shard_map/ppermute | solution.py:513
  396.0 17.6 %collective-permute-start.35 = (f32[256,1024]{1,0:T(8,128)}, f32[256,1024]{1,0:T(8,128)}, u32[]{:S(2)}, u32[]{:S(2)}) collective-permute-start(f32[256,1024]{1,0:T(8,128)} %get-tuple-element.135), channel_id=1, source_target_pairs={{0,6},{2,0},{4,14},{6,4},{8,2},{10,8},{12,22},{14,12},{16,10},{18,... | collective-permute-start | bytes 3145736 | tf_op jit(solution)/shard_map/ppermute | solution.py:514
  396.5 9.1 %collective-permute-start.31 = (f32[192,256]{1,0:T(8,128)S(1)}, f32[192,256]{1,0:T(8,128)S(1)}, u32[]{:S(2)}, u32[]{:S(2)}) collective-permute-start(f32[192,256]{1,0:T(8,128)S(1)} %get-tuple-element.128.here), channel_id=1, source_target_pairs={{0,1},{1,0},{2,3},{3,2},{4,5},{5,4},{6,7},{7,6},{8,9},{9,8},{10,11... | collective-permute-start | bytes 589832 | tf_op jit(solution)/shard_map/ppermute | solution.py:377
  (23 other events, 91.5 us)
Sparse Core Ops, SparseCore 0:
  11.3 183.2 all-gather.1

commit v3 on v2

--- a/solution.py
+++ b/solution.py
@@ -24,6 +24,34 @@
 
 def params(limit=VMEM_LIMIT):
     return pltpu.CompilerParams(vmem_limit_bytes=limit)
+
+
+def teacher_block(teacher, buf, sems):
+    count, _, block = buf.shape
+    step = pl.program_id(0)
+
+    def fetch(i, start):
+        return pltpu.make_async_copy(
+            teacher.at[:, pl.ds(start, block)], buf.at[i], sems.at[i]
+        )
+
+    @pl.when(step == 0)
+    def _():
+        for i in range(count):
+            fetch(i, i * block).start()
+
+    fetch(step, pl.multiple_of(step * block, LANES)).wait()
+    return buf.at[step]
+
+
+def teacher_scratch(teacher, block):
+    tokens, width = teacher.shape
+    count = width // block
+    return [pltpu.VMEM((count, tokens, block), teacher.dtype), pltpu.SemaphoreType.DMA((count,))]
+
+
+def in_hbm(x):
+    return pltpu.with_memory_space_constraint(x, pltpu.HBM)
 
 
 def split(x):
@@ -74,10 +102,11 @@
         out_shape=[shape, shape],
         compiler_params=params(STREAM_LIMIT),
         name="teacher_stats",
-    )(teacher)
-
-
-def column_kernel(t_ref, a_ref, r1_ref, r2_ref, out_ref, new_ref, *, unroll):
+    )(in_hbm(teacher))
+
+
+def column_kernel(teacher, a_ref, r1_ref, r2_ref, out_ref, new_ref, buf, sems, *, unroll):
+    t_ref = teacher_block(teacher, buf, sems)
     tokens, block = t_ref.shape
 
     @pl.when(pl.program_id(0) == 0)
@@ -113,18 +142,20 @@
     return pl.pallas_call(
         lambda *refs: column_kernel(*refs, unroll=min(16, shard // LANES)),
         grid=(width // block,),
-        in_specs=[pl.BlockSpec((tokens, block), lambda i: (0, i)), whole, whole, whole],
+        in_specs=[pl.BlockSpec(memory_space=pltpu.HBM), whole, whole, whole],
+        scratch_shapes=teacher_scratch(teacher, block),
         out_specs=[pl.BlockSpec((1, 1, shard), lambda i: (i, 0, 0)), whole],
         out_shape=[
             jax.ShapeDtypeStruct((owners, 1, shard), F32),
             jax.ShapeDtypeStruct((tokens, LANES), F32),
         ],
-        compiler_params=params(STREAM_LIMIT),
+        compiler_params=params(),
         name="column_sums",
-    )(teacher, offset, row_here, row_there)
-
-
-def row_kernel(t_ref, a_ref, c_ref, out_ref, col_ref, *, unroll, balance):
+    )(in_hbm(teacher), offset, row_here, row_there)
+
+
+def row_kernel(teacher, a_ref, c_ref, out_ref, col_ref, buf, sems, *, unroll, balance):
+    t_ref = teacher_block(teacher, buf, sems)
     tokens, block = t_ref.shape
     span = LANES * unroll
     col_ref[...] = balance / c_ref[0]
@@ -159,15 +190,20 @@
     return pl.pallas_call(
         lambda *refs: row_kernel(*refs, unroll=min(16, block // LANES), balance=balance),
         grid=(width // block,),
-        in_specs=[pl.BlockSpec((tokens, block), lambda i: (0, i)), whole, pl.BlockSpec((1, 1, block), lambda i: (i, 0, 0))],
+        in_specs=[
+            pl.BlockSpec(memory_space=pltpu.HBM),
+            whole,
+            pl.BlockSpec((1, 1, block), lambda i: (i, 0, 0)),
+        ],
+        scratch_shapes=teacher_scratch(teacher, block),
         out_specs=[whole, cols],
         out_shape=[
             jax.ShapeDtypeStruct((tokens, LANES), F32),
             jax.ShapeDtypeStruct((1, width), F32),
         ],
-        compiler_params=params(STREAM_LIMIT),
+        compiler_params=params(),
         name="row_sums",
-    )(teacher, offset, sums)
+    )(in_hbm(teacher), offset, sums)
 
 
 def parts_of_left(hi, lo, axis):
@@ -214,7 +250,7 @@
 def student_pass(u_turned, protos):
     tokens = u_turned.shape[1]
     rows, depth = protos.shape
-    block = min(rows // 2, 4096)
+    block = min(rows // 2, 2048)
     stat = pl.BlockSpec((8, tokens), lambda i: (0, 0))
     shape = jax.ShapeDtypeStruct((8, tokens), F32)
     return pl.pallas_call(
@@ -229,19 +265,29 @@
         scratch_shapes=[pltpu.VMEM((min(block // 2, 512), tokens), F32)] * 2,
         compiler_params=params(STREAM_LIMIT),
         name="student_stats",
-    )(u_turned, protos)
-
-
-def grad_kernel(own, u_parts, t_parts, lse, offset, tok_in, *refs, blocks, arrivals, parity):
-    teach, cols, protos = refs[:blocks], refs[blocks : 2 * blocks], refs[2 * blocks : 3 * blocks]
-    arrived = refs[3 * blocks : 3 * blocks + arrivals]
-    outs = refs[3 * blocks + arrivals : 4 * blocks + arrivals]
-    tok_out = refs[4 * blocks + arrivals]
-
-    @pl.when(pl.program_id(0) == 0)
+    )(u_turned, in_hbm(protos))
+
+
+def grad_kernel(own, u_parts, t_parts, lse, offset, tok_in, teacher, *refs, slots, arrivals, parity):
+    blocks = len(slots)
+    cols, protos = refs[:blocks], refs[blocks : 2 * blocks]
+    arrived = refs[2 * blocks : 2 * blocks + arrivals]
+    outs = refs[2 * blocks + arrivals : 3 * blocks + arrivals]
+    tok_out, teach, sems = refs[3 * blocks + arrivals :]
+    width, block = teach.shape[2], protos[0].shape[0]
+    step = pl.program_id(0)
+
+    def fetch(i):
+        start = pl.multiple_of(own[slots[i]] * width, LANES)
+        return pltpu.make_async_copy(teacher.at[:, pl.ds(start, width)], teach.at[i], sems.at[i])
+
+    @pl.when(step == 0)
     def _():
+        for i in range(blocks):
+            fetch(i).start()
         tok_out[...] = tok_in[...]
 
+    columns = pl.ds(pl.multiple_of(step * block, LANES), block)
     token_part = tok_out[...]
     lse_col = lse[:, :1]
     off_col = offset[:, :1]
@@ -249,7 +295,12 @@
         w_hi, w_lo = split(protos[i][...])
         logits = dot(u_parts[...], parts_of_right(w_hi, w_lo, 1), ((1,), (1,)))
         student = jnp.exp2(logits - lse_col)
-        target = jnp.exp2(teach[i][...].astype(F32) * TEACH - off_col) * cols[i][...]
+
+        @pl.when(step == 0)
+        def _():
+            fetch(i).wait()
+
+        target = jnp.exp2(teach[i, :, columns].astype(F32) * TEACH - off_col) * cols[i][...]
         g_hi, g_lo = split(student - target)
         part = dot(t_parts[...], parts_of_right(g_hi, g_lo, 0))
         if arrivals == 1:
@@ -262,7 +313,7 @@
     tok_out[...] = token_part
 
 
-def grad_step(own, slots, consts, tok, teacher, cols, protos, arrived, width, limit):
+def grad_step(own, slots, consts, tok, teacher, cols, protos, arrived, width):
     tokens, depth = tok.shape
     block = min(width, 512)
     count = width // block
@@ -285,26 +336,30 @@
         grid=(count,),
         in_specs=[whole(c.shape) for c in consts]
         + [whole(tok.shape)]
-        + [picked((tokens, block), slot) for slot in slots]
+        + [pl.BlockSpec(memory_space=pltpu.HBM)]
         + [picked((1, block), slot) for slot in slots]
         + [rows((block, depth), slot) for slot in slots]
         + [across((depth, block)) for x in arrived],
         out_specs=[across((depth, block)) for slot in slots] + [whole(tok.shape)],
+        scratch_shapes=[
+            pltpu.VMEM((blocks, tokens, width), teacher.dtype),
+            pltpu.SemaphoreType.DMA((blocks,)),
+        ],
     )
     *parts, tok = pl.pallas_call(
         lambda *refs: grad_kernel(
-            *refs, blocks=blocks, arrivals=len(arrived), parity=own.shape[0] - 1
+            *refs, slots=slots, arrivals=len(arrived), parity=own.shape[0] - 1
         ),
         grid_spec=grid,
         out_shape=[jax.ShapeDtypeStruct((depth, width), F32) for slot in slots]
         + [jax.ShapeDtypeStruct(tok.shape, F32)],
-        compiler_params=params(limit),
+        compiler_params=params(),
         name="grad_blocks",
     )(
         own,
         *consts,
         tok,
-        *([teacher] * blocks),
+        in_hbm(teacher),
         *([cols] * blocks),
         *([protos] * blocks),
         *arrived,
@@ -488,14 +543,14 @@
     token_part = jnp.zeros(unit_tok.shape, F32)
     consts = (u_parts, t_parts, lse, offset)
 
-    def blocks_of(slots, arrived, limit=VMEM_LIMIT):
+    def blocks_of(slots, arrived):
         return grad_step(
-            own, slots, consts, token_part, teacher_logits, cols, gathered, arrived, width, limit
+            own, slots, consts, token_part, teacher_logits, cols, gathered, arrived, width
         )
 
     crossed = [None, None]
     for sub in range(2):
-        (part,), token_part = blocks_of((slot(half, sub),), [], STREAM_LIMIT)
+        (part,), token_part = blocks_of((slot(half, sub),), [])
         crossed[sub] = swap(part, "dp", dp_count, 1)
     waiting = [[crossed[0]], [crossed[1]]]
     mine = []
@@ -507,7 +562,6 @@
             (first, second), token_part = blocks_of(
                 (slot(far, sub), slot(-far, sub)),
                 waiting[sub],
-                STREAM_LIMIT if far == half - 1 else VMEM_LIMIT,
             )
             waiting[sub] = [
                 lax.ppermute(first, "dp", ahead),

time: 433 us -> 425 us (0.982)
  Pallas kernels: 216 us -> 204 us
  local copies, waits for them, and re-layouts: 23.2 us -> 11.9 us
  waiting for transfers between devices: 103 us -> 114 us
    all_gather x1, waiting for transfers between devices: 0.02 us -> 18.5 us  [body(): gathered = lax.all_gather(weights, 'dp', axis=0, tiled=True)]
    pallas_call x3, Pallas kernels: 38.3 us -> 21.5 us  [row_pass(): pl.pallas_call(lambda *refs: row_kernel(*refs, unroll=min(16, block // LA...]
    pallas_call x18, Pallas kernels: 100 us -> 116 us  [grad_step(): pl.pallas_call(lambda *refs: grad_kernel(*refs, slots=slots, arrivals=len...]
    pallas_call x3, Pallas kernels: 38.8 us -> 24 us  [column_pass(): pl.pallas_call(lambda *refs: column_kernel(*refs, unroll=min(16, shard //...]
    unnamed x91 -> x35, local copies, waits for them, and re-layouts: 16 us -> 4.69 us
    ppermute x14, starting transfers between devices: 2.94 us -> 10.7 us  [body(): lax.ppermute(first, 'dp', ahead)]
    pallas_call x1, Pallas kernels: 18.9 us -> 23.5 us  [student_pass(): pl.pallas_call(student_kernel, grid=(rows // block,), in_specs=[pl.BlockS...]
    ppermute x14, waiting for transfers between devices: 16 us -> 11.6 us  [body(): lax.ppermute(first, 'dp', ahead)]
  transfers between devices with their start and end apart: 42 -> 42, of which waited for: 33 -> 34; matrix products, arithmetic and copies ran while one was open for 2% -> 3% of each run, Pallas kernels for 45% -> 41%
where the time goes in v3:
time: 425 us; the launch traced here: 418 us
  Pallas kernels  204 us (48%)
  waiting for transfers between devices  114 us (27%)
  starting transfers between devices  50.8 us (12%)
  blocking collectives  16.8 us (4%)
  between operations  15 us (4%)
  local copies, waits for them, and re-layouts  11.9 us (3%)
  other arithmetic  5.33 us (1%)
    pallas_call x18, Pallas kernels, grad_step(): pl.pallas_call(lambda *refs: grad_kernel(*refs, slots=slots, arrivals=len...  116 us
    ppermute x14, waiting for transfers between devices, body(): lax.ppermute(second, 'dp', behind)  29.8 us
    all_to_all x3, waiting for transfers between devices, column_total(): lax.all_to_all(jnp.broadcast_to(mine, x.shape), 'dp', 0, 0, tiled=True)  26.5 us
    pallas_call x3, Pallas kernels, column_pass(): pl.pallas_call(lambda *refs: column_kernel(*refs, unroll=min(16, shard //...  24 us
    pallas_call x1, Pallas kernels, student_pass(): pl.pallas_call(student_kernel, grid=(rows // block,), in_specs=[pl.BlockS...  23.5 us
    pallas_call x3, Pallas kernels, row_pass(): pl.pallas_call(lambda *refs: row_kernel(*refs, unroll=min(16, block // LA...  21.5 us
    all_gather x1, waiting for transfers between devices, body(): gathered = lax.all_gather(weights, 'dp', axis=0, tiled=True)  18.5 us
    all_to_all x2, waiting for transfers between devices, column_total(): lax.all_to_all(x, 'dp', 0, 0, tiled=True)  17.1 us
  transfers between devices with their start and end apart: 42, of which 34 were waited for; matrix products, arithmetic and copies ran while one was open for 3% of the time, Pallas kernels for 41%

profile of v3, /device:TPU:1, one launch (start us, length us, event | category | flops | bytes accessed | tf_op | source)
XLA Modules:
  0.0 417.9 jit_solution(2425381291411045422)
XLA Ops:
  7.2 2.1 multiply_reduce_fusion
  9.5 1.7 divide_multiply_fusion
  11.2 13.0 %teacher_stats.1 = (f32[192,128]{1,0:T(8,128)S(1)}, f32[192,128]{1,0:T(8,128)S(1)}) custom-call(bf16[192,32768]{1,0:T(8,128)(2,1)} %refs_6_.35), custom_call_target="tpu_custom_call" | custom-call | tf_op jit(solution)/shard_map/teacher_stats/pallas_call | solution.py:97
  24.4 2.1 collective-permute-start.1
  28.4 6.4 %column_sums.3 = (f32[16,1,2048]{2,1,0:T(1,128)S(1)}, f32[192,128]{1,0:T(8,128)S(1)}) custom-call(bf16[192,32768]{1,0:T(8,128)(2,1)} %refs_6_.35, f32[192,128]{1,0:T(8,128)S(1)} %broadcast_in_dim.98.refs_1_, f32[192,128]{1,0:T(8,128)S(1)} %iota.17.refs_2_, f32[192,128]{1,0:T(8,128)S(1)} %broadcast_in_dim.101.refs_3_), custom_call_target="tpu_custom_call" | custom-call | tf_op jit(solution)/shard_map/column_sums/pallas_call | solution.py:142
  34.9 16.8 %all_to_all.30 = f32[16,1,2048]{2,1,0:T(1,128)S(1)} all-to-all(f32[16,1,2048]{2,1,0:T(1,128)S(1)} %get-tuple-element.76), channel_id=1, replica_groups=mesh['dp'=16,'proto'=2] {'dp'}, dimensions={0} | all-to-all | bytes 262144 | tf_op jit(solution)/shard_map/all_to_all | solution.py:443
  52.5 4.5 %all-to-all-start.1 = ((f32[16,1,2048]{2,1,0:T(1,128)}), f32[16,1,2048]{2,1,0:T(1,128)S(1)}, u32[]{:S(2)}, u32[]{:S(2)}) async-start(f32[16,1,2048]{2,1,0:T(1,128)} %broadcast_in_dim.102), calls=%async_computation.1 | async-start | bytes 262144 | tf_op jit(solution)/shard_map/all_to_all | solution.py:444
  57.0 9.3 %all-to-all-done.1.refs_2_ = f32[16,1,2048]{2,1,0:T(1,128)S(1)} async-done(((f32[16,1,2048]{2,1,0:T(1,128)}), f32[16,1,2048]{2,1,0:T(1,128)S(1)}, u32[]{:S(2)}, u32[]{:S(2)}) %all-to-all-start.1) | async-done | bytes 131104 | tf_op jit(solution)/shard_map/all_to_all | solution.py:444
  66.4 7.3 %row_sums.3 = (f32[192,128]{1,0:T(8,128)S(1)}, f32[1,32768]{1,0:T(1,128)}) custom-call(bf16[192,32768]{1,0:T(8,128)(2,1)} %refs_6_.35, f32[192,128]{1,0:T(8,128)S(1)} %get-tuple-element.75.refs_1_, f32[16,1,2048]{2,1,0:T(1,128)S(1)} %all-to-all-done.1.refs_2_), custom_call_target="tpu_custom_call" | custom-call | tf_op jit(solution)/shard_map/row_sums/pallas_call | solution.py:190
  75.1 2.5 collective-permute-done.2.refs_3_
  77.6 8.8 %column_sums.4 = (f32[16,1,2048]{2,1,0:T(1,128)}, f32[192,128]{1,0:T(8,128)S(1)}) custom-call(bf16[192,32768]{1,0:T(8,128)(2,1)} %refs_6_.35, f32[192,128]{1,0:T(8,128)S(1)} %get-tuple-element.75.refs_1_, f32[192,128]{1,0:T(8,128)S(1)} %get-tuple-element.77.refs_2_, f32[192,128]{1,0:T(8,128)S(1)} %collective-permute-done.2.refs_3_), custom_call_target="tpu_custom_call" | custom-call | tf_op jit(solution)/shard_map/column_sums/pallas_call | solution.py:142
  86.4 5.3 %all-to-all-start.2 = ((f32[16,1,2048]{2,1,0:T(1,128)}), f32[16,1,2048]{2,1,0:T(1,128)S(1)}, u32[]{:S(2)}, u32[]{:S(2)}) async-start(f32[16,1,2048]{2,1,0:T(1,128)} %get-tuple-element.79), calls=%async_computation.2 | async-start | bytes 262144 | tf_op jit(solution)/shard_map/all_to_all | solution.py:443
  93.1 7.9 %all-to-all-done.2 = f32[16,1,2048]{2,1,0:T(1,128)S(1)} async-done(((f32[16,1,2048]{2,1,0:T(1,128)}), f32[16,1,2048]{2,1,0:T(1,128)S(1)}, u32[]{:S(2)}, u32[]{:S(2)}) %all-to-all-start.2) | async-done | bytes 131104 | tf_op jit(solution)/shard_map/all_to_all | solution.py:443
  101.8 4.5 %all-to-all-start.3 = ((f32[16,1,2048]{2,1,0:T(1,128)}), f32[16,1,2048]{2,1,0:T(1,128)S(1)}, u32[]{:S(2)}, u32[]{:S(2)}) async-start(f32[16,1,2048]{2,1,0:T(1,128)} %broadcast_in_dim.103), calls=%async_computation.3 | async-start | bytes 262144 | tf_op jit(solution)/shard_map/all_to_all | solution.py:444
  106.5 9.1 %all-to-all-done.3.refs_2_ = f32[16,1,2048]{2,1,0:T(1,128)S(1)} async-done(((f32[16,1,2048]{2,1,0:T(1,128)}), f32[16,1,2048]{2,1,0:T(1,128)S(1)}, u32[]{:S(2)}, u32[]{:S(2)}) %all-to-all-start.3) | async-done | bytes 131104 | tf_op jit(solution)/shard_map/all_to_all | solution.py:444
  115.7 7.3 %row_sums.4 = (f32[192,128]{1,0:T(8,128)S(1)}, f32[1,32768]{1,0:T(1,128)}) custom-call(bf16[192,32768]{1,0:T(8,128)(2,1)} %refs_6_.35, f32[192,128]{1,0:T(8,128)S(1)} %get-tuple-element.78.refs_1_, f32[16,1,2048]{2,1,0:T(1,128)S(1)} %all-to-all-done.3.refs_2_), custom_call_target="tpu_custom_call" | custom-call | tf_op jit(solution)/shard_map/row_sums/pallas_call | solution.py:190
  124.3 2.5 collective-permute-done.3.refs_3_
  126.9 8.8 %column_sums.5 = (f32[16,1,2048]{2,1,0:T(1,128)}, f32[192,128]{1,0:T(8,128)S(1)}) custom-call(bf16[192,32768]{1,0:T(8,128)(2,1)} %refs_6_.35, f32[192,128]{1,0:T(8,128)S(1)} %get-tuple-element.78.refs_1_, f32[192,128]{1,0:T(8,128)S(1)} %get-tuple-element.80.refs_2_, f32[192,128]{1,0:T(8,128)S(1)} %collective-permute-done.3.refs_3_), custom_call_target="tpu_custom_call" | custom-call | tf_op jit(solution)/shard_map/column_sums/pallas_call | solution.py:142
  135.6 5.3 %all-to-all-start.4 = ((f32[16,1,2048]{2,1,0:T(1,128)}), f32[16,1,2048]{2,1,0:T(1,128)S(1)}, u32[]{:S(2)}, u32[]{:S(2)}) async-start(f32[16,1,2048]{2,1,0:T(1,128)} %get-tuple-element.82), calls=%async_computation.4 | async-start | bytes 262144 | tf_op jit(solution)/shard_map/all_to_all | solution.py:443
  141.0 9.3 %all-to-all-done.4 = f32[16,1,2048]{2,1,0:T(1,128)S(1)} async-done(((f32[16,1,2048]{2,1,0:T(1,128)}), f32[16,1,2048]{2,1,0:T(1,128)S(1)}, u32[]{:S(2)}, u32[]{:S(2)}) %all-to-all-start.4) | async-done | bytes 131104 | tf_op jit(solution)/shard_map/all_to_all | solution.py:443
  151.1 4.8 %all-to-all-start.5 = ((f32[16,1,2048]{2,1,0:T(1,128)}), f32[16,1,2048]{2,1,0:T(1,128)S(1)}, u32[]{:S(2)}, u32[]{:S(2)}) async-start(f32[16,1,2048]{2,1,0:T(1,128)} %broadcast_in_dim.104), calls=%async_computation.5 | async-start | bytes 262144 | tf_op jit(solution)/shard_map/all_to_all | solution.py:444
  157.0 8.1 %all-to-all-done.5.refs_2_ = f32[16,1,2048]{2,1,0:T(1,128)S(1)} async-done(((f32[16,1,2048]{2,1,0:T(1,128)}), f32[16,1,2048]{2,1,0:T(1,128)S(1)}, u32[]{:S(2)}, u32[]{:S(2)}) %all-to-all-start.5) | async-done | bytes 131104 | tf_op jit(solution)/shard_map/all_to_all | solution.py:444
  165.1 6.9 %row_sums.5 = (f32[192,128]{1,0:T(8,128)S(1)}, f32[1,32768]{1,0:T(1,128)S(1)}) custom-call(bf16[192,32768]{1,0:T(8,128)(2,1)} %refs_6_.35, f32[192,128]{1,0:T(8,128)S(1)} %get-tuple-element.81.refs_1_, f32[16,1,2048]{2,1,0:T(1,128)S(1)} %all-to-all-done.5.refs_2_), custom_call_target="tpu_custom_call" | custom-call | tf_op jit(solution)/shard_map/row_sums/pallas_call | solution.py:190
  173.6 2.4 collective-permute-done.4
  176.1 18.5 %all-gather.2.cloned.1.call-done.w_ref.refs_8_.refs_9_.refs_10_ = f32[32768,256]{1,0:T(8,128)} async-done(((f32[2048,256]{1,0:T(8,128)}), f32[32768,256]{1,0:T(8,128)}) %all-gather.2.cloned.1.call-update) | async-done | bytes 33554448 | tf_op jit(solution)/shard_map/all_gather | solution.py:505
  194.6 23.5 %student_stats.1 = (f32[8,192]{1,0:T(8,128)S(1)}, f32[8,192]{1,0:T(8,128)S(1)}) custom-call(bf16[768,192]{1,0:T(8,128)(2,1)S(1)} %copy.80.u_ref, f32[32768,256]{1,0:T(8,128)} %all-gather.2.cloned.1.call-done.w_ref.refs_8_.refs_9_.refs_10_), custom_call_target="tpu_custom_call" | custom-call | tf_op jit(solution)/shard_map/student_stats/pallas_call | solution.py:256
  220.8 4.9 %grad_blocks.18 = (f32[256,1024]{1,0:T(8,128)S(1)}, f32[192,256]{1,0:T(8,128)S(1)}) custom-call(s32[33]{0:T(128)S(1)} %dynamic-slice_bitcast_fusion.refs_0_, bf16[192,768]{1,0:T(8,128)(2,1)S(1)} %get-tuple-element.144.refs_1_, bf16[256,576]{1,0:T(8,128)(2,1)S(1)} %copy.102.refs_2_, f32[192,128]{1,0:T(8,128)S(1)} %broadcast_in_dim.96.refs_3_, ...), custom_call_target="tpu_custom_call" | custom-call | tf_op jit(solution)/shard_map/grad_blocks/pallas_call | solution.py:349
  225.7 1.5 collective-permute-start.5
  227.1 4.9 %grad_blocks.19 = (f32[256,1024]{1,0:T(8,128)S(1)}, f32[192,256]{1,0:T(8,128)S(1)}) custom-call(s32[33]{0:T(128)S(1)} %dynamic-slice_bitcast_fusion.refs_0_, bf16[192,768]{1,0:T(8,128)(2,1)S(1)} %get-tuple-element.144.refs_1_, bf16[256,576]{1,0:T(8,128)(2,1)S(1)} %copy.102.refs_2_, f32[192,128]{1,0:T(8,128)S(1)} %broadcast_in_dim.96.refs_3_, ...), custom_call_target="tpu_custom_call" | custom-call | tf_op jit(solution)/shard_map/grad_blocks/pallas_call | solution.py:349
  232.1 6.9 %grad_blocks.20 = (f32[256,1024]{1,0:T(8,128)S(1)}, f32[256,1024]{1,0:T(8,128)S(1)}, f32[192,256]{1,0:T(8,128)S(1)}) custom-call(s32[33]{0:T(128)S(1)} %dynamic-slice_bitcast_fusion.refs_0_, bf16[192,768]{1,0:T(8,128)(2,1)S(1)} %get-tuple-element.144.refs_1_, bf16[256,576]{1,0:T(8,128)(2,1)S(1)} %copy.102.refs_2_, f32[192,128]{1,0:T(8,128)S(1)} %broadcast_in_dim.96.refs_3_, ...), custom_call_target="tpu_custom_call" | custom-call | tf_op jit(solution)/shard_map/grad_blocks/pallas_call | solution.py:349
  239.0 5.9 %collective-permute-start.7 = (f32[256,1024]{1,0:T(8,128)S(1)}, f32[256,1024]{1,0:T(8,128)S(1)}, u32[]{:S(2)}, u32[]{:S(2)}) collective-permute-start(f32[256,1024]{1,0:T(8,128)S(1)} %get-tuple-element.91), channel_id=1, source_target_pairs={{0,2},{2,8},{4,6},{6,0},{8,10},{10,16},{12,14},{14,4},{16,18},{18,... | collective-permute-start | bytes 3145736 | tf_op jit(solution)/shard_map/ppermute | solution.py:567
  244.8 6.9 %grad_blocks.21 = (f32[256,1024]{1,0:T(8,128)S(1)}, f32[256,1024]{1,0:T(8,128)S(1)}, f32[192,256]{1,0:T(8,128)S(1)}) custom-call(s32[33]{0:T(128)S(1)} %dynamic-slice_bitcast_fusion.refs_0_, bf16[192,768]{1,0:T(8,128)(2,1)S(1)} %get-tuple-element.144.refs_1_, bf16[256,576]{1,0:T(8,128)(2,1)S(1)} %copy.102.refs_2_, f32[192,128]{1,0:T(8,128)S(1)} %broadcast_in_dim.96.refs_3_, ...), custom_call_target="tpu_custom_call" | custom-call | tf_op jit(solution)/shard_map/grad_blocks/pallas_call | solution.py:349
  251.7 1.8 collective-permute-start.9
  253.5 3.1 collective-permute-done.7.refs_11_
  256.6 2.8 collective-permute-done.8.refs_12_
  259.3 6.9 %grad_blocks.22 = (f32[256,1024]{1,0:T(8,128)S(1)}, f32[256,1024]{1,0:T(8,128)S(1)}, f32[192,256]{1,0:T(8,128)S(1)}) custom-call(s32[33]{0:T(128)S(1)} %dynamic-slice_bitcast_fusion.refs_0_, bf16[192,768]{1,0:T(8,128)(2,1)S(1)} %get-tuple-element.144.refs_1_, bf16[256,576]{1,0:T(8,128)(2,1)S(1)} %copy.102.refs_2_, f32[192,128]{1,0:T(8,128)S(1)} %broadcast_in_dim.96.refs_3_, ...), custom_call_target="tpu_custom_call" | custom-call | tf_op jit(solution)/shard_map/grad_blocks/pallas_call | solution.py:349
  267.8 2.8 collective-permute-done.10.refs_12_
  270.6 6.9 %grad_blocks.23 = (f32[256,1024]{1,0:T(8,128)S(1)}, f32[256,1024]{1,0:T(8,128)S(1)}, f32[192,256]{1,0:T(8,128)S(1)}) custom-call(s32[33]{0:T(128)S(1)} %dynamic-slice_bitcast_fusion.refs_0_, bf16[192,768]{1,0:T(8,128)(2,1)S(1)} %get-tuple-element.144.refs_1_, bf16[256,576]{1,0:T(8,128)(2,1)S(1)} %copy.102.refs_2_, f32[192,128]{1,0:T(8,128)S(1)} %broadcast_in_dim.96.refs_3_, ...), custom_call_target="tpu_custom_call" | custom-call | tf_op jit(solution)/shard_map/grad_blocks/pallas_call | solution.py:349
  278.0 4.9 %grad_blocks.24 = (f32[256,1024]{1,0:T(8,128)S(1)}, f32[192,256]{1,0:T(8,128)S(1)}) custom-call(s32[33]{0:T(128)S(1)} %dynamic-slice_bitcast_fusion.refs_0_, bf16[192,768]{1,0:T(8,128)(2,1)S(1)} %get-tuple-element.144.refs_1_, bf16[256,576]{1,0:T(8,128)(2,1)S(1)} %copy.102.refs_2_, f32[192,128]{1,0:T(8,128)S(1)} %broadcast_in_dim.96.refs_3_, ...), custom_call_target="tpu_custom_call" | custom-call | tf_op jit(solution)/shard_map/grad_blocks/pallas_call | solution.py:349
  282.9 6.9 %grad_blocks.25 = (f32[256,1024]{1,0:T(8,128)S(1)}, f32[256,1024]{1,0:T(8,128)S(1)}, f32[192,256]{1,0:T(8,128)S(1)}) custom-call(s32[33]{0:T(128)S(1)} %dynamic-slice_bitcast_fusion.refs_0_, bf16[192,768]{1,0:T(8,128)(2,1)S(1)} %get-tuple-element.144.refs_1_, bf16[256,576]{1,0:T(8,128)(2,1)S(1)} %copy.102.refs_2_, f32[192,128]{1,0:T(8,128)S(1)} %broadcast_in_dim.96.refs_3_, ...), custom_call_target="tpu_custom_call" | custom-call | tf_op jit(solution)/shard_map/grad_blocks/pallas_call | solution.py:349
  291.1 1.9 collective-permute-done.14.refs_12_
  293.0 6.9 %grad_blocks.26 = (f32[256,1024]{1,0:T(8,128)S(1)}, f32[256,1024]{1,0:T(8,128)S(1)}, f32[192,256]{1,0:T(8,128)S(1)}) custom-call(s32[33]{0:T(128)S(1)} %dynamic-slice_bitcast_fusion.refs_0_, bf16[192,768]{1,0:T(8,128)(2,1)S(1)} %get-tuple-element.144.refs_1_, bf16[256,576]{1,0:T(8,128)(2,1)S(1)} %copy.102.refs_2_, f32[192,128]{1,0:T(8,128)S(1)} %broadcast_in_dim.96.refs_3_, ...), custom_call_target="tpu_custom_call" | custom-call | tf_op jit(solution)/shard_map/grad_blocks/pallas_call | solution.py:349
  300.5 4.9 %grad_blocks.27 = (f32[256,1024]{1,0:T(8,128)S(1)}, f32[192,256]{1,0:T(8,128)S(1)}) custom-call(s32[33]{0:T(128)S(1)} %dynamic-slice_bitcast_fusion.refs_0_, bf16[192,768]{1,0:T(8,128)(2,1)S(1)} %get-tuple-element.144.refs_1_, bf16[256,576]{1,0:T(8,128)(2,1)S(1)} %copy.102.refs_2_, f32[192,128]{1,0:T(8,128)S(1)} %broadcast_in_dim.96.refs_3_, ...), custom_call_target="tpu_custom_call" | custom-call | tf_op jit(solution)/shard_map/grad_blocks/pallas_call | solution.py:349
  305.6 6.8 %grad_blocks.28 = (f32[256,1024]{1,0:T(8,128)S(1)}, f32[256,1024]{1,0:T(8,128)S(1)}, f32[192,256]{1,0:T(8,128)S(1)}) custom-call(s32[33]{0:T(128)S(1)} %dynamic-slice_bitcast_fusion.refs_0_, bf16[192,768]{1,0:T(8,128)(2,1)S(1)} %get-tuple-element.144.refs_1_, bf16[256,576]{1,0:T(8,128)(2,1)S(1)} %copy.102.refs_2_, f32[192,128]{1,0:T(8,128)S(1)} %broadcast_in_dim.96.refs_3_, ...), custom_call_target="tpu_custom_call" | custom-call | tf_op jit(solution)/shard_map/grad_blocks/pallas_call | solution.py:349
  314.1 2.8 collective-permute-done.18.refs_12_
  316.9 6.9 %grad_blocks.29 = (f32[256,1024]{1,0:T(8,128)S(1)}, f32[256,1024]{1,0:T(8,128)S(1)}, f32[192,256]{1,0:T(8,128)S(1)}) custom-call(s32[33]{0:T(128)S(1)} %dynamic-slice_bitcast_fusion.refs_0_, bf16[192,768]{1,0:T(8,128)(2,1)S(1)} %get-tuple-element.144.refs_1_, bf16[256,576]{1,0:T(8,128)(2,1)S(1)} %copy.102.refs_2_, f32[192,128]{1,0:T(8,128)S(1)} %broadcast_in_dim.96.refs_3_, ...), custom_call_target="tpu_custom_call" | custom-call | tf_op jit(solution)/shard_map/grad_blocks/pallas_call | solution.py:349
  325.3 2.8 collective-permute-done.20.refs_12_
  328.1 6.9 %grad_blocks.30 = (f32[256,1024]{1,0:T(8,128)S(1)}, f32[256,1024]{1,0:T(8,128)S(1)}, f32[192,256]{1,0:T(8,128)S(1)}) custom-call(s32[33]{0:T(128)S(1)} %dynamic-slice_bitcast_fusion.refs_0_, bf16[192,768]{1,0:T(8,128)(2,1)S(1)} %get-tuple-element.144.refs_1_, bf16[256,576]{1,0:T(8,128)(2,1)S(1)} %copy.102.refs_2_, f32[192,128]{1,0:T(8,128)S(1)} %broadcast_in_dim.96.refs_3_, ...), custom_call_target="tpu_custom_call" | custom-call | tf_op jit(solution)/shard_map/grad_blocks/pallas_call | solution.py:349
  336.6 2.8 collective-permute-done.22.refs_12_
  339.4 6.9 %grad_blocks.31 = (f32[256,1024]{1,0:T(8,128)S(1)}, f32[256,1024]{1,0:T(8,128)S(1)}, f32[192,256]{1,0:T(8,128)S(1)}) custom-call(s32[33]{0:T(128)S(1)} %dynamic-slice_bitcast_fusion.refs_0_, bf16[192,768]{1,0:T(8,128)(2,1)S(1)} %get-tuple-element.144.refs_1_, bf16[256,576]{1,0:T(8,128)(2,1)S(1)} %copy.102.refs_2_, f32[192,128]{1,0:T(8,128)S(1)} %broadcast_in_dim.96.refs_3_, ...), custom_call_target="tpu_custom_call" | custom-call | tf_op jit(solution)/shard_map/grad_blocks/pallas_call | solution.py:349
  347.8 2.8 collective-permute-done.24.refs_12_
  350.6 6.9 %grad_blocks.32 = (f32[256,1024]{1,0:T(8,128)S(1)}, f32[256,1024]{1,0:T(8,128)S(1)}, f32[192,256]{1,0:T(8,128)S(1)}) custom-call(s32[33]{0:T(128)S(1)} %dynamic-slice_bitcast_fusion.refs_0_, bf16[192,768]{1,0:T(8,128)(2,1)S(1)} %get-tuple-element.144.refs_1_, bf16[256,576]{1,0:T(8,128)(2,1)S(1)} %copy.102.refs_2_, f32[192,128]{1,0:T(8,128)S(1)} %broadcast_in_dim.96.refs_3_, ...), custom_call_target="tpu_custom_call" | custom-call | tf_op jit(solution)/shard_map/grad_blocks/pallas_call | solution.py:349
  359.0 2.8 collective-permute-done.26.refs_12_
  361.8 6.9 %grad_blocks.33 = (f32[256,1024]{1,0:T(8,128)S(1)}, f32[256,1024]{1,0:T(8,128)S(1)}, f32[192,256]{1,0:T(8,128)S(1)}) custom-call(s32[33]{0:T(128)S(1)} %dynamic-slice_bitcast_fusion.refs_0_, bf16[192,768]{1,0:T(8,128)(2,1)S(1)} %get-tuple-element.144.refs_1_, bf16[256,576]{1,0:T(8,128)(2,1)S(1)} %copy.102.refs_2_, f32[192,128]{1,0:T(8,128)S(1)} %broadcast_in_dim.96.refs_3_, ...), custom_call_target="tpu_custom_call" | custom-call | tf_op jit(solution)/shard_map/grad_blocks/pallas_call | solution.py:349
  370.3 2.8 collective-permute-done.28.refs_12_
  373.1 7.3 %grad_blocks.34 = (f32[256,1024]{1,0:T(8,128)}, f32[256,1024]{1,0:T(8,128)}, f32[192,256]{1,0:T(8,128)S(1)}) custom-call(s32[33]{0:T(128)S(1)} %dynamic-slice_bitcast_fusion.refs_0_, bf16[192,768]{1,0:T(8,128)(2,1)S(1)} %get-tuple-element.144.refs_1_, bf16[256,576]{1,0:T(8,128)(2,1)S(1)} %copy.102.refs_2_, f32[192,128]{1,0:T(8,128)S(1)} %broadcast_in_dim.96.refs_3_, ...), custom_call_target="tpu_custom_call" | custom-call | tf_op jit(solution)/shard_map/grad_blocks/pallas_call | solution.py:349
  381.5 2.9 collective-permute-done.30.refs_12_
  384.4 7.3 %grad_blocks.35 = (f32[256,1024]{1,0:T(8,128)}, f32[256,1024]{1,0:T(8,128)}, f32[192,256]{1,0:T(8,128)S(1)}) custom-call(s32[33]{0:T(128)S(1)} %dynamic-slice_bitcast_fusion.refs_0_, bf16[192,768]{1,0:T(8,128)(2,1)S(1)} %get-tuple-element.144.refs_1_, bf16[256,576]{1,0:T(8,128)(2,1)S(1)} %copy.102.refs_2_, f32[192,128]{1,0:T(8,128)S(1)} %broadcast_in_dim.96.refs_3_, ...), custom_call_target="tpu_custom_call" | custom-call | tf_op jit(solution)/shard_map/grad_blocks/pallas_call | solution.py:349
  393.7 1.9 copy.103
  395.7 3.0 proto_grads.2
  400.0 2.3 scatter_custom_fusion
  402.3 1.8 collective-permute-done.34.b
  404.1 2.5 collective-permute-done.35.c
  407.9 2.9 proto_grads.3
  (136 shorter events, 34.4 us)
Async XLA Ops:
  7.2 85.1 %copy-start = (f32[1024,256]{1,0:T(8,128)S(1)}, f32[1024,256]{1,0:T(8,128)}, u32[]{:S(2)}) copy-start(f32[1024,256]{1,0:T(8,128)} %param.7) | copy-start | bytes 3145732
  7.2 2.3 copy-start.11
  7.2 2.2 copy-start.8
  7.2 187.4 %all-gather.2.cloned.1.call-start = ((), (), s32[]{:S(2)}) async-start(), calls=%async_computation.6 | async-start | bytes 35651584 | tf_op jit(solution)/shard_map/all_gather | solution.py:505
  24.4 3.5 collective-permute-start.1
  52.5 13.9 %all-to-all-start.1 = ((f32[16,1,2048]{2,1,0:T(1,128)}), f32[16,1,2048]{2,1,0:T(1,128)S(1)}, u32[]{:S(2)}, u32[]{:S(2)}) async-start(f32[16,1,2048]{2,1,0:T(1,128)} %broadcast_in_dim.102), calls=%async_computation.1 | async-start | bytes 262144 | tf_op jit(solution)/shard_map/all_to_all | solution.py:444
  66.4 8.6 %copy-start.16 = (s32[3]{0:T(128)S(1)}, s32[3]{0:T(128)}, u32[]{:S(2)}) copy-start(s32[3]{0:T(128)} %param.8) | copy-start | bytes 40
  73.7 3.9 collective-permute-start.2
  75.0 16.6 %copy-start.15 = (s32[192]{0:T(256)S(1)}, s32[192]{0:T(256)}, u32[]{:S(2)}) copy-start(s32[192]{0:T(256)} %param.9) | copy-start | bytes 2308
  86.4 14.6 %all-to-all-start.2 = ((f32[16,1,2048]{2,1,0:T(1,128)}), f32[16,1,2048]{2,1,0:T(1,128)S(1)}, u32[]{:S(2)}, u32[]{:S(2)}) async-start(f32[16,1,2048]{2,1,0:T(1,128)} %get-tuple-element.79), calls=%async_computation.2 | async-start | bytes 262144 | tf_op jit(solution)/shard_map/all_to_all | solution.py:443
  91.7 0.6 copy-start.14
  101.8 13.9 %all-to-all-start.3 = ((f32[16,1,2048]{2,1,0:T(1,128)}), f32[16,1,2048]{2,1,0:T(1,128)S(1)}, u32[]{:S(2)}, u32[]{:S(2)}) async-start(f32[16,1,2048]{2,1,0:T(1,128)} %broadcast_in_dim.103), calls=%async_computation.3 | async-start | bytes 262144 | tf_op jit(solution)/shard_map/all_to_all | solution.py:444
  106.5 17.7 %copy-start.12 = (f32[192]{0:T(256)}, f32[192]{0:T(256)S(1)}, u32[]{:S(2)}) copy-start(f32[192]{0:T(256)S(1)} %add_rsqrt_fusion) | copy-start | bytes 2308
  122.9 3.9 collective-permute-start.3
  124.3 16.6 %copy-start.2 = (f32[192,256]{1,0:T(8,128)}, f32[192,256]{1,0:T(8,128)S(1)}, u32[]{:S(2)}) copy-start(f32[192,256]{1,0:T(8,128)S(1)} %get-tuple-element.140.unit) | copy-start | bytes 589828
  135.6 14.6 %all-to-all-start.4 = ((f32[16,1,2048]{2,1,0:T(1,128)}), f32[16,1,2048]{2,1,0:T(1,128)S(1)}, u32[]{:S(2)}, u32[]{:S(2)}) async-start(f32[16,1,2048]{2,1,0:T(1,128)} %get-tuple-element.82), calls=%async_computation.4 | async-start | bytes 262144 | tf_op jit(solution)/shard_map/all_to_all | solution.py:443
  151.1 14.0 %all-to-all-start.5 = ((f32[16,1,2048]{2,1,0:T(1,128)}), f32[16,1,2048]{2,1,0:T(1,128)S(1)}, u32[]{:S(2)}, u32[]{:S(2)}) async-start(f32[16,1,2048]{2,1,0:T(1,128)} %broadcast_in_dim.104), calls=%async_computation.5 | async-start | bytes 262144 | tf_op jit(solution)/shard_map/all_to_all | solution.py:444
  172.0 3.9 collective-permute-start.4
  218.2 2.5 collective-permute-start
  225.7 6.4 %collective-permute-start.5 = (f32[256,1024]{1,0:T(8,128)S(1)}, f32[256,1024]{1,0:T(8,128)S(1)}, u32[]{:S(2)}, u32[]{:S(2)}) collective-permute-start(f32[256,1024]{1,0:T(8,128)S(1)} %get-tuple-element.87), channel_id=1, source_target_pairs={{0,2},{2,0},{4,6},{6,4},{8,10},{10,8},{12,14},{14,12},{16,18},{18,... | collective-permute-start | bytes 3145736 | tf_op jit(solution)/shard_map/ppermute | solution.py:432
  232.0 12.8 %collective-permute-start.6 = (f32[256,1024]{1,0:T(8,128)S(1)}, f32[256,1024]{1,0:T(8,128)S(1)}, u32[]{:S(2)}, u32[]{:S(2)}) collective-permute-start(f32[256,1024]{1,0:T(8,128)S(1)} %get-tuple-element.89), channel_id=1, source_target_pairs={{0,2},{2,0},{4,6},{6,4},{8,10},{10,8},{12,14},{14,12},{16,18},{18,... | collective-permute-start | bytes 3145736 | tf_op jit(solution)/shard_map/ppermute | solution.py:432
  239.0 17.6 %collective-permute-start.7 = (f32[256,1024]{1,0:T(8,128)S(1)}, f32[256,1024]{1,0:T(8,128)S(1)}, u32[]{:S(2)}, u32[]{:S(2)}) collective-permute-start(f32[256,1024]{1,0:T(8,128)S(1)} %get-tuple-element.91), channel_id=1, source_target_pairs={{0,2},{2,8},{4,6},{6,0},{8,10},{10,16},{12,14},{14,4},{16,18},{18,... | collective-permute-start | bytes 3145736 | tf_op jit(solution)/shard_map/ppermute | solution.py:567
  244.8 14.5 %collective-permute-start.8 = (f32[256,1024]{1,0:T(8,128)S(1)}, f32[256,1024]{1,0:T(8,128)S(1)}, u32[]{:S(2)}, u32[]{:S(2)}) collective-permute-start(f32[256,1024]{1,0:T(8,128)S(1)} %get-tuple-element.92), channel_id=1, source_target_pairs={{0,6},{2,0},{4,14},{6,4},{8,2},{10,8},{12,22},{14,12},{16,10},{18,... | collective-permute-start | bytes 3145736 | tf_op jit(solution)/shard_map/ppermute | solution.py:568
  251.7 16.1 %collective-permute-start.9 = (f32[256,1024]{1,0:T(8,128)S(1)}, f32[256,1024]{1,0:T(8,128)S(1)}, u32[]{:S(2)}, u32[]{:S(2)}) collective-permute-start(f32[256,1024]{1,0:T(8,128)S(1)} %get-tuple-element.94), channel_id=1, source_target_pairs={{0,2},{2,8},{4,6},{6,0},{8,10},{10,16},{12,14},{14,4},{16,18},{18,... | collective-permute-start | bytes 3145736 | tf_op jit(solution)/shard_map/ppermute | solution.py:567
  253.5 17.1 %collective-permute-start.10 = (f32[256,1024]{1,0:T(8,128)S(1)}, f32[256,1024]{1,0:T(8,128)S(1)}, u32[]{:S(2)}, u32[]{:S(2)}) collective-permute-start(f32[256,1024]{1,0:T(8,128)S(1)} %get-tuple-element.95), channel_id=1, source_target_pairs={{0,6},{2,0},{4,14},{6,4},{8,2},{10,8},{12,22},{14,12},{16,10},{18,... | collective-permute-start | bytes 3145736 | tf_op jit(solution)/shard_map/ppermute | solution.py:568
  266.2 16.7 %collective-permute-start.11 = (f32[256,1024]{1,0:T(8,128)S(1)}, f32[256,1024]{1,0:T(8,128)S(1)}, u32[]{:S(2)}, u32[]{:S(2)}) collective-permute-start(f32[256,1024]{1,0:T(8,128)S(1)} %get-tuple-element.98), channel_id=1, source_target_pairs={{0,2},{2,8},{4,6},{6,0},{8,10},{10,16},{12,14},{14,4},{16,18},{18,... | collective-permute-start | bytes 3145736 | tf_op jit(solution)/shard_map/ppermute | solution.py:567
  266.3 16.6 %collective-permute-start.12 = (f32[256,1024]{1,0:T(8,128)S(1)}, f32[256,1024]{1,0:T(8,128)S(1)}, u32[]{:S(2)}, u32[]{:S(2)}) collective-permute-start(f32[256,1024]{1,0:T(8,128)S(1)} %get-tuple-element.99), channel_id=1, source_target_pairs={{0,6},{2,0},{4,14},{6,4},{8,2},{10,8},{12,22},{14,12},{16,10},{18,... | collective-permute-start | bytes 3145736 | tf_op jit(solution)/shard_map/ppermute | solution.py:568
  277.4 13.7 %collective-permute-start.13 = (f32[256,1024]{1,0:T(8,128)S(1)}, f32[256,1024]{1,0:T(8,128)S(1)}, u32[]{:S(2)}, u32[]{:S(2)}) collective-permute-start(f32[256,1024]{1,0:T(8,128)S(1)} %get-tuple-element.101), channel_id=1, source_target_pairs={{0,2},{2,8},{4,6},{6,0},{8,10},{10,16},{12,14},{14,4},{16,18},{18,... | collective-permute-start | bytes 3145736 | tf_op jit(solution)/shard_map/ppermute | solution.py:567
  277.5 15.5 %collective-permute-start.14 = (f32[256,1024]{1,0:T(8,128)S(1)}, f32[256,1024]{1,0:T(8,128)S(1)}, u32[]{:S(2)}, u32[]{:S(2)}) collective-permute-start(f32[256,1024]{1,0:T(8,128)S(1)} %get-tuple-element.102), channel_id=1, source_target_pairs={{0,6},{2,0},{4,14},{6,4},{8,2},{10,8},{12,22},{14,12},{16,10},{18,... | collective-permute-start | bytes 3145736 | tf_op jit(solution)/shard_map/ppermute | solution.py:568
  282.9 6.9 %copy-start.4 = (f32[256,1024]{1,0:T(8,128)}, f32[256,1024]{1,0:T(8,128)S(1)}, u32[]{:S(2)}) copy-start(f32[256,1024]{1,0:T(8,128)S(1)} %get-tuple-element.129.a) | copy-start | bytes 3145732
  289.8 15.6 %collective-permute-start.15 = (f32[256,1024]{1,0:T(8,128)S(1)}, f32[256,1024]{1,0:T(8,128)S(1)}, u32[]{:S(2)}, u32[]{:S(2)}) collective-permute-start(f32[256,1024]{1,0:T(8,128)S(1)} %get-tuple-element.105), channel_id=1, source_target_pairs={{0,2},{2,8},{4,6},{6,0},{8,10},{10,16},{12,14},{14,4},{16,18},{18,... | collective-permute-start | bytes 3145736 | tf_op jit(solution)/shard_map/ppermute | solution.py:567
  291.1 14.5 %collective-permute-start.16 = (f32[256,1024]{1,0:T(8,128)S(1)}, f32[256,1024]{1,0:T(8,128)S(1)}, u32[]{:S(2)}, u32[]{:S(2)}) collective-permute-start(f32[256,1024]{1,0:T(8,128)S(1)} %get-tuple-element.106), channel_id=1, source_target_pairs={{0,6},{2,0},{4,14},{6,4},{8,2},{10,8},{12,22},{14,12},{16,10},{18,... | collective-permute-start | bytes 3145736 | tf_op jit(solution)/shard_map/ppermute | solution.py:568
  299.9 14.2 %collective-permute-start.17 = (f32[256,1024]{1,0:T(8,128)S(1)}, f32[256,1024]{1,0:T(8,128)S(1)}, u32[]{:S(2)}, u32[]{:S(2)}) collective-permute-start(f32[256,1024]{1,0:T(8,128)S(1)} %get-tuple-element.108), channel_id=1, source_target_pairs={{0,2},{2,8},{4,6},{6,0},{8,10},{10,16},{12,14},{14,4},{16,18},{18,... | collective-permute-start | bytes 3145736 | tf_op jit(solution)/shard_map/ppermute | solution.py:567
  300.0 16.9 %collective-permute-start.18 = (f32[256,1024]{1,0:T(8,128)S(1)}, f32[256,1024]{1,0:T(8,128)S(1)}, u32[]{:S(2)}, u32[]{:S(2)}) collective-permute-start(f32[256,1024]{1,0:T(8,128)S(1)} %get-tuple-element.109), channel_id=1, source_target_pairs={{0,6},{2,0},{4,14},{6,4},{8,2},{10,8},{12,22},{14,12},{16,10},{18,... | collective-permute-start | bytes 3145736 | tf_op jit(solution)/shard_map/ppermute | solution.py:568
  305.3 7.2 %copy-start.6 = (f32[256,1024]{1,0:T(8,128)}, f32[256,1024]{1,0:T(8,128)S(1)}, u32[]{:S(2)}) copy-start(f32[256,1024]{1,0:T(8,128)S(1)} %get-tuple-element.133.a) | copy-start | bytes 3145732
  312.5 12.8 %collective-permute-start.19 = (f32[256,1024]{1,0:T(8,128)S(1)}, f32[256,1024]{1,0:T(8,128)S(1)}, u32[]{:S(2)}, u32[]{:S(2)}) collective-permute-start(f32[256,1024]{1,0:T(8,128)S(1)} %get-tuple-element.111), channel_id=1, source_target_pairs={{0,2},{2,8},{4,6},{6,0},{8,10},{10,16},{12,14},{14,4},{16,18},{18,... | collective-permute-start | bytes 3145736 | tf_op jit(solution)/shard_map/ppermute | solution.py:567
  313.6 14.5 %collective-permute-start.20 = (f32[256,1024]{1,0:T(8,128)S(1)}, f32[256,1024]{1,0:T(8,128)S(1)}, u32[]{:S(2)}, u32[]{:S(2)}) collective-permute-start(f32[256,1024]{1,0:T(8,128)S(1)} %get-tuple-element.112), channel_id=1, source_target_pairs={{0,6},{2,0},{4,14},{6,4},{8,2},{10,8},{12,22},{14,12},{16,10},{18,... | collective-permute-start | bytes 3145736 | tf_op jit(solution)/shard_map/ppermute | solution.py:568
  323.7 12.8 %collective-permute-start.21 = (f32[256,1024]{1,0:T(8,128)S(1)}, f32[256,1024]{1,0:T(8,128)S(1)}, u32[]{:S(2)}, u32[]{:S(2)}) collective-permute-start(f32[256,1024]{1,0:T(8,128)S(1)} %get-tuple-element.114), channel_id=1, source_target_pairs={{0,2},{2,8},{4,6},{6,0},{8,10},{10,16},{12,14},{14,4},{16,18},{18,... | collective-permute-start | bytes 3145736 | tf_op jit(solution)/shard_map/ppermute | solution.py:567
  323.8 15.5 %collective-permute-start.22 = (f32[256,1024]{1,0:T(8,128)S(1)}, f32[256,1024]{1,0:T(8,128)S(1)}, u32[]{:S(2)}, u32[]{:S(2)}) collective-permute-start(f32[256,1024]{1,0:T(8,128)S(1)} %get-tuple-element.115), channel_id=1, source_target_pairs={{0,6},{2,0},{4,14},{6,4},{8,2},{10,8},{12,22},{14,12},{16,10},{18,... | collective-permute-start | bytes 3145736 | tf_op jit(solution)/shard_map/ppermute | solution.py:568
  335.0 12.8 %collective-permute-start.23 = (f32[256,1024]{1,0:T(8,128)S(1)}, f32[256,1024]{1,0:T(8,128)S(1)}, u32[]{:S(2)}, u32[]{:S(2)}) collective-permute-start(f32[256,1024]{1,0:T(8,128)S(1)} %get-tuple-element.117), channel_id=1, source_target_pairs={{0,2},{2,8},{4,6},{6,0},{8,10},{10,16},{12,14},{14,4},{16,18},{18,... | collective-permute-start | bytes 3145736 | tf_op jit(solution)/shard_map/ppermute | solution.py:567
  335.0 15.5 %collective-permute-start.24 = (f32[256,1024]{1,0:T(8,128)S(1)}, f32[256,1024]{1,0:T(8,128)S(1)}, u32[]{:S(2)}, u32[]{:S(2)}) collective-permute-start(f32[256,1024]{1,0:T(8,128)S(1)} %get-tuple-element.118), channel_id=1, source_target_pairs={{0,6},{2,0},{4,14},{6,4},{8,2},{10,8},{12,22},{14,12},{16,10},{18,... | collective-permute-start | bytes 3145736 | tf_op jit(solution)/shard_map/ppermute | solution.py:568
  346.2 12.8 %collective-permute-start.25 = (f32[256,1024]{1,0:T(8,128)S(1)}, f32[256,1024]{1,0:T(8,128)S(1)}, u32[]{:S(2)}, u32[]{:S(2)}) collective-permute-start(f32[256,1024]{1,0:T(8,128)S(1)} %get-tuple-element.120), channel_id=1, source_target_pairs={{0,2},{2,8},{4,6},{6,0},{8,10},{10,16},{12,14},{14,4},{16,18},{18,... | collective-permute-start | bytes 3145736 | tf_op jit(solution)/shard_map/ppermute | solution.py:567
  346.3 15.5 %collective-permute-start.26 = (f32[256,1024]{1,0:T(8,128)S(1)}, f32[256,1024]{1,0:T(8,128)S(1)}, u32[]{:S(2)}, u32[]{:S(2)}) collective-permute-start(f32[256,1024]{1,0:T(8,128)S(1)} %get-tuple-element.121), channel_id=1, source_target_pairs={{0,6},{2,0},{4,14},{6,4},{8,2},{10,8},{12,22},{14,12},{16,10},{18,... | collective-permute-start | bytes 3145736 | tf_op jit(solution)/shard_map/ppermute | solution.py:568
  357.5 12.8 %collective-permute-start.27 = (f32[256,1024]{1,0:T(8,128)S(1)}, f32[256,1024]{1,0:T(8,128)S(1)}, u32[]{:S(2)}, u32[]{:S(2)}) collective-permute-start(f32[256,1024]{1,0:T(8,128)S(1)} %get-tuple-element.123), channel_id=1, source_target_pairs={{0,2},{2,8},{4,6},{6,0},{8,10},{10,16},{12,14},{14,4},{16,18},{18,... | collective-permute-start | bytes 3145736 | tf_op jit(solution)/shard_map/ppermute | solution.py:567
  357.5 15.5 %collective-permute-start.28 = (f32[256,1024]{1,0:T(8,128)S(1)}, f32[256,1024]{1,0:T(8,128)S(1)}, u32[]{:S(2)}, u32[]{:S(2)}) collective-permute-start(f32[256,1024]{1,0:T(8,128)S(1)} %get-tuple-element.124), channel_id=1, source_target_pairs={{0,6},{2,0},{4,14},{6,4},{8,2},{10,8},{12,22},{14,12},{16,10},{18,... | collective-permute-start | bytes 3145736 | tf_op jit(solution)/shard_map/ppermute | solution.py:568
  368.7 12.8 %collective-permute-start.29 = (f32[256,1024]{1,0:T(8,128)S(1)}, f32[256,1024]{1,0:T(8,128)S(1)}, u32[]{:S(2)}, u32[]{:S(2)}) collective-permute-start(f32[256,1024]{1,0:T(8,128)S(1)} %get-tuple-element.126), channel_id=1, source_target_pairs={{0,2},{2,8},{4,6},{6,0},{8,10},{10,16},{12,14},{14,4},{16,18},{18,... | collective-permute-start | bytes 3145736 | tf_op jit(solution)/shard_map/ppermute | solution.py:567
  368.8 15.6 %collective-permute-start.30 = (f32[256,1024]{1,0:T(8,128)S(1)}, f32[256,1024]{1,0:T(8,128)S(1)}, u32[]{:S(2)}, u32[]{:S(2)}) collective-permute-start(f32[256,1024]{1,0:T(8,128)S(1)} %get-tuple-element.127), channel_id=1, source_target_pairs={{0,6},{2,0},{4,14},{6,4},{8,2},{10,8},{12,22},{14,12},{16,10},{18,... | collective-permute-start | bytes 3145736 | tf_op jit(solution)/shard_map/ppermute | solution.py:568
  380.4 15.2 %collective-permute-start.32 = (f32[256,1024]{1,0:T(8,128)}, f32[256,1024]{1,0:T(8,128)}, u32[]{:S(2)}, u32[]{:S(2)}) collective-permute-start(f32[256,1024]{1,0:T(8,128)} %get-tuple-element.130), channel_id=1, source_target_pairs={{0,2},{2,8},{4,6},{6,0},{8,10},{10,16},{12,14},{14,4},{16,18},{18,... | collective-permute-start | bytes 3145736 | tf_op jit(solution)/shard_map/ppermute | solution.py:567
  380.4 15.2 %collective-permute-start.33 = (f32[256,1024]{1,0:T(8,128)}, f32[256,1024]{1,0:T(8,128)}, u32[]{:S(2)}, u32[]{:S(2)}) collective-permute-start(f32[256,1024]{1,0:T(8,128)} %get-tuple-element.131), channel_id=1, source_target_pairs={{0,6},{2,0},{4,14},{6,4},{8,2},{10,8},{12,22},{14,12},{16,10},{18,... | collective-permute-start | bytes 3145736 | tf_op jit(solution)/shard_map/ppermute | solution.py:568
  391.7 12.4 %collective-permute-start.34 = (f32[256,1024]{1,0:T(8,128)}, f32[256,1024]{1,0:T(8,128)}, u32[]{:S(2)}, u32[]{:S(2)}) collective-permute-start(f32[256,1024]{1,0:T(8,128)} %get-tuple-element.134), channel_id=1, source_target_pairs={{0,2},{2,8},{4,6},{6,0},{8,10},{10,16},{12,14},{14,4},{16,18},{18,... | collective-permute-start | bytes 3145736 | tf_op jit(solution)/shard_map/ppermute | solution.py:567
  391.8 14.8 %collective-permute-start.35 = (f32[256,1024]{1,0:T(8,128)}, f32[256,1024]{1,0:T(8,128)}, u32[]{:S(2)}, u32[]{:S(2)}) collective-permute-start(f32[256,1024]{1,0:T(8,128)} %get-tuple-element.135), channel_id=1, source_target_pairs={{0,6},{2,0},{4,14},{6,4},{8,2},{10,8},{12,22},{14,12},{16,10},{18,... | collective-permute-start | bytes 3145736 | tf_op jit(solution)/shard_map/ppermute | solution.py:568
  392.4 3.2 copy-start.5
  392.4 3.2 copy-start.9
  392.4 6.6 %collective-permute-start.31 = (f32[192,256]{1,0:T(8,128)S(1)}, f32[192,256]{1,0:T(8,128)S(1)}, u32[]{:S(2)}, u32[]{:S(2)}) collective-permute-start(f32[192,256]{1,0:T(8,128)S(1)} %get-tuple-element.128.here), channel_id=1, source_target_pairs={{0,1},{1,0},{2,3},{3,2},{4,5},{5,4},{6,7},{7,6},{8,9},{9,8},{10,11... | collective-permute-start | bytes 589832 | tf_op jit(solution)/shard_map/ppermute | solution.py:432
  395.6 3.4 copy-start.13
  395.7 3.5 copy-start.3
  399.1 0.7 copy-start.10
  406.6 4.3 %copy-start.1 = (f32[1024,256]{1,0:T(8,128)S(1)}, f32[1024,256]{1,0:T(8,128)}, u32[]{:S(2)}) copy-start(f32[1024,256]{1,0:T(8,128)} %param.7) | copy-start | bytes 3145732
  406.6 1.3 copy-start.7
Sparse Core Ops, SparseCore 0:
  11.3 183.2 all-gather.1

commit v4 on v3

--- a/solution.py
+++ b/solution.py
@@ -214,80 +214,71 @@
     return jnp.concatenate([hi, hi, lo], axis=axis)
 
 
-def student_kernel(u_ref, w_ref, m_ref, s_ref, score_a, score_b):
-    rows, tokens = score_a.shape
+def student_kernel(u_ref, w_hbm, m_ref, s_ref, w_ref, score_a, score_b, sems):
+    piece, tokens = score_a.shape
     held = (score_b, score_a)
-    step = pl.program_id(0)
-
-    def scores(start):
-        w_hi, w_lo = split(w_ref[start : start + rows, :])
-        return dot(parts_of_left(w_hi, w_lo, 1), u_ref[...])
+    count, rows, _ = w_ref.shape
+
+    def fetch(i):
+        start = pl.multiple_of(i * rows, rows)
+        return pltpu.make_async_copy(w_hbm.at[pl.ds(start, rows), :], w_ref.at[i], sems.at[i])
 
     def merge(logits, largest, total):
-        logits = logits.reshape(rows // 8, 8, tokens)
+        logits = logits.reshape(piece // 8, 8, tokens)
         best = jnp.maximum(largest, jnp.max(logits, axis=0))
         fresh = jnp.sum(jnp.exp2(logits - best[None]), axis=0)
         return best, total * jnp.exp2(largest - best) + fresh
 
-    @pl.when(step == 0)
-    def _():
-        m_ref[...] = jnp.full_like(m_ref, -1e30)
-        s_ref[...] = jnp.zeros_like(s_ref)
-        score_b[...] = jnp.full_like(score_b, -1e30)
-
-    stats = m_ref[...], s_ref[...]
-    pieces = w_ref.shape[0] // rows
-    for i in range(pieces):
-        held[(i + 1) % 2][...] = scores(i * rows)
-        stats = merge(held[i % 2][...], *stats)
-    m_ref[...], s_ref[...] = stats
-
-    @pl.when(step == pl.num_programs(0) - 1)
-    def _():
-        m_ref[...], s_ref[...] = merge(score_b[...], m_ref[...], s_ref[...])
+    for i in range(count):
+        fetch(i).start()
+    score_b[...] = jnp.full_like(score_b, -1e30)
+
+    def block(i, stats):
+        fetch(i).wait()
+        for j in range(rows // piece):
+            w_hi, w_lo = split(w_ref[i, j * piece : (j + 1) * piece, :])
+            held[(j + 1) % 2][...] = dot(parts_of_left(w_hi, w_lo, 1), u_ref[...])
+            stats = merge(held[j % 2][...], *stats)
+        return stats
+
+    start = (jnp.full(m_ref.shape, -1e30, F32), jnp.zeros(s_ref.shape, F32))
+    stats = lax.fori_loop(0, count, block, start)
+    m_ref[...], s_ref[...] = merge(score_b[...], *stats)
 
 
 def student_pass(u_turned, protos):
     tokens = u_turned.shape[1]
     rows, depth = protos.shape
     block = min(rows // 2, 2048)
-    stat = pl.BlockSpec((8, tokens), lambda i: (0, 0))
+    count = rows // block
+    vmem = pl.BlockSpec(memory_space=pltpu.VMEM)
     shape = jax.ShapeDtypeStruct((8, tokens), F32)
     return pl.pallas_call(
         student_kernel,
-        grid=(rows // block,),
-        in_specs=[
-            pl.BlockSpec(u_turned.shape, lambda i: (0, 0)),
-            pl.BlockSpec((block, depth), lambda i: (i, 0)),
+        in_specs=[vmem, pl.BlockSpec(memory_space=pltpu.HBM)],
+        out_specs=[vmem, vmem],
+        out_shape=[shape, shape],
+        scratch_shapes=[
+            pltpu.VMEM((count, block, depth), F32),
+            pltpu.VMEM((512, tokens), F32),
+            pltpu.VMEM((512, tokens), F32),
+            pltpu.SemaphoreType.DMA((count,)),
         ],
-        out_specs=[stat, stat],
-        out_shape=[shape, shape],
-        scratch_shapes=[pltpu.VMEM((min(block // 2, 512), tokens), F32)] * 2,
         compiler_params=params(STREAM_LIMIT),
         name="student_stats",
     )(u_turned, in_hbm(protos))
 
 
-def grad_kernel(own, u_parts, t_parts, lse, offset, tok_in, teacher, *refs, slots, arrivals, parity):
-    blocks = len(slots)
-    cols, protos = refs[:blocks], refs[blocks : 2 * blocks]
-    arrived = refs[2 * blocks : 2 * blocks + arrivals]
-    outs = refs[2 * blocks + arrivals : 3 * blocks + arrivals]
-    tok_out, teach, sems = refs[3 * blocks + arrivals :]
-    width, block = teach.shape[2], protos[0].shape[0]
-    step = pl.program_id(0)
-
-    def fetch(i):
-        start = pl.multiple_of(own[slots[i]] * width, LANES)
-        return pltpu.make_async_copy(teacher.at[:, pl.ds(start, width)], teach.at[i], sems.at[i])
-
-    @pl.when(step == 0)
+def grad_kernel(own, u_parts, t_parts, lse, offset, tok_in, *refs, blocks, arrivals, parity):
+    teach, cols, protos = refs[:blocks], refs[blocks : 2 * blocks], refs[2 * blocks : 3 * blocks]
+    arrived = refs[3 * blocks : 3 * blocks + arrivals]
+    outs = refs[3 * blocks + arrivals : 4 * blocks + arrivals]
+    tok_out = refs[4 * blocks + arrivals]
+
+    @pl.when(pl.program_id(0) == 0)
     def _():
-        for i in range(blocks):
-            fetch(i).start()
         tok_out[...] = tok_in[...]
 
-    columns = pl.ds(pl.multiple_of(step * block, LANES), block)
     token_part = tok_out[...]
     lse_col = lse[:, :1]
     off_col = offset[:, :1]
@@ -295,12 +286,7 @@
         w_hi, w_lo = split(protos[i][...])
         logits = dot(u_parts[...], parts_of_right(w_hi, w_lo, 1), ((1,), (1,)))
         student = jnp.exp2(logits - lse_col)
-
-        @pl.when(step == 0)
-        def _():
-            fetch(i).wait()
-
-        target = jnp.exp2(teach[i, :, columns].astype(F32) * TEACH - off_col) * cols[i][...]
+        target = jnp.exp2(teach[i][...].astype(F32) * TEACH - off_col) * cols[i][...]
         g_hi, g_lo = split(student - target)
         part = dot(t_parts[...], parts_of_right(g_hi, g_lo, 0))
         if arrivals == 1:
@@ -336,19 +322,15 @@
         grid=(count,),
         in_specs=[whole(c.shape) for c in consts]
         + [whole(tok.shape)]
-        + [pl.BlockSpec(memory_space=pltpu.HBM)]
+        + [picked((tokens, block), slot) for slot in slots]
         + [picked((1, block), slot) for slot in slots]
         + [rows((block, depth), slot) for slot in slots]
         + [across((depth, block)) for x in arrived],
         out_specs=[across((depth, block)) for slot in slots] + [whole(tok.shape)],
-        scratch_shapes=[
-            pltpu.VMEM((blocks, tokens, width), teacher.dtype),
-            pltpu.SemaphoreType.DMA((blocks,)),
-        ],
     )
     *parts, tok = pl.pallas_call(
         lambda *refs: grad_kernel(
-            *refs, slots=slots, arrivals=len(arrived), parity=own.shape[0] - 1
+            *refs, blocks=blocks, arrivals=len(arrived), parity=own.shape[0] - 1
         ),
         grid_spec=grid,
         out_shape=[jax.ShapeDtypeStruct((depth, width), F32) for slot in slots]
@@ -359,7 +341,7 @@
         own,
         *consts,
         tok,
-        in_hbm(teacher),
+        *([in_hbm(teacher)] * blocks),
         *([cols] * blocks),
         *([protos] * blocks),
         *arrived,
@@ -569,7 +551,7 @@
             ]
     token_here, token_there = sum_pair(token_part, "proto", proto_count)
     turned, gain_row = prototypes.T, gain[None, :]
-    grads = proto_grads(turned, gain_row, [mine[0], *waiting[0]], 0, ())
+    grads = proto_grads(turned, gain_row, [in_hbm(mine[0]), *waiting[0]], 0, ())
     input_grad = token_grads(
         token_here,
         token_there,
@@ -577,7 +559,7 @@
         jnp.broadcast_to(inverse, (tokens_here, LANES)),
         grads[1],
     )
-    grads = proto_grads(turned, gain_row, [mine[1], *waiting[1]], 1, grads)
+    grads = proto_grads(turned, gain_row, [in_hbm(mine[1]), *waiting[1]], 1, grads)
     grad_proto, grad_gain = grads[0], grads[1].reshape(shard)
     grad_packed = jnp.zeros(packed.shape, F32).at[row_index].set(input_grad)
     return (grad_packed, grad_proto, grad_gain)

time: 425 us -> 415 us (0.976)
  Pallas kernels: 204 us -> 179 us
  waiting for transfers between devices: 114 us -> 130 us
    pallas_call x19, Pallas kernels: 140 us -> 114 us  [the longest x18 94.8 us: grad_step(): pl.pallas_call(lambda *refs: grad_kernel(*refs, blocks=blocks, arrivals=l...]
    ppermute x14, waiting for transfers between devices: 11.6 us -> 25.3 us  [body(): lax.ppermute(first, 'dp', ahead)]
  transfers between devices with their start and end apart: 42 -> 42, of which waited for: 34 -> 36; matrix products, arithmetic and copies ran while one was open for 3% -> 3% of each run, Pallas kernels for 41% -> 37%
where the time goes in v4:
time: 415 us; the launch traced here: 409 us
  Pallas kernels  179 us (43%)
  waiting for transfers between devices  130 us (31%)
  starting transfers between devices  49.1 us (12%)
  blocking collectives  16.8 us (4%)
  between operations  15.2 us (4%)
  local copies, waits for them, and re-layouts  13.8 us (3%)
  other arithmetic  5.33 us (1%)
    pallas_call x18, Pallas kernels, grad_step(): pl.pallas_call(lambda *refs: grad_kernel(*refs, blocks=blocks, arrivals=l...  94.8 us
    ppermute x14, waiting for transfers between devices, body(): lax.ppermute(second, 'dp', behind)  32.9 us
    all_to_all x3, waiting for transfers between devices, column_total(): lax.all_to_all(jnp.broadcast_to(mine, x.shape), 'dp', 0, 0, tiled=True)  26.5 us
    ppermute x14, waiting for transfers between devices, body(): lax.ppermute(first, 'dp', ahead)  25.3 us
    pallas_call x3, Pallas kernels, column_pass(): pl.pallas_call(lambda *refs: column_kernel(*refs, unroll=min(16, shard //...  24 us
    pallas_call x3, Pallas kernels, row_pass(): pl.pallas_call(lambda *refs: row_kernel(*refs, unroll=min(16, block // LA...  21.5 us
    pallas_call x1, Pallas kernels, student_pass(): pl.pallas_call(student_kernel, in_specs=[vmem, pl.BlockSpec(memory_space=...  19.6 us
    all_gather x1, waiting for transfers between devices, body(): gathered = lax.all_gather(weights, 'dp', axis=0, tiled=True)  18.4 us
  transfers between devices with their start and end apart: 42, of which 36 were waited for; matrix products, arithmetic and copies ran while one was open for 3% of the time, Pallas kernels for 37%

profile of v4, /device:TPU:1, one launch (start us, length us, event | category | flops | bytes accessed | tf_op | source)
XLA Modules:
  0.0 409.3 jit_solution(4672724640609744209)
XLA Ops:
  11.2 13.0 %teacher_stats.1 = (f32[192,128]{1,0:T(8,128)S(1)}, f32[192,128]{1,0:T(8,128)S(1)}) custom-call(bf16[192,32768]{1,0:T(8,128)(2,1)} %refs_7_.27), custom_call_target="tpu_custom_call" | custom-call | tf_op jit(solution)/shard_map/teacher_stats/pallas_call | solution.py:97
  24.4 2.1 collective-permute-start.1
  28.4 6.4 %column_sums.3 = (f32[16,1,2048]{2,1,0:T(1,128)S(1)}, f32[192,128]{1,0:T(8,128)S(1)}) custom-call(bf16[192,32768]{1,0:T(8,128)(2,1)} %refs_7_.27, f32[192,128]{1,0:T(8,128)S(1)} %broadcast_in_dim.98.refs_1_, f32[192,128]{1,0:T(8,128)S(1)} %iota.17.refs_2_, f32[192,128]{1,0:T(8,128)S(1)} %broadcast_in_dim.101.refs_3_), custom_call_target="tpu_custom_call" | custom-call | tf_op jit(solution)/shard_map/column_sums/pallas_call | solution.py:142
  34.9 16.8 %all_to_all.30 = f32[16,1,2048]{2,1,0:T(1,128)S(1)} all-to-all(f32[16,1,2048]{2,1,0:T(1,128)S(1)} %get-tuple-element.76), channel_id=1, replica_groups=mesh['dp'=16,'proto'=2] {'dp'}, dimensions={0} | all-to-all | bytes 262144 | tf_op jit(solution)/shard_map/all_to_all | solution.py:425
  52.5 4.5 %all-to-all-start.1 = ((f32[16,1,2048]{2,1,0:T(1,128)}), f32[16,1,2048]{2,1,0:T(1,128)S(1)}, u32[]{:S(2)}, u32[]{:S(2)}) async-start(f32[16,1,2048]{2,1,0:T(1,128)} %broadcast_in_dim.102), calls=%async_computation.1 | async-start | bytes 262144 | tf_op jit(solution)/shard_map/all_to_all | solution.py:426
  57.0 9.3 %all-to-all-done.1.refs_2_ = f32[16,1,2048]{2,1,0:T(1,128)S(1)} async-done(((f32[16,1,2048]{2,1,0:T(1,128)}), f32[16,1,2048]{2,1,0:T(1,128)S(1)}, u32[]{:S(2)}, u32[]{:S(2)}) %all-to-all-start.1) | async-done | bytes 131104 | tf_op jit(solution)/shard_map/all_to_all | solution.py:426
  66.4 7.3 %row_sums.3 = (f32[192,128]{1,0:T(8,128)S(1)}, f32[1,32768]{1,0:T(1,128)}) custom-call(bf16[192,32768]{1,0:T(8,128)(2,1)} %refs_7_.27, f32[192,128]{1,0:T(8,128)S(1)} %get-tuple-element.75.refs_1_, f32[16,1,2048]{2,1,0:T(1,128)S(1)} %all-to-all-done.1.refs_2_), custom_call_target="tpu_custom_call" | custom-call | tf_op jit(solution)/shard_map/row_sums/pallas_call | solution.py:190
  75.1 2.5 collective-permute-done.2.refs_3_
  77.6 8.8 %column_sums.4 = (f32[16,1,2048]{2,1,0:T(1,128)}, f32[192,128]{1,0:T(8,128)S(1)}) custom-call(bf16[192,32768]{1,0:T(8,128)(2,1)} %refs_7_.27, f32[192,128]{1,0:T(8,128)S(1)} %get-tuple-element.75.refs_1_, f32[192,128]{1,0:T(8,128)S(1)} %get-tuple-element.77.refs_2_, f32[192,128]{1,0:T(8,128)S(1)} %collective-permute-done.2.refs_3_), custom_call_target="tpu_custom_call" | custom-call | tf_op jit(solution)/shard_map/column_sums/pallas_call | solution.py:142
  86.4 5.3 %all-to-all-start.2 = ((f32[16,1,2048]{2,1,0:T(1,128)}), f32[16,1,2048]{2,1,0:T(1,128)S(1)}, u32[]{:S(2)}, u32[]{:S(2)}) async-start(f32[16,1,2048]{2,1,0:T(1,128)} %get-tuple-element.79), calls=%async_computation.2 | async-start | bytes 262144 | tf_op jit(solution)/shard_map/all_to_all | solution.py:425
  93.1 7.9 %all-to-all-done.2 = f32[16,1,2048]{2,1,0:T(1,128)S(1)} async-done(((f32[16,1,2048]{2,1,0:T(1,128)}), f32[16,1,2048]{2,1,0:T(1,128)S(1)}, u32[]{:S(2)}, u32[]{:S(2)}) %all-to-all-start.2) | async-done | bytes 131104 | tf_op jit(solution)/shard_map/all_to_all | solution.py:425
  101.8 4.5 %all-to-all-start.3 = ((f32[16,1,2048]{2,1,0:T(1,128)}), f32[16,1,2048]{2,1,0:T(1,128)S(1)}, u32[]{:S(2)}, u32[]{:S(2)}) async-start(f32[16,1,2048]{2,1,0:T(1,128)} %broadcast_in_dim.103), calls=%async_computation.3 | async-start | bytes 262144 | tf_op jit(solution)/shard_map/all_to_all | solution.py:426
  106.5 9.1 %all-to-all-done.3.refs_2_ = f32[16,1,2048]{2,1,0:T(1,128)S(1)} async-done(((f32[16,1,2048]{2,1,0:T(1,128)}), f32[16,1,2048]{2,1,0:T(1,128)S(1)}, u32[]{:S(2)}, u32[]{:S(2)}) %all-to-all-start.3) | async-done | bytes 131104 | tf_op jit(solution)/shard_map/all_to_all | solution.py:426
  115.7 7.3 %row_sums.4 = (f32[192,128]{1,0:T(8,128)S(1)}, f32[1,32768]{1,0:T(1,128)}) custom-call(bf16[192,32768]{1,0:T(8,128)(2,1)} %refs_7_.27, f32[192,128]{1,0:T(8,128)S(1)} %get-tuple-element.78.refs_1_, f32[16,1,2048]{2,1,0:T(1,128)S(1)} %all-to-all-done.3.refs_2_), custom_call_target="tpu_custom_call" | custom-call | tf_op jit(solution)/shard_map/row_sums/pallas_call | solution.py:190
  124.3 2.5 collective-permute-done.3.refs_3_
  126.9 8.8 %column_sums.5 = (f32[16,1,2048]{2,1,0:T(1,128)}, f32[192,128]{1,0:T(8,128)S(1)}) custom-call(bf16[192,32768]{1,0:T(8,128)(2,1)} %refs_7_.27, f32[192,128]{1,0:T(8,128)S(1)} %get-tuple-element.78.refs_1_, f32[192,128]{1,0:T(8,128)S(1)} %get-tuple-element.80.refs_2_, f32[192,128]{1,0:T(8,128)S(1)} %collective-permute-done.3.refs_3_), custom_call_target="tpu_custom_call" | custom-call | tf_op jit(solution)/shard_map/column_sums/pallas_call | solution.py:142
  135.7 5.3 %all-to-all-start.4 = ((f32[16,1,2048]{2,1,0:T(1,128)}), f32[16,1,2048]{2,1,0:T(1,128)S(1)}, u32[]{:S(2)}, u32[]{:S(2)}) async-start(f32[16,1,2048]{2,1,0:T(1,128)} %get-tuple-element.82), calls=%async_computation.4 | async-start | bytes 262144 | tf_op jit(solution)/shard_map/all_to_all | solution.py:425
  141.0 9.3 %all-to-all-done.4 = f32[16,1,2048]{2,1,0:T(1,128)S(1)} async-done(((f32[16,1,2048]{2,1,0:T(1,128)}), f32[16,1,2048]{2,1,0:T(1,128)S(1)}, u32[]{:S(2)}, u32[]{:S(2)}) %all-to-all-start.4) | async-done | bytes 131104 | tf_op jit(solution)/shard_map/all_to_all | solution.py:425
  151.1 4.8 %all-to-all-start.5 = ((f32[16,1,2048]{2,1,0:T(1,128)}), f32[16,1,2048]{2,1,0:T(1,128)S(1)}, u32[]{:S(2)}, u32[]{:S(2)}) async-start(f32[16,1,2048]{2,1,0:T(1,128)} %broadcast_in_dim.104), calls=%async_computation.5 | async-start | bytes 262144 | tf_op jit(solution)/shard_map/all_to_all | solution.py:426
  157.1 8.1 %all-to-all-done.5.refs_2_ = f32[16,1,2048]{2,1,0:T(1,128)S(1)} async-done(((f32[16,1,2048]{2,1,0:T(1,128)}), f32[16,1,2048]{2,1,0:T(1,128)S(1)}, u32[]{:S(2)}, u32[]{:S(2)}) %all-to-all-start.5) | async-done | bytes 131104 | tf_op jit(solution)/shard_map/all_to_all | solution.py:426
  165.2 7.0 %row_sums.5 = (f32[192,128]{1,0:T(8,128)S(1)}, f32[1,32768]{1,0:T(1,128)S(1)}) custom-call(bf16[192,32768]{1,0:T(8,128)(2,1)} %refs_7_.27, f32[192,128]{1,0:T(8,128)S(1)} %get-tuple-element.81.refs_1_, f32[16,1,2048]{2,1,0:T(1,128)S(1)} %all-to-all-done.5.refs_2_), custom_call_target="tpu_custom_call" | custom-call | tf_op jit(solution)/shard_map/row_sums/pallas_call | solution.py:190
  173.7 2.4 collective-permute-done.4
  176.2 18.4 %all-gather.2.cloned.1.call-done.w_hbm.refs_8_.refs_10_.refs_11_ = f32[32768,256]{1,0:T(8,128)} async-done(((f32[2048,256]{1,0:T(8,128)}), f32[32768,256]{1,0:T(8,128)}) %all-gather.2.cloned.1.call-update) | async-done | bytes 33554448 | tf_op jit(solution)/shard_map/all_gather | solution.py:487
  194.6 19.6 %student_stats.1 = (f32[8,192]{1,0:T(8,128)S(1)}, f32[8,192]{1,0:T(8,128)S(1)}) custom-call(bf16[768,192]{1,0:T(8,128)(2,1)S(1)} %copy.80.u_ref, f32[32768,256]{1,0:T(8,128)} %all-gather.2.cloned.1.call-done.w_hbm.refs_8_.refs_10_.refs_11_), custom_call_target="tpu_custom_call" | custom-call | tf_op jit(solution)/shard_map/student_stats/pallas_call | solution.py:256
  216.9 3.7 grad_blocks.18
  222.1 3.7 grad_blocks.19
  225.9 5.6 %grad_blocks.20 = (f32[256,1024]{1,0:T(8,128)S(1)}, f32[256,1024]{1,0:T(8,128)S(1)}, f32[192,256]{1,0:T(8,128)S(1)}) custom-call(s32[33]{0:T(128)S(1)} %dynamic-slice_bitcast_fusion.refs_0_, bf16[192,768]{1,0:T(8,128)(2,1)S(1)} %get-tuple-element.144.refs_1_, bf16[256,576]{1,0:T(8,128)(2,1)S(1)} %copy.102.refs_2_, f32[192,128]{1,0:T(8,128)S(1)} %broadcast_in_dim.96.refs_3_, ...), custom_call_target="tpu_custom_call" | custom-call | tf_op jit(solution)/shard_map/grad_blocks/pallas_call | solution.py:331
  231.6 5.8 %collective-permute-start.7 = (f32[256,1024]{1,0:T(8,128)S(1)}, f32[256,1024]{1,0:T(8,128)S(1)}, u32[]{:S(2)}, u32[]{:S(2)}) collective-permute-start(f32[256,1024]{1,0:T(8,128)S(1)} %get-tuple-element.91), channel_id=1, source_target_pairs={{0,2},{2,8},{4,6},{6,0},{8,10},{10,16},{12,14},{14,4},{16,18},{18,... | collective-permute-start | bytes 3145736 | tf_op jit(solution)/shard_map/ppermute | solution.py:549
  237.4 5.6 %grad_blocks.21 = (f32[256,1024]{1,0:T(8,128)S(1)}, f32[256,1024]{1,0:T(8,128)S(1)}, f32[192,256]{1,0:T(8,128)S(1)}) custom-call(s32[33]{0:T(128)S(1)} %dynamic-slice_bitcast_fusion.refs_0_, bf16[192,768]{1,0:T(8,128)(2,1)S(1)} %get-tuple-element.144.refs_1_, bf16[256,576]{1,0:T(8,128)(2,1)S(1)} %copy.102.refs_2_, f32[192,128]{1,0:T(8,128)S(1)} %broadcast_in_dim.96.refs_3_, ...), custom_call_target="tpu_custom_call" | custom-call | tf_op jit(solution)/shard_map/grad_blocks/pallas_call | solution.py:331
  244.8 4.3 %collective-permute-done.7.refs_12_ = f32[256,1024]{1,0:T(8,128)S(1)} collective-permute-done((f32[256,1024]{1,0:T(8,128)S(1)}, f32[256,1024]{1,0:T(8,128)S(1)}, u32[]{:S(2)}, u32[]{:S(2)}) %collective-permute-start.7) | collective-permute-done | bytes 1048608 | tf_op jit(solution)/shard_map/ppermute | solution.py:549
  249.2 2.8 collective-permute-done.8.refs_13_
  251.9 5.6 %grad_blocks.22 = (f32[256,1024]{1,0:T(8,128)S(1)}, f32[256,1024]{1,0:T(8,128)S(1)}, f32[192,256]{1,0:T(8,128)S(1)}) custom-call(s32[33]{0:T(128)S(1)} %dynamic-slice_bitcast_fusion.refs_0_, bf16[192,768]{1,0:T(8,128)(2,1)S(1)} %get-tuple-element.144.refs_1_, bf16[256,576]{1,0:T(8,128)(2,1)S(1)} %copy.102.refs_2_, f32[192,128]{1,0:T(8,128)S(1)} %broadcast_in_dim.96.refs_3_, ...), custom_call_target="tpu_custom_call" | custom-call | tf_op jit(solution)/shard_map/grad_blocks/pallas_call | solution.py:331
  258.1 2.3 collective-permute-done.9.refs_12_
  260.4 2.8 collective-permute-done.10.refs_13_
  263.2 5.6 %grad_blocks.23 = (f32[256,1024]{1,0:T(8,128)S(1)}, f32[256,1024]{1,0:T(8,128)S(1)}, f32[192,256]{1,0:T(8,128)S(1)}) custom-call(s32[33]{0:T(128)S(1)} %dynamic-slice_bitcast_fusion.refs_0_, bf16[192,768]{1,0:T(8,128)(2,1)S(1)} %get-tuple-element.144.refs_1_, bf16[256,576]{1,0:T(8,128)(2,1)S(1)} %copy.102.refs_2_, f32[192,128]{1,0:T(8,128)S(1)} %broadcast_in_dim.96.refs_3_, ...), custom_call_target="tpu_custom_call" | custom-call | tf_op jit(solution)/shard_map/grad_blocks/pallas_call | solution.py:331
  269.5 3.7 grad_blocks.24
  274.4 5.6 %grad_blocks.25 = (f32[256,1024]{1,0:T(8,128)S(1)}, f32[256,1024]{1,0:T(8,128)S(1)}, f32[192,256]{1,0:T(8,128)S(1)}) custom-call(s32[33]{0:T(128)S(1)} %dynamic-slice_bitcast_fusion.refs_0_, bf16[192,768]{1,0:T(8,128)(2,1)S(1)} %get-tuple-element.144.refs_1_, bf16[256,576]{1,0:T(8,128)(2,1)S(1)} %copy.102.refs_2_, f32[192,128]{1,0:T(8,128)S(1)} %broadcast_in_dim.96.refs_3_, ...), custom_call_target="tpu_custom_call" | custom-call | tf_op jit(solution)/shard_map/grad_blocks/pallas_call | solution.py:331
  280.6 2.3 collective-permute-done.13.refs_12_
  282.9 2.8 collective-permute-done.14.refs_13_
  285.6 5.6 %grad_blocks.26 = (f32[256,1024]{1,0:T(8,128)S(1)}, f32[256,1024]{1,0:T(8,128)S(1)}, f32[192,256]{1,0:T(8,128)S(1)}) custom-call(s32[33]{0:T(128)S(1)} %dynamic-slice_bitcast_fusion.refs_0_, bf16[192,768]{1,0:T(8,128)(2,1)S(1)} %get-tuple-element.144.refs_1_, bf16[256,576]{1,0:T(8,128)(2,1)S(1)} %copy.102.refs_2_, f32[192,128]{1,0:T(8,128)S(1)} %broadcast_in_dim.96.refs_3_, ...), custom_call_target="tpu_custom_call" | custom-call | tf_op jit(solution)/shard_map/grad_blocks/pallas_call | solution.py:331
  291.8 3.7 grad_blocks.27
  296.9 5.6 %grad_blocks.28 = (f32[256,1024]{1,0:T(8,128)S(1)}, f32[256,1024]{1,0:T(8,128)S(1)}, f32[192,256]{1,0:T(8,128)S(1)}) custom-call(s32[33]{0:T(128)S(1)} %dynamic-slice_bitcast_fusion.refs_0_, bf16[192,768]{1,0:T(8,128)(2,1)S(1)} %get-tuple-element.144.refs_1_, bf16[256,576]{1,0:T(8,128)(2,1)S(1)} %copy.102.refs_2_, f32[192,128]{1,0:T(8,128)S(1)} %broadcast_in_dim.96.refs_3_, ...), custom_call_target="tpu_custom_call" | custom-call | tf_op jit(solution)/shard_map/grad_blocks/pallas_call | solution.py:331
  303.0 2.3 collective-permute-done.17.refs_12_
  305.3 2.8 collective-permute-done.18.refs_13_
  308.1 5.6 %grad_blocks.29 = (f32[256,1024]{1,0:T(8,128)S(1)}, f32[256,1024]{1,0:T(8,128)S(1)}, f32[192,256]{1,0:T(8,128)S(1)}) custom-call(s32[33]{0:T(128)S(1)} %dynamic-slice_bitcast_fusion.refs_0_, bf16[192,768]{1,0:T(8,128)(2,1)S(1)} %get-tuple-element.144.refs_1_, bf16[256,576]{1,0:T(8,128)(2,1)S(1)} %copy.102.refs_2_, f32[192,128]{1,0:T(8,128)S(1)} %broadcast_in_dim.96.refs_3_, ...), custom_call_target="tpu_custom_call" | custom-call | tf_op jit(solution)/shard_map/grad_blocks/pallas_call | solution.py:331
  314.3 2.3 collective-permute-done.19.refs_12_
  316.6 2.8 collective-permute-done.20.refs_13_
  319.3 5.6 %grad_blocks.30 = (f32[256,1024]{1,0:T(8,128)S(1)}, f32[256,1024]{1,0:T(8,128)S(1)}, f32[192,256]{1,0:T(8,128)S(1)}) custom-call(s32[33]{0:T(128)S(1)} %dynamic-slice_bitcast_fusion.refs_0_, bf16[192,768]{1,0:T(8,128)(2,1)S(1)} %get-tuple-element.144.refs_1_, bf16[256,576]{1,0:T(8,128)(2,1)S(1)} %copy.102.refs_2_, f32[192,128]{1,0:T(8,128)S(1)} %broadcast_in_dim.96.refs_3_, ...), custom_call_target="tpu_custom_call" | custom-call | tf_op jit(solution)/shard_map/grad_blocks/pallas_call | solution.py:331
  327.8 2.8 collective-permute-done.22.refs_13_
  330.6 5.6 %grad_blocks.31 = (f32[256,1024]{1,0:T(8,128)S(1)}, f32[256,1024]{1,0:T(8,128)S(1)}, f32[192,256]{1,0:T(8,128)S(1)}) custom-call(s32[33]{0:T(128)S(1)} %dynamic-slice_bitcast_fusion.refs_0_, bf16[192,768]{1,0:T(8,128)(2,1)S(1)} %get-tuple-element.144.refs_1_, bf16[256,576]{1,0:T(8,128)(2,1)S(1)} %copy.102.refs_2_, f32[192,128]{1,0:T(8,128)S(1)} %broadcast_in_dim.96.refs_3_, ...), custom_call_target="tpu_custom_call" | custom-call | tf_op jit(solution)/shard_map/grad_blocks/pallas_call | solution.py:331
  336.8 2.3 collective-permute-done.23.refs_12_
  339.0 2.8 collective-permute-done.24.refs_13_
  341.8 5.6 %grad_blocks.32 = (f32[256,1024]{1,0:T(8,128)S(1)}, f32[256,1024]{1,0:T(8,128)S(1)}, f32[192,256]{1,0:T(8,128)S(1)}) custom-call(s32[33]{0:T(128)S(1)} %dynamic-slice_bitcast_fusion.refs_0_, bf16[192,768]{1,0:T(8,128)(2,1)S(1)} %get-tuple-element.144.refs_1_, bf16[256,576]{1,0:T(8,128)(2,1)S(1)} %copy.102.refs_2_, f32[192,128]{1,0:T(8,128)S(1)} %broadcast_in_dim.96.refs_3_, ...), custom_call_target="tpu_custom_call" | custom-call | tf_op jit(solution)/shard_map/grad_blocks/pallas_call | solution.py:331
  348.0 2.3 collective-permute-done.25.refs_12_
  350.3 2.8 collective-permute-done.26.refs_13_
  353.1 5.6 %grad_blocks.33 = (f32[256,1024]{1,0:T(8,128)S(1)}, f32[256,1024]{1,0:T(8,128)S(1)}, f32[192,256]{1,0:T(8,128)S(1)}) custom-call(s32[33]{0:T(128)S(1)} %dynamic-slice_bitcast_fusion.refs_0_, bf16[192,768]{1,0:T(8,128)(2,1)S(1)} %get-tuple-element.144.refs_1_, bf16[256,576]{1,0:T(8,128)(2,1)S(1)} %copy.102.refs_2_, f32[192,128]{1,0:T(8,128)S(1)} %broadcast_in_dim.96.refs_3_, ...), custom_call_target="tpu_custom_call" | custom-call | tf_op jit(solution)/shard_map/grad_blocks/pallas_call | solution.py:331
  359.2 2.3 collective-permute-done.27.refs_12_
  361.5 2.8 collective-permute-done.28.refs_13_
  364.3 6.3 %grad_blocks.34 = (f32[256,1024]{1,0:T(8,128)}, f32[256,1024]{1,0:T(8,128)}, f32[192,256]{1,0:T(8,128)S(1)}) custom-call(s32[33]{0:T(128)S(1)} %dynamic-slice_bitcast_fusion.refs_0_, bf16[192,768]{1,0:T(8,128)(2,1)S(1)} %get-tuple-element.144.refs_1_, bf16[256,576]{1,0:T(8,128)(2,1)S(1)} %copy.102.refs_2_, f32[192,128]{1,0:T(8,128)S(1)} %broadcast_in_dim.96.refs_3_, ...), custom_call_target="tpu_custom_call" | custom-call | tf_op jit(solution)/shard_map/grad_blocks/pallas_call | solution.py:331
  372.7 2.9 collective-permute-done.30.refs_13_
  375.6 6.3 %grad_blocks.35 = (f32[256,1024]{1,0:T(8,128)}, f32[256,1024]{1,0:T(8,128)}, f32[192,256]{1,0:T(8,128)S(1)}) custom-call(s32[33]{0:T(128)S(1)} %dynamic-slice_bitcast_fusion.refs_0_, bf16[192,768]{1,0:T(8,128)(2,1)S(1)} %get-tuple-element.144.refs_1_, bf16[256,576]{1,0:T(8,128)(2,1)S(1)} %copy.102.refs_2_, f32[192,128]{1,0:T(8,128)S(1)} %broadcast_in_dim.96.refs_3_, ...), custom_call_target="tpu_custom_call" | custom-call | tf_op jit(solution)/shard_map/grad_blocks/pallas_call | solution.py:331
  386.8 3.2 proto_grads.2
  391.6 2.6 scatter_custom_fusion
  399.1 2.9 proto_grads.3
  (138 shorter events, 45.8 us)
Async XLA Ops:
  7.2 85.1 %copy-start = (f32[1024,256]{1,0:T(8,128)S(1)}, f32[1024,256]{1,0:T(8,128)}, u32[]{:S(2)}) copy-start(f32[1024,256]{1,0:T(8,128)} %param.7) | copy-start | bytes 3145732
  7.2 2.3 copy-start.12
  7.2 2.2 copy-start.9
  7.2 187.4 %all-gather.2.cloned.1.call-start = ((), (), s32[]{:S(2)}) async-start(), calls=%async_computation.6 | async-start | bytes 35651584 | tf_op jit(solution)/shard_map/all_gather | solution.py:487
  24.4 3.5 collective-permute-start.1
  52.5 13.9 %all-to-all-start.1 = ((f32[16,1,2048]{2,1,0:T(1,128)}), f32[16,1,2048]{2,1,0:T(1,128)S(1)}, u32[]{:S(2)}, u32[]{:S(2)}) async-start(f32[16,1,2048]{2,1,0:T(1,128)} %broadcast_in_dim.102), calls=%async_computation.1 | async-start | bytes 262144 | tf_op jit(solution)/shard_map/all_to_all | solution.py:426
  66.4 8.6 %copy-start.17 = (s32[3]{0:T(128)S(1)}, s32[3]{0:T(128)}, u32[]{:S(2)}) copy-start(s32[3]{0:T(128)} %param.8) | copy-start | bytes 40
  73.7 3.9 collective-permute-start.2
  75.0 16.6 %copy-start.16 = (s32[192]{0:T(256)S(1)}, s32[192]{0:T(256)}, u32[]{:S(2)}) copy-start(s32[192]{0:T(256)} %param.9) | copy-start | bytes 2308
  86.4 14.6 %all-to-all-start.2 = ((f32[16,1,2048]{2,1,0:T(1,128)}), f32[16,1,2048]{2,1,0:T(1,128)S(1)}, u32[]{:S(2)}, u32[]{:S(2)}) async-start(f32[16,1,2048]{2,1,0:T(1,128)} %get-tuple-element.79), calls=%async_computation.2 | async-start | bytes 262144 | tf_op jit(solution)/shard_map/all_to_all | solution.py:425
  91.7 0.6 copy-start.15
  101.8 13.9 %all-to-all-start.3 = ((f32[16,1,2048]{2,1,0:T(1,128)}), f32[16,1,2048]{2,1,0:T(1,128)S(1)}, u32[]{:S(2)}, u32[]{:S(2)}) async-start(f32[16,1,2048]{2,1,0:T(1,128)} %broadcast_in_dim.103), calls=%async_computation.3 | async-start | bytes 262144 | tf_op jit(solution)/shard_map/all_to_all | solution.py:426
  106.5 17.7 %copy-start.13 = (f32[192]{0:T(256)}, f32[192]{0:T(256)S(1)}, u32[]{:S(2)}) copy-start(f32[192]{0:T(256)S(1)} %add_rsqrt_fusion) | copy-start | bytes 2308
  122.9 3.9 collective-permute-start.3
  124.3 16.7 %copy-start.2 = (f32[192,256]{1,0:T(8,128)}, f32[192,256]{1,0:T(8,128)S(1)}, u32[]{:S(2)}) copy-start(f32[192,256]{1,0:T(8,128)S(1)} %get-tuple-element.140.unit) | copy-start | bytes 589828
  135.7 14.6 %all-to-all-start.4 = ((f32[16,1,2048]{2,1,0:T(1,128)}), f32[16,1,2048]{2,1,0:T(1,128)S(1)}, u32[]{:S(2)}, u32[]{:S(2)}) async-start(f32[16,1,2048]{2,1,0:T(1,128)} %get-tuple-element.82), calls=%async_computation.4 | async-start | bytes 262144 | tf_op jit(solution)/shard_map/all_to_all | solution.py:425
  151.1 14.0 %all-to-all-start.5 = ((f32[16,1,2048]{2,1,0:T(1,128)}), f32[16,1,2048]{2,1,0:T(1,128)S(1)}, u32[]{:S(2)}, u32[]{:S(2)}) async-start(f32[16,1,2048]{2,1,0:T(1,128)} %broadcast_in_dim.104), calls=%async_computation.5 | async-start | bytes 262144 | tf_op jit(solution)/shard_map/all_to_all | solution.py:426
  172.1 3.9 collective-permute-start.4
  214.2 2.5 collective-permute-start
  220.6 5.3 %collective-permute-start.5 = (f32[256,1024]{1,0:T(8,128)S(1)}, f32[256,1024]{1,0:T(8,128)S(1)}, u32[]{:S(2)}, u32[]{:S(2)}) collective-permute-start(f32[256,1024]{1,0:T(8,128)S(1)} %get-tuple-element.87), channel_id=1, source_target_pairs={{0,2},{2,0},{4,6},{6,4},{8,10},{10,8},{12,14},{14,12},{16,18},{18,... | collective-permute-start | bytes 3145736 | tf_op jit(solution)/shard_map/ppermute | solution.py:414
  225.9 11.6 %collective-permute-start.6 = (f32[256,1024]{1,0:T(8,128)S(1)}, f32[256,1024]{1,0:T(8,128)S(1)}, u32[]{:S(2)}, u32[]{:S(2)}) collective-permute-start(f32[256,1024]{1,0:T(8,128)S(1)} %get-tuple-element.89), channel_id=1, source_target_pairs={{0,2},{2,0},{4,6},{6,4},{8,10},{10,8},{12,14},{14,12},{16,18},{18,... | collective-permute-start | bytes 3145736 | tf_op jit(solution)/shard_map/ppermute | solution.py:414
  231.6 17.6 %collective-permute-start.7 = (f32[256,1024]{1,0:T(8,128)S(1)}, f32[256,1024]{1,0:T(8,128)S(1)}, u32[]{:S(2)}, u32[]{:S(2)}) collective-permute-start(f32[256,1024]{1,0:T(8,128)S(1)} %get-tuple-element.91), channel_id=1, source_target_pairs={{0,2},{2,8},{4,6},{6,0},{8,10},{10,16},{12,14},{14,4},{16,18},{18,... | collective-permute-start | bytes 3145736 | tf_op jit(solution)/shard_map/ppermute | solution.py:549
  237.4 14.5 %collective-permute-start.8 = (f32[256,1024]{1,0:T(8,128)S(1)}, f32[256,1024]{1,0:T(8,128)S(1)}, u32[]{:S(2)}, u32[]{:S(2)}) collective-permute-start(f32[256,1024]{1,0:T(8,128)S(1)} %get-tuple-element.92), channel_id=1, source_target_pairs={{0,6},{2,0},{4,14},{6,4},{8,2},{10,8},{12,22},{14,12},{16,10},{18,... | collective-permute-start | bytes 3145736 | tf_op jit(solution)/shard_map/ppermute | solution.py:550
  243.0 17.4 %collective-permute-start.9 = (f32[256,1024]{1,0:T(8,128)S(1)}, f32[256,1024]{1,0:T(8,128)S(1)}, u32[]{:S(2)}, u32[]{:S(2)}) collective-permute-start(f32[256,1024]{1,0:T(8,128)S(1)} %get-tuple-element.94), channel_id=1, source_target_pairs={{0,2},{2,8},{4,6},{6,0},{8,10},{10,16},{12,14},{14,4},{16,18},{18,... | collective-permute-start | bytes 3145736 | tf_op jit(solution)/shard_map/ppermute | solution.py:549
  244.8 18.3 %collective-permute-start.10 = (f32[256,1024]{1,0:T(8,128)S(1)}, f32[256,1024]{1,0:T(8,128)S(1)}, u32[]{:S(2)}, u32[]{:S(2)}) collective-permute-start(f32[256,1024]{1,0:T(8,128)S(1)} %get-tuple-element.95), channel_id=1, source_target_pairs={{0,6},{2,0},{4,14},{6,4},{8,2},{10,8},{12,22},{14,12},{16,10},{18,... | collective-permute-start | bytes 3145736 | tf_op jit(solution)/shard_map/ppermute | solution.py:550
  257.5 15.8 %collective-permute-start.11 = (f32[256,1024]{1,0:T(8,128)S(1)}, f32[256,1024]{1,0:T(8,128)S(1)}, u32[]{:S(2)}, u32[]{:S(2)}) collective-permute-start(f32[256,1024]{1,0:T(8,128)S(1)} %get-tuple-element.98), channel_id=1, source_target_pairs={{0,2},{2,8},{4,6},{6,0},{8,10},{10,16},{12,14},{14,4},{16,18},{18,... | collective-permute-start | bytes 3145736 | tf_op jit(solution)/shard_map/ppermute | solution.py:549
  257.6 16.8 %collective-permute-start.12 = (f32[256,1024]{1,0:T(8,128)S(1)}, f32[256,1024]{1,0:T(8,128)S(1)}, u32[]{:S(2)}, u32[]{:S(2)}) collective-permute-start(f32[256,1024]{1,0:T(8,128)S(1)} %get-tuple-element.99), channel_id=1, source_target_pairs={{0,6},{2,0},{4,14},{6,4},{8,2},{10,8},{12,22},{14,12},{16,10},{18,... | collective-permute-start | bytes 3145736 | tf_op jit(solution)/shard_map/ppermute | solution.py:550
  268.8 14.1 %collective-permute-start.13 = (f32[256,1024]{1,0:T(8,128)S(1)}, f32[256,1024]{1,0:T(8,128)S(1)}, u32[]{:S(2)}, u32[]{:S(2)}) collective-permute-start(f32[256,1024]{1,0:T(8,128)S(1)} %get-tuple-element.101), channel_id=1, source_target_pairs={{0,2},{2,8},{4,6},{6,0},{8,10},{10,16},{12,14},{14,4},{16,18},{18,... | collective-permute-start | bytes 3145736 | tf_op jit(solution)/shard_map/ppermute | solution.py:549
  268.8 16.8 %collective-permute-start.14 = (f32[256,1024]{1,0:T(8,128)S(1)}, f32[256,1024]{1,0:T(8,128)S(1)}, u32[]{:S(2)}, u32[]{:S(2)}) collective-permute-start(f32[256,1024]{1,0:T(8,128)S(1)} %get-tuple-element.102), channel_id=1, source_target_pairs={{0,6},{2,0},{4,14},{6,4},{8,2},{10,8},{12,22},{14,12},{16,10},{18,... | collective-permute-start | bytes 3145736 | tf_op jit(solution)/shard_map/ppermute | solution.py:550
  273.3 6.7 %copy-start.4 = (f32[256,1024]{1,0:T(8,128)}, f32[256,1024]{1,0:T(8,128)S(1)}, u32[]{:S(2)}) copy-start(f32[256,1024]{1,0:T(8,128)S(1)} %get-tuple-element.129.a) | copy-start | bytes 3145732
  280.0 15.5 %collective-permute-start.15 = (f32[256,1024]{1,0:T(8,128)S(1)}, f32[256,1024]{1,0:T(8,128)S(1)}, u32[]{:S(2)}, u32[]{:S(2)}) collective-permute-start(f32[256,1024]{1,0:T(8,128)S(1)} %get-tuple-element.105), channel_id=1, source_target_pairs={{0,2},{2,8},{4,6},{6,0},{8,10},{10,16},{12,14},{14,4},{16,18},{18,... | collective-permute-start | bytes 3145736 | tf_op jit(solution)/shard_map/ppermute | solution.py:549
  280.3 16.6 %collective-permute-start.16 = (f32[256,1024]{1,0:T(8,128)S(1)}, f32[256,1024]{1,0:T(8,128)S(1)}, u32[]{:S(2)}, u32[]{:S(2)}) collective-permute-start(f32[256,1024]{1,0:T(8,128)S(1)} %get-tuple-element.106), channel_id=1, source_target_pairs={{0,6},{2,0},{4,14},{6,4},{8,2},{10,8},{12,22},{14,12},{16,10},{18,... | collective-permute-start | bytes 3145736 | tf_op jit(solution)/shard_map/ppermute | solution.py:550
  291.2 14.1 %collective-permute-start.17 = (f32[256,1024]{1,0:T(8,128)S(1)}, f32[256,1024]{1,0:T(8,128)S(1)}, u32[]{:S(2)}, u32[]{:S(2)}) collective-permute-start(f32[256,1024]{1,0:T(8,128)S(1)} %get-tuple-element.108), channel_id=1, source_target_pairs={{0,2},{2,8},{4,6},{6,0},{8,10},{10,16},{12,14},{14,4},{16,18},{18,... | collective-permute-start | bytes 3145736 | tf_op jit(solution)/shard_map/ppermute | solution.py:549
  291.3 16.8 %collective-permute-start.18 = (f32[256,1024]{1,0:T(8,128)S(1)}, f32[256,1024]{1,0:T(8,128)S(1)}, u32[]{:S(2)}, u32[]{:S(2)}) collective-permute-start(f32[256,1024]{1,0:T(8,128)S(1)} %get-tuple-element.109), channel_id=1, source_target_pairs={{0,6},{2,0},{4,14},{6,4},{8,2},{10,8},{12,22},{14,12},{16,10},{18,... | collective-permute-start | bytes 3145736 | tf_op jit(solution)/shard_map/ppermute | solution.py:550
  295.6 6.9 %copy-start.5 = (f32[256,1024]{1,0:T(8,128)}, f32[256,1024]{1,0:T(8,128)S(1)}, u32[]{:S(2)}) copy-start(f32[256,1024]{1,0:T(8,128)S(1)} %get-tuple-element.133.a) | copy-start | bytes 3145732
  302.5 14.1 %collective-permute-start.19 = (f32[256,1024]{1,0:T(8,128)S(1)}, f32[256,1024]{1,0:T(8,128)S(1)}, u32[]{:S(2)}, u32[]{:S(2)}) collective-permute-start(f32[256,1024]{1,0:T(8,128)S(1)} %get-tuple-element.111), channel_id=1, source_target_pairs={{0,2},{2,8},{4,6},{6,0},{8,10},{10,16},{12,14},{14,4},{16,18},{18,... | collective-permute-start | bytes 3145736 | tf_op jit(solution)/shard_map/ppermute | solution.py:549
  302.6 16.8 %collective-permute-start.20 = (f32[256,1024]{1,0:T(8,128)S(1)}, f32[256,1024]{1,0:T(8,128)S(1)}, u32[]{:S(2)}, u32[]{:S(2)}) collective-permute-start(f32[256,1024]{1,0:T(8,128)S(1)} %get-tuple-element.112), channel_id=1, source_target_pairs={{0,6},{2,0},{4,14},{6,4},{8,2},{10,8},{12,22},{14,12},{16,10},{18,... | collective-permute-start | bytes 3145736 | tf_op jit(solution)/shard_map/ppermute | solution.py:550
  313.7 14.1 %collective-permute-start.21 = (f32[256,1024]{1,0:T(8,128)S(1)}, f32[256,1024]{1,0:T(8,128)S(1)}, u32[]{:S(2)}, u32[]{:S(2)}) collective-permute-start(f32[256,1024]{1,0:T(8,128)S(1)} %get-tuple-element.114), channel_id=1, source_target_pairs={{0,2},{2,8},{4,6},{6,0},{8,10},{10,16},{12,14},{14,4},{16,18},{18,... | collective-permute-start | bytes 3145736 | tf_op jit(solution)/shard_map/ppermute | solution.py:549
  313.8 16.8 %collective-permute-start.22 = (f32[256,1024]{1,0:T(8,128)S(1)}, f32[256,1024]{1,0:T(8,128)S(1)}, u32[]{:S(2)}, u32[]{:S(2)}) collective-permute-start(f32[256,1024]{1,0:T(8,128)S(1)} %get-tuple-element.115), channel_id=1, source_target_pairs={{0,6},{2,0},{4,14},{6,4},{8,2},{10,8},{12,22},{14,12},{16,10},{18,... | collective-permute-start | bytes 3145736 | tf_op jit(solution)/shard_map/ppermute | solution.py:550
  325.0 14.1 %collective-permute-start.23 = (f32[256,1024]{1,0:T(8,128)S(1)}, f32[256,1024]{1,0:T(8,128)S(1)}, u32[]{:S(2)}, u32[]{:S(2)}) collective-permute-start(f32[256,1024]{1,0:T(8,128)S(1)} %get-tuple-element.117), channel_id=1, source_target_pairs={{0,2},{2,8},{4,6},{6,0},{8,10},{10,16},{12,14},{14,4},{16,18},{18,... | collective-permute-start | bytes 3145736 | tf_op jit(solution)/shard_map/ppermute | solution.py:549
  325.0 16.8 %collective-permute-start.24 = (f32[256,1024]{1,0:T(8,128)S(1)}, f32[256,1024]{1,0:T(8,128)S(1)}, u32[]{:S(2)}, u32[]{:S(2)}) collective-permute-start(f32[256,1024]{1,0:T(8,128)S(1)} %get-tuple-element.118), channel_id=1, source_target_pairs={{0,6},{2,0},{4,14},{6,4},{8,2},{10,8},{12,22},{14,12},{16,10},{18,... | collective-permute-start | bytes 3145736 | tf_op jit(solution)/shard_map/ppermute | solution.py:550
  336.2 14.1 %collective-permute-start.25 = (f32[256,1024]{1,0:T(8,128)S(1)}, f32[256,1024]{1,0:T(8,128)S(1)}, u32[]{:S(2)}, u32[]{:S(2)}) collective-permute-start(f32[256,1024]{1,0:T(8,128)S(1)} %get-tuple-element.120), channel_id=1, source_target_pairs={{0,2},{2,8},{4,6},{6,0},{8,10},{10,16},{12,14},{14,4},{16,18},{18,... | collective-permute-start | bytes 3145736 | tf_op jit(solution)/shard_map/ppermute | solution.py:549
  336.3 16.8 %collective-permute-start.26 = (f32[256,1024]{1,0:T(8,128)S(1)}, f32[256,1024]{1,0:T(8,128)S(1)}, u32[]{:S(2)}, u32[]{:S(2)}) collective-permute-start(f32[256,1024]{1,0:T(8,128)S(1)} %get-tuple-element.121), channel_id=1, source_target_pairs={{0,6},{2,0},{4,14},{6,4},{8,2},{10,8},{12,22},{14,12},{16,10},{18,... | collective-permute-start | bytes 3145736 | tf_op jit(solution)/shard_map/ppermute | solution.py:550
  347.4 14.1 %collective-permute-start.27 = (f32[256,1024]{1,0:T(8,128)S(1)}, f32[256,1024]{1,0:T(8,128)S(1)}, u32[]{:S(2)}, u32[]{:S(2)}) collective-permute-start(f32[256,1024]{1,0:T(8,128)S(1)} %get-tuple-element.123), channel_id=1, source_target_pairs={{0,2},{2,8},{4,6},{6,0},{8,10},{10,16},{12,14},{14,4},{16,18},{18,... | collective-permute-start | bytes 3145736 | tf_op jit(solution)/shard_map/ppermute | solution.py:549
  347.5 16.8 %collective-permute-start.28 = (f32[256,1024]{1,0:T(8,128)S(1)}, f32[256,1024]{1,0:T(8,128)S(1)}, u32[]{:S(2)}, u32[]{:S(2)}) collective-permute-start(f32[256,1024]{1,0:T(8,128)S(1)} %get-tuple-element.124), channel_id=1, source_target_pairs={{0,6},{2,0},{4,14},{6,4},{8,2},{10,8},{12,22},{14,12},{16,10},{18,... | collective-permute-start | bytes 3145736 | tf_op jit(solution)/shard_map/ppermute | solution.py:550
  358.7 14.1 %collective-permute-start.29 = (f32[256,1024]{1,0:T(8,128)S(1)}, f32[256,1024]{1,0:T(8,128)S(1)}, u32[]{:S(2)}, u32[]{:S(2)}) collective-permute-start(f32[256,1024]{1,0:T(8,128)S(1)} %get-tuple-element.126), channel_id=1, source_target_pairs={{0,2},{2,8},{4,6},{6,0},{8,10},{10,16},{12,14},{14,4},{16,18},{18,... | collective-permute-start | bytes 3145736 | tf_op jit(solution)/shard_map/ppermute | solution.py:549
  358.7 16.9 %collective-permute-start.30 = (f32[256,1024]{1,0:T(8,128)S(1)}, f32[256,1024]{1,0:T(8,128)S(1)}, u32[]{:S(2)}, u32[]{:S(2)}) collective-permute-start(f32[256,1024]{1,0:T(8,128)S(1)} %get-tuple-element.127), channel_id=1, source_target_pairs={{0,6},{2,0},{4,14},{6,4},{8,2},{10,8},{12,22},{14,12},{16,10},{18,... | collective-permute-start | bytes 3145736 | tf_op jit(solution)/shard_map/ppermute | solution.py:550
  370.5 15.1 %collective-permute-start.32 = (f32[256,1024]{1,0:T(8,128)}, f32[256,1024]{1,0:T(8,128)}, u32[]{:S(2)}, u32[]{:S(2)}) collective-permute-start(f32[256,1024]{1,0:T(8,128)} %get-tuple-element.130), channel_id=1, source_target_pairs={{0,2},{2,8},{4,6},{6,0},{8,10},{10,16},{12,14},{14,4},{16,18},{18,... | collective-permute-start | bytes 3145736 | tf_op jit(solution)/shard_map/ppermute | solution.py:549
  370.6 16.2 %collective-permute-start.33 = (f32[256,1024]{1,0:T(8,128)}, f32[256,1024]{1,0:T(8,128)}, u32[]{:S(2)}, u32[]{:S(2)}) collective-permute-start(f32[256,1024]{1,0:T(8,128)} %get-tuple-element.131), channel_id=1, source_target_pairs={{0,6},{2,0},{4,14},{6,4},{8,2},{10,8},{12,22},{14,12},{16,10},{18,... | collective-permute-start | bytes 3145736 | tf_op jit(solution)/shard_map/ppermute | solution.py:550
  382.0 13.3 %collective-permute-start.34 = (f32[256,1024]{1,0:T(8,128)}, f32[256,1024]{1,0:T(8,128)S(1)}, u32[]{:S(2)}, u32[]{:S(2)}) collective-permute-start(f32[256,1024]{1,0:T(8,128)} %get-tuple-element.134), channel_id=1, source_target_pairs={{0,2},{2,8},{4,6},{6,0},{8,10},{10,16},{12,14},{14,4},{16,18},{18,... | collective-permute-start | bytes 3145736 | tf_op jit(solution)/shard_map/ppermute | solution.py:549
  382.0 15.8 %collective-permute-start.35 = (f32[256,1024]{1,0:T(8,128)}, f32[256,1024]{1,0:T(8,128)}, u32[]{:S(2)}, u32[]{:S(2)}) collective-permute-start(f32[256,1024]{1,0:T(8,128)} %get-tuple-element.135), channel_id=1, source_target_pairs={{0,6},{2,0},{4,14},{6,4},{8,2},{10,8},{12,22},{14,12},{16,10},{18,... | collective-permute-start | bytes 3145736 | tf_op jit(solution)/shard_map/ppermute | solution.py:550
  382.5 4.3 %copy-start.10 = (f32[2048]{0:T(1024)S(1)}, f32[2048]{0:T(1024)}, u32[]{:S(2)}) copy-start(f32[2048]{0:T(1024)} %param.12) | copy-start | bytes 24580
  382.5 7.4 %collective-permute-start.31 = (f32[192,256]{1,0:T(8,128)S(1)}, f32[192,256]{1,0:T(8,128)S(1)}, u32[]{:S(2)}, u32[]{:S(2)}) collective-permute-start(f32[192,256]{1,0:T(8,128)S(1)} %get-tuple-element.128.here), channel_id=1, source_target_pairs={{0,1},{1,0},{2,3},{3,2},{4,5},{5,4},{6,7},{7,6},{8,9},{9,8},{10,11... | collective-permute-start | bytes 589832 | tf_op jit(solution)/shard_map/ppermute | solution.py:414
  386.8 3.2 copy-start.14
  386.8 3.3 copy-start.3
  390.0 0.7 copy-start.11
  390.9 0.7 copy-start.8
  395.3 1.0 copy-start.6
  397.8 4.2 %copy-start.1 = (f32[1024,256]{1,0:T(8,128)S(1)}, f32[1024,256]{1,0:T(8,128)}, u32[]{:S(2)}) copy-start(f32[1024,256]{1,0:T(8,128)} %param.7) | copy-start | bytes 3145732
  397.8 1.3 copy-start.7
Sparse Core Ops, SparseCore 0:
  11.3 183.2 all-gather.1

commit v5 on v4

--- a/solution.py
+++ b/solution.py
@@ -260,8 +260,8 @@
         out_shape=[shape, shape],
         scratch_shapes=[
             pltpu.VMEM((count, block, depth), F32),
-            pltpu.VMEM((512, tokens), F32),
-            pltpu.VMEM((512, tokens), F32),
+            pltpu.VMEM((256, tokens), F32),
+            pltpu.VMEM((256, tokens), F32),
             pltpu.SemaphoreType.DMA((count,)),
         ],
         compiler_params=params(STREAM_LIMIT),
@@ -383,7 +383,7 @@
             jax.ShapeDtypeStruct((1, 2 * width), F32),
         ],
         input_output_aliases={5 + i: i for i in range(len(done))},
-        compiler_params=params(),
+        compiler_params=params(VMEM_LIMIT // 2),
         name="proto_grads",
     )(turned, gain_row, *parts, *done)
 
@@ -401,7 +401,7 @@
         in_specs=[vmem] * 4 + [pl.BlockSpec(memory_space=pl.ANY)],
         out_specs=vmem,
         out_shape=jax.ShapeDtypeStruct(unit.shape, F32),
-        compiler_params=params(),
+        compiler_params=params(VMEM_LIMIT // 2),
         name="token_grads",
     )(here, there, unit, inverse, after)
 

time: 415 us -> 415 us (level)
  no operation moved by 1% of the time
where the time goes in v5:
time: 415 us; the launch traced here: 409 us
  Pallas kernels  179 us (43%)
  waiting for transfers between devices  130 us (31%)
  starting transfers between devices  49.1 us (12%)
  blocking collectives  16.8 us (4%)
  between operations  15.2 us (4%)
  local copies, waits for them, and re-layouts  13.8 us (3%)
  other arithmetic  5.33 us (1%)
    pallas_call x18, Pallas kernels, grad_step(): pl.pallas_call(lambda *refs: grad_kernel(*refs, blocks=blocks, arrivals=l...  94.8 us
    ppermute x14, waiting for transfers between devices, body(): lax.ppermute(second, 'dp', behind)  32.9 us
    all_to_all x3, waiting for transfers between devices, column_total(): lax.all_to_all(jnp.broadcast_to(mine, x.shape), 'dp', 0, 0, tiled=True)  26.5 us
    ppermute x14, waiting for transfers between devices, body(): lax.ppermute(first, 'dp', ahead)  25.2 us
    pallas_call x3, Pallas kernels, column_pass(): pl.pallas_call(lambda *refs: column_kernel(*refs, unroll=min(16, shard //...  24 us
    pallas_call x3, Pallas kernels, row_pass(): pl.pallas_call(lambda *refs: row_kernel(*refs, unroll=min(16, block // LA...  21.5 us
    pallas_call x1, Pallas kernels, student_pass(): pl.pallas_call(student_kernel, in_specs=[vmem, pl.BlockSpec(memory_space=...  19.1 us
    all_gather x1, waiting for transfers between devices, body(): gathered = lax.all_gather(weights, 'dp', axis=0, tiled=True)  18.4 us
  transfers between devices with their start and end apart: 42, of which 36 were waited for; matrix products, arithmetic and copies ran while one was open for 3% of the time, Pallas kernels for 37%

profile of v5, /device:TPU:1, one launch (start us, length us, event | category | flops | bytes accessed | tf_op | source)
XLA Modules:
  0.0 408.8 jit_solution(12403018887544232840)
XLA Ops:
  11.2 13.0 %teacher_stats.1 = (f32[192,128]{1,0:T(8,128)S(1)}, f32[192,128]{1,0:T(8,128)S(1)}) custom-call(bf16[192,32768]{1,0:T(8,128)(2,1)} %refs_7_.27), custom_call_target="tpu_custom_call" | custom-call | tf_op jit(solution)/shard_map/teacher_stats/pallas_call | solution.py:97
  24.4 2.1 collective-permute-start.1
  28.4 6.4 %column_sums.3 = (f32[16,1,2048]{2,1,0:T(1,128)S(1)}, f32[192,128]{1,0:T(8,128)S(1)}) custom-call(bf16[192,32768]{1,0:T(8,128)(2,1)} %refs_7_.27, f32[192,128]{1,0:T(8,128)S(1)} %broadcast_in_dim.98.refs_1_, f32[192,128]{1,0:T(8,128)S(1)} %iota.17.refs_2_, f32[192,128]{1,0:T(8,128)S(1)} %broadcast_in_dim.101.refs_3_), custom_call_target="tpu_custom_call" | custom-call | tf_op jit(solution)/shard_map/column_sums/pallas_call | solution.py:142
  34.9 16.8 %all_to_all.30 = f32[16,1,2048]{2,1,0:T(1,128)S(1)} all-to-all(f32[16,1,2048]{2,1,0:T(1,128)S(1)} %get-tuple-element.76), channel_id=1, replica_groups=mesh['dp'=16,'proto'=2] {'dp'}, dimensions={0} | all-to-all | bytes 262144 | tf_op jit(solution)/shard_map/all_to_all | solution.py:425
  52.5 4.5 %all-to-all-start.1 = ((f32[16,1,2048]{2,1,0:T(1,128)}), f32[16,1,2048]{2,1,0:T(1,128)S(1)}, u32[]{:S(2)}, u32[]{:S(2)}) async-start(f32[16,1,2048]{2,1,0:T(1,128)} %broadcast_in_dim.102), calls=%async_computation.1 | async-start | bytes 262144 | tf_op jit(solution)/shard_map/all_to_all | solution.py:426
  57.0 9.3 %all-to-all-done.1.refs_2_ = f32[16,1,2048]{2,1,0:T(1,128)S(1)} async-done(((f32[16,1,2048]{2,1,0:T(1,128)}), f32[16,1,2048]{2,1,0:T(1,128)S(1)}, u32[]{:S(2)}, u32[]{:S(2)}) %all-to-all-start.1) | async-done | bytes 131104 | tf_op jit(solution)/shard_map/all_to_all | solution.py:426
  66.4 7.3 %row_sums.3 = (f32[192,128]{1,0:T(8,128)S(1)}, f32[1,32768]{1,0:T(1,128)}) custom-call(bf16[192,32768]{1,0:T(8,128)(2,1)} %refs_7_.27, f32[192,128]{1,0:T(8,128)S(1)} %get-tuple-element.75.refs_1_, f32[16,1,2048]{2,1,0:T(1,128)S(1)} %all-to-all-done.1.refs_2_), custom_call_target="tpu_custom_call" | custom-call | tf_op jit(solution)/shard_map/row_sums/pallas_call | solution.py:190
  75.1 2.5 collective-permute-done.2.refs_3_
  77.6 8.8 %column_sums.4 = (f32[16,1,2048]{2,1,0:T(1,128)}, f32[192,128]{1,0:T(8,128)S(1)}) custom-call(bf16[192,32768]{1,0:T(8,128)(2,1)} %refs_7_.27, f32[192,128]{1,0:T(8,128)S(1)} %get-tuple-element.75.refs_1_, f32[192,128]{1,0:T(8,128)S(1)} %get-tuple-element.77.refs_2_, f32[192,128]{1,0:T(8,128)S(1)} %collective-permute-done.2.refs_3_), custom_call_target="tpu_custom_call" | custom-call | tf_op jit(solution)/shard_map/column_sums/pallas_call | solution.py:142
  86.4 5.3 %all-to-all-start.2 = ((f32[16,1,2048]{2,1,0:T(1,128)}), f32[16,1,2048]{2,1,0:T(1,128)S(1)}, u32[]{:S(2)}, u32[]{:S(2)}) async-start(f32[16,1,2048]{2,1,0:T(1,128)} %get-tuple-element.79), calls=%async_computation.2 | async-start | bytes 262144 | tf_op jit(solution)/shard_map/all_to_all | solution.py:425
  93.1 7.9 %all-to-all-done.2 = f32[16,1,2048]{2,1,0:T(1,128)S(1)} async-done(((f32[16,1,2048]{2,1,0:T(1,128)}), f32[16,1,2048]{2,1,0:T(1,128)S(1)}, u32[]{:S(2)}, u32[]{:S(2)}) %all-to-all-start.2) | async-done | bytes 131104 | tf_op jit(solution)/shard_map/all_to_all | solution.py:425
  101.8 4.5 %all-to-all-start.3 = ((f32[16,1,2048]{2,1,0:T(1,128)}), f32[16,1,2048]{2,1,0:T(1,128)S(1)}, u32[]{:S(2)}, u32[]{:S(2)}) async-start(f32[16,1,2048]{2,1,0:T(1,128)} %broadcast_in_dim.103), calls=%async_computation.3 | async-start | bytes 262144 | tf_op jit(solution)/shard_map/all_to_all | solution.py:426
  106.5 9.1 %all-to-all-done.3.refs_2_ = f32[16,1,2048]{2,1,0:T(1,128)S(1)} async-done(((f32[16,1,2048]{2,1,0:T(1,128)}), f32[16,1,2048]{2,1,0:T(1,128)S(1)}, u32[]{:S(2)}, u32[]{:S(2)}) %all-to-all-start.3) | async-done | bytes 131104 | tf_op jit(solution)/shard_map/all_to_all | solution.py:426
  115.7 7.3 %row_sums.4 = (f32[192,128]{1,0:T(8,128)S(1)}, f32[1,32768]{1,0:T(1,128)}) custom-call(bf16[192,32768]{1,0:T(8,128)(2,1)} %refs_7_.27, f32[192,128]{1,0:T(8,128)S(1)} %get-tuple-element.78.refs_1_, f32[16,1,2048]{2,1,0:T(1,128)S(1)} %all-to-all-done.3.refs_2_), custom_call_target="tpu_custom_call" | custom-call | tf_op jit(solution)/shard_map/row_sums/pallas_call | solution.py:190
  124.3 2.5 collective-permute-done.3.refs_3_
  126.9 8.8 %column_sums.5 = (f32[16,1,2048]{2,1,0:T(1,128)}, f32[192,128]{1,0:T(8,128)S(1)}) custom-call(bf16[192,32768]{1,0:T(8,128)(2,1)} %refs_7_.27, f32[192,128]{1,0:T(8,128)S(1)} %get-tuple-element.78.refs_1_, f32[192,128]{1,0:T(8,128)S(1)} %get-tuple-element.80.refs_2_, f32[192,128]{1,0:T(8,128)S(1)} %collective-permute-done.3.refs_3_), custom_call_target="tpu_custom_call" | custom-call | tf_op jit(solution)/shard_map/column_sums/pallas_call | solution.py:142
  135.7 5.3 %all-to-all-start.4 = ((f32[16,1,2048]{2,1,0:T(1,128)}), f32[16,1,2048]{2,1,0:T(1,128)S(1)}, u32[]{:S(2)}, u32[]{:S(2)}) async-start(f32[16,1,2048]{2,1,0:T(1,128)} %get-tuple-element.82), calls=%async_computation.4 | async-start | bytes 262144 | tf_op jit(solution)/shard_map/all_to_all | solution.py:425
  141.0 9.3 %all-to-all-done.4 = f32[16,1,2048]{2,1,0:T(1,128)S(1)} async-done(((f32[16,1,2048]{2,1,0:T(1,128)}), f32[16,1,2048]{2,1,0:T(1,128)S(1)}, u32[]{:S(2)}, u32[]{:S(2)}) %all-to-all-start.4) | async-done | bytes 131104 | tf_op jit(solution)/shard_map/all_to_all | solution.py:425
  151.1 4.8 %all-to-all-start.5 = ((f32[16,1,2048]{2,1,0:T(1,128)}), f32[16,1,2048]{2,1,0:T(1,128)S(1)}, u32[]{:S(2)}, u32[]{:S(2)}) async-start(f32[16,1,2048]{2,1,0:T(1,128)} %broadcast_in_dim.104), calls=%async_computation.5 | async-start | bytes 262144 | tf_op jit(solution)/shard_map/all_to_all | solution.py:426
  157.1 8.1 %all-to-all-done.5.refs_2_ = f32[16,1,2048]{2,1,0:T(1,128)S(1)} async-done(((f32[16,1,2048]{2,1,0:T(1,128)}), f32[16,1,2048]{2,1,0:T(1,128)S(1)}, u32[]{:S(2)}, u32[]{:S(2)}) %all-to-all-start.5) | async-done | bytes 131104 | tf_op jit(solution)/shard_map/all_to_all | solution.py:426
  165.2 7.0 %row_sums.5 = (f32[192,128]{1,0:T(8,128)S(1)}, f32[1,32768]{1,0:T(1,128)S(1)}) custom-call(bf16[192,32768]{1,0:T(8,128)(2,1)} %refs_7_.27, f32[192,128]{1,0:T(8,128)S(1)} %get-tuple-element.81.refs_1_, f32[16,1,2048]{2,1,0:T(1,128)S(1)} %all-to-all-done.5.refs_2_), custom_call_target="tpu_custom_call" | custom-call | tf_op jit(solution)/shard_map/row_sums/pallas_call | solution.py:190
  173.7 2.4 collective-permute-done.4
  176.2 18.4 %all-gather.2.cloned.1.call-done.w_hbm.refs_8_.refs_10_.refs_11_ = f32[32768,256]{1,0:T(8,128)} async-done(((f32[2048,256]{1,0:T(8,128)}), f32[32768,256]{1,0:T(8,128)}) %all-gather.2.cloned.1.call-update) | async-done | bytes 33554448 | tf_op jit(solution)/shard_map/all_gather | solution.py:487
  194.6 19.1 %student_stats.1 = (f32[8,192]{1,0:T(8,128)S(1)}, f32[8,192]{1,0:T(8,128)S(1)}) custom-call(bf16[768,192]{1,0:T(8,128)(2,1)S(1)} %copy.80.u_ref, f32[32768,256]{1,0:T(8,128)} %all-gather.2.cloned.1.call-done.w_hbm.refs_8_.refs_10_.refs_11_), custom_call_target="tpu_custom_call" | custom-call | tf_op jit(solution)/shard_map/student_stats/pallas_call | solution.py:256
  216.4 3.7 grad_blocks.18
  221.6 3.7 grad_blocks.19
  225.4 5.6 %grad_blocks.20 = (f32[256,1024]{1,0:T(8,128)S(1)}, f32[256,1024]{1,0:T(8,128)S(1)}, f32[192,256]{1,0:T(8,128)S(1)}) custom-call(s32[33]{0:T(128)S(1)} %dynamic-slice_bitcast_fusion.refs_0_, bf16[192,768]{1,0:T(8,128)(2,1)S(1)} %get-tuple-element.144.refs_1_, bf16[256,576]{1,0:T(8,128)(2,1)S(1)} %copy.102.refs_2_, f32[192,128]{1,0:T(8,128)S(1)} %broadcast_in_dim.96.refs_3_, ...), custom_call_target="tpu_custom_call" | custom-call | tf_op jit(solution)/shard_map/grad_blocks/pallas_call | solution.py:331
  231.1 5.8 %collective-permute-start.7 = (f32[256,1024]{1,0:T(8,128)S(1)}, f32[256,1024]{1,0:T(8,128)S(1)}, u32[]{:S(2)}, u32[]{:S(2)}) collective-permute-start(f32[256,1024]{1,0:T(8,128)S(1)} %get-tuple-element.91), channel_id=1, source_target_pairs={{0,2},{2,8},{4,6},{6,0},{8,10},{10,16},{12,14},{14,4},{16,18},{18,... | collective-permute-start | bytes 3145736 | tf_op jit(solution)/shard_map/ppermute | solution.py:549
  236.9 5.6 %grad_blocks.21 = (f32[256,1024]{1,0:T(8,128)S(1)}, f32[256,1024]{1,0:T(8,128)S(1)}, f32[192,256]{1,0:T(8,128)S(1)}) custom-call(s32[33]{0:T(128)S(1)} %dynamic-slice_bitcast_fusion.refs_0_, bf16[192,768]{1,0:T(8,128)(2,1)S(1)} %get-tuple-element.144.refs_1_, bf16[256,576]{1,0:T(8,128)(2,1)S(1)} %copy.102.refs_2_, f32[192,128]{1,0:T(8,128)S(1)} %broadcast_in_dim.96.refs_3_, ...), custom_call_target="tpu_custom_call" | custom-call | tf_op jit(solution)/shard_map/grad_blocks/pallas_call | solution.py:331
  244.3 4.3 %collective-permute-done.7.refs_12_ = f32[256,1024]{1,0:T(8,128)S(1)} collective-permute-done((f32[256,1024]{1,0:T(8,128)S(1)}, f32[256,1024]{1,0:T(8,128)S(1)}, u32[]{:S(2)}, u32[]{:S(2)}) %collective-permute-start.7) | collective-permute-done | bytes 1048608 | tf_op jit(solution)/shard_map/ppermute | solution.py:549
  248.6 2.8 collective-permute-done.8.refs_13_
  251.4 5.6 %grad_blocks.22 = (f32[256,1024]{1,0:T(8,128)S(1)}, f32[256,1024]{1,0:T(8,128)S(1)}, f32[192,256]{1,0:T(8,128)S(1)}) custom-call(s32[33]{0:T(128)S(1)} %dynamic-slice_bitcast_fusion.refs_0_, bf16[192,768]{1,0:T(8,128)(2,1)S(1)} %get-tuple-element.144.refs_1_, bf16[256,576]{1,0:T(8,128)(2,1)S(1)} %copy.102.refs_2_, f32[192,128]{1,0:T(8,128)S(1)} %broadcast_in_dim.96.refs_3_, ...), custom_call_target="tpu_custom_call" | custom-call | tf_op jit(solution)/shard_map/grad_blocks/pallas_call | solution.py:331
  257.6 2.3 collective-permute-done.9.refs_12_
  259.9 2.8 collective-permute-done.10.refs_13_
  262.6 5.6 %grad_blocks.23 = (f32[256,1024]{1,0:T(8,128)S(1)}, f32[256,1024]{1,0:T(8,128)S(1)}, f32[192,256]{1,0:T(8,128)S(1)}) custom-call(s32[33]{0:T(128)S(1)} %dynamic-slice_bitcast_fusion.refs_0_, bf16[192,768]{1,0:T(8,128)(2,1)S(1)} %get-tuple-element.144.refs_1_, bf16[256,576]{1,0:T(8,128)(2,1)S(1)} %copy.102.refs_2_, f32[192,128]{1,0:T(8,128)S(1)} %broadcast_in_dim.96.refs_3_, ...), custom_call_target="tpu_custom_call" | custom-call | tf_op jit(solution)/shard_map/grad_blocks/pallas_call | solution.py:331
  269.0 3.7 grad_blocks.24
  273.9 5.6 %grad_blocks.25 = (f32[256,1024]{1,0:T(8,128)S(1)}, f32[256,1024]{1,0:T(8,128)S(1)}, f32[192,256]{1,0:T(8,128)S(1)}) custom-call(s32[33]{0:T(128)S(1)} %dynamic-slice_bitcast_fusion.refs_0_, bf16[192,768]{1,0:T(8,128)(2,1)S(1)} %get-tuple-element.144.refs_1_, bf16[256,576]{1,0:T(8,128)(2,1)S(1)} %copy.102.refs_2_, f32[192,128]{1,0:T(8,128)S(1)} %broadcast_in_dim.96.refs_3_, ...), custom_call_target="tpu_custom_call" | custom-call | tf_op jit(solution)/shard_map/grad_blocks/pallas_call | solution.py:331
  280.1 2.3 collective-permute-done.13.refs_12_
  282.3 2.8 collective-permute-done.14.refs_13_
  285.1 5.6 %grad_blocks.26 = (f32[256,1024]{1,0:T(8,128)S(1)}, f32[256,1024]{1,0:T(8,128)S(1)}, f32[192,256]{1,0:T(8,128)S(1)}) custom-call(s32[33]{0:T(128)S(1)} %dynamic-slice_bitcast_fusion.refs_0_, bf16[192,768]{1,0:T(8,128)(2,1)S(1)} %get-tuple-element.144.refs_1_, bf16[256,576]{1,0:T(8,128)(2,1)S(1)} %copy.102.refs_2_, f32[192,128]{1,0:T(8,128)S(1)} %broadcast_in_dim.96.refs_3_, ...), custom_call_target="tpu_custom_call" | custom-call | tf_op jit(solution)/shard_map/grad_blocks/pallas_call | solution.py:331
  291.3 3.7 grad_blocks.27
  296.4 5.6 %grad_blocks.28 = (f32[256,1024]{1,0:T(8,128)S(1)}, f32[256,1024]{1,0:T(8,128)S(1)}, f32[192,256]{1,0:T(8,128)S(1)}) custom-call(s32[33]{0:T(128)S(1)} %dynamic-slice_bitcast_fusion.refs_0_, bf16[192,768]{1,0:T(8,128)(2,1)S(1)} %get-tuple-element.144.refs_1_, bf16[256,576]{1,0:T(8,128)(2,1)S(1)} %copy.102.refs_2_, f32[192,128]{1,0:T(8,128)S(1)} %broadcast_in_dim.96.refs_3_, ...), custom_call_target="tpu_custom_call" | custom-call | tf_op jit(solution)/shard_map/grad_blocks/pallas_call | solution.py:331
  302.5 2.3 collective-permute-done.17.refs_12_
  304.8 2.8 collective-permute-done.18.refs_13_
  307.6 5.6 %grad_blocks.29 = (f32[256,1024]{1,0:T(8,128)S(1)}, f32[256,1024]{1,0:T(8,128)S(1)}, f32[192,256]{1,0:T(8,128)S(1)}) custom-call(s32[33]{0:T(128)S(1)} %dynamic-slice_bitcast_fusion.refs_0_, bf16[192,768]{1,0:T(8,128)(2,1)S(1)} %get-tuple-element.144.refs_1_, bf16[256,576]{1,0:T(8,128)(2,1)S(1)} %copy.102.refs_2_, f32[192,128]{1,0:T(8,128)S(1)} %broadcast_in_dim.96.refs_3_, ...), custom_call_target="tpu_custom_call" | custom-call | tf_op jit(solution)/shard_map/grad_blocks/pallas_call | solution.py:331
  313.8 2.3 collective-permute-done.19.refs_12_
  316.0 2.8 collective-permute-done.20.refs_13_
  318.8 5.6 %grad_blocks.30 = (f32[256,1024]{1,0:T(8,128)S(1)}, f32[256,1024]{1,0:T(8,128)S(1)}, f32[192,256]{1,0:T(8,128)S(1)}) custom-call(s32[33]{0:T(128)S(1)} %dynamic-slice_bitcast_fusion.refs_0_, bf16[192,768]{1,0:T(8,128)(2,1)S(1)} %get-tuple-element.144.refs_1_, bf16[256,576]{1,0:T(8,128)(2,1)S(1)} %copy.102.refs_2_, f32[192,128]{1,0:T(8,128)S(1)} %broadcast_in_dim.96.refs_3_, ...), custom_call_target="tpu_custom_call" | custom-call | tf_op jit(solution)/shard_map/grad_blocks/pallas_call | solution.py:331
  327.3 2.8 collective-permute-done.22.refs_13_
  330.1 5.6 %grad_blocks.31 = (f32[256,1024]{1,0:T(8,128)S(1)}, f32[256,1024]{1,0:T(8,128)S(1)}, f32[192,256]{1,0:T(8,128)S(1)}) custom-call(s32[33]{0:T(128)S(1)} %dynamic-slice_bitcast_fusion.refs_0_, bf16[192,768]{1,0:T(8,128)(2,1)S(1)} %get-tuple-element.144.refs_1_, bf16[256,576]{1,0:T(8,128)(2,1)S(1)} %copy.102.refs_2_, f32[192,128]{1,0:T(8,128)S(1)} %broadcast_in_dim.96.refs_3_, ...), custom_call_target="tpu_custom_call" | custom-call | tf_op jit(solution)/shard_map/grad_blocks/pallas_call | solution.py:331
  336.2 2.3 collective-permute-done.23.refs_12_
  338.5 2.8 collective-permute-done.24.refs_13_
  341.3 5.6 %grad_blocks.32 = (f32[256,1024]{1,0:T(8,128)S(1)}, f32[256,1024]{1,0:T(8,128)S(1)}, f32[192,256]{1,0:T(8,128)S(1)}) custom-call(s32[33]{0:T(128)S(1)} %dynamic-slice_bitcast_fusion.refs_0_, bf16[192,768]{1,0:T(8,128)(2,1)S(1)} %get-tuple-element.144.refs_1_, bf16[256,576]{1,0:T(8,128)(2,1)S(1)} %copy.102.refs_2_, f32[192,128]{1,0:T(8,128)S(1)} %broadcast_in_dim.96.refs_3_, ...), custom_call_target="tpu_custom_call" | custom-call | tf_op jit(solution)/shard_map/grad_blocks/pallas_call | solution.py:331
  347.5 2.3 collective-permute-done.25.refs_12_
  349.8 2.8 collective-permute-done.26.refs_13_
  352.5 5.6 %grad_blocks.33 = (f32[256,1024]{1,0:T(8,128)S(1)}, f32[256,1024]{1,0:T(8,128)S(1)}, f32[192,256]{1,0:T(8,128)S(1)}) custom-call(s32[33]{0:T(128)S(1)} %dynamic-slice_bitcast_fusion.refs_0_, bf16[192,768]{1,0:T(8,128)(2,1)S(1)} %get-tuple-element.144.refs_1_, bf16[256,576]{1,0:T(8,128)(2,1)S(1)} %copy.102.refs_2_, f32[192,128]{1,0:T(8,128)S(1)} %broadcast_in_dim.96.refs_3_, ...), custom_call_target="tpu_custom_call" | custom-call | tf_op jit(solution)/shard_map/grad_blocks/pallas_call | solution.py:331
  358.7 2.3 collective-permute-done.27.refs_12_
  361.0 2.8 collective-permute-done.28.refs_13_
  363.8 6.3 %grad_blocks.34 = (f32[256,1024]{1,0:T(8,128)}, f32[256,1024]{1,0:T(8,128)}, f32[192,256]{1,0:T(8,128)S(1)}) custom-call(s32[33]{0:T(128)S(1)} %dynamic-slice_bitcast_fusion.refs_0_, bf16[192,768]{1,0:T(8,128)(2,1)S(1)} %get-tuple-element.144.refs_1_, bf16[256,576]{1,0:T(8,128)(2,1)S(1)} %copy.102.refs_2_, f32[192,128]{1,0:T(8,128)S(1)} %broadcast_in_dim.96.refs_3_, ...), custom_call_target="tpu_custom_call" | custom-call | tf_op jit(solution)/shard_map/grad_blocks/pallas_call | solution.py:331
  372.2 2.9 collective-permute-done.30.refs_13_
  375.1 6.3 %grad_blocks.35 = (f32[256,1024]{1,0:T(8,128)}, f32[256,1024]{1,0:T(8,128)}, f32[192,256]{1,0:T(8,128)S(1)}) custom-call(s32[33]{0:T(128)S(1)} %dynamic-slice_bitcast_fusion.refs_0_, bf16[192,768]{1,0:T(8,128)(2,1)S(1)} %get-tuple-element.144.refs_1_, bf16[256,576]{1,0:T(8,128)(2,1)S(1)} %copy.102.refs_2_, f32[192,128]{1,0:T(8,128)S(1)} %broadcast_in_dim.96.refs_3_, ...), custom_call_target="tpu_custom_call" | custom-call | tf_op jit(solution)/shard_map/grad_blocks/pallas_call | solution.py:331
  386.2 3.2 proto_grads.2
  391.1 2.6 scatter_custom_fusion
  398.6 2.9 proto_grads.3
  (138 shorter events, 45.8 us)
Async XLA Ops:
  7.2 85.1 %copy-start = (f32[1024,256]{1,0:T(8,128)S(1)}, f32[1024,256]{1,0:T(8,128)}, u32[]{:S(2)}) copy-start(f32[1024,256]{1,0:T(8,128)} %param.7) | copy-start | bytes 3145732
  7.2 2.3 copy-start.12
  7.2 2.2 copy-start.9
  7.2 187.4 %all-gather.2.cloned.1.call-start = ((), (), s32[]{:S(2)}) async-start(), calls=%async_computation.6 | async-start | bytes 35651584 | tf_op jit(solution)/shard_map/all_gather | solution.py:487
  24.4 3.5 collective-permute-start.1
  52.5 13.9 %all-to-all-start.1 = ((f32[16,1,2048]{2,1,0:T(1,128)}), f32[16,1,2048]{2,1,0:T(1,128)S(1)}, u32[]{:S(2)}, u32[]{:S(2)}) async-start(f32[16,1,2048]{2,1,0:T(1,128)} %broadcast_in_dim.102), calls=%async_computation.1 | async-start | bytes 262144 | tf_op jit(solution)/shard_map/all_to_all | solution.py:426
  66.4 8.6 %copy-start.17 = (s32[3]{0:T(128)S(1)}, s32[3]{0:T(128)}, u32[]{:S(2)}) copy-start(s32[3]{0:T(128)} %param.8) | copy-start | bytes 40
  73.7 3.9 collective-permute-start.2
  75.0 16.6 %copy-start.16 = (s32[192]{0:T(256)S(1)}, s32[192]{0:T(256)}, u32[]{:S(2)}) copy-start(s32[192]{0:T(256)} %param.9) | copy-start | bytes 2308
  86.4 14.6 %all-to-all-start.2 = ((f32[16,1,2048]{2,1,0:T(1,128)}), f32[16,1,2048]{2,1,0:T(1,128)S(1)}, u32[]{:S(2)}, u32[]{:S(2)}) async-start(f32[16,1,2048]{2,1,0:T(1,128)} %get-tuple-element.79), calls=%async_computation.2 | async-start | bytes 262144 | tf_op jit(solution)/shard_map/all_to_all | solution.py:425
  91.7 0.6 copy-start.15
  101.8 13.9 %all-to-all-start.3 = ((f32[16,1,2048]{2,1,0:T(1,128)}), f32[16,1,2048]{2,1,0:T(1,128)S(1)}, u32[]{:S(2)}, u32[]{:S(2)}) async-start(f32[16,1,2048]{2,1,0:T(1,128)} %broadcast_in_dim.103), calls=%async_computation.3 | async-start | bytes 262144 | tf_op jit(solution)/shard_map/all_to_all | solution.py:426
  106.5 17.7 %copy-start.13 = (f32[192]{0:T(256)}, f32[192]{0:T(256)S(1)}, u32[]{:S(2)}) copy-start(f32[192]{0:T(256)S(1)} %add_rsqrt_fusion) | copy-start | bytes 2308
  122.9 3.9 collective-permute-start.3
  124.3 16.7 %copy-start.2 = (f32[192,256]{1,0:T(8,128)}, f32[192,256]{1,0:T(8,128)S(1)}, u32[]{:S(2)}) copy-start(f32[192,256]{1,0:T(8,128)S(1)} %get-tuple-element.140.unit) | copy-start | bytes 589828
  135.7 14.6 %all-to-all-start.4 = ((f32[16,1,2048]{2,1,0:T(1,128)}), f32[16,1,2048]{2,1,0:T(1,128)S(1)}, u32[]{:S(2)}, u32[]{:S(2)}) async-start(f32[16,1,2048]{2,1,0:T(1,128)} %get-tuple-element.82), calls=%async_computation.4 | async-start | bytes 262144 | tf_op jit(solution)/shard_map/all_to_all | solution.py:425
  151.1 14.0 %all-to-all-start.5 = ((f32[16,1,2048]{2,1,0:T(1,128)}), f32[16,1,2048]{2,1,0:T(1,128)S(1)}, u32[]{:S(2)}, u32[]{:S(2)}) async-start(f32[16,1,2048]{2,1,0:T(1,128)} %broadcast_in_dim.104), calls=%async_computation.5 | async-start | bytes 262144 | tf_op jit(solution)/shard_map/all_to_all | solution.py:426
  172.1 3.9 collective-permute-start.4
  213.7 2.5 collective-permute-start
  220.1 5.3 %collective-permute-start.5 = (f32[256,1024]{1,0:T(8,128)S(1)}, f32[256,1024]{1,0:T(8,128)S(1)}, u32[]{:S(2)}, u32[]{:S(2)}) collective-permute-start(f32[256,1024]{1,0:T(8,128)S(1)} %get-tuple-element.87), channel_id=1, source_target_pairs={{0,2},{2,0},{4,6},{6,4},{8,10},{10,8},{12,14},{14,12},{16,18},{18,... | collective-permute-start | bytes 3145736 | tf_op jit(solution)/shard_map/ppermute | solution.py:414
  225.3 11.6 %collective-permute-start.6 = (f32[256,1024]{1,0:T(8,128)S(1)}, f32[256,1024]{1,0:T(8,128)S(1)}, u32[]{:S(2)}, u32[]{:S(2)}) collective-permute-start(f32[256,1024]{1,0:T(8,128)S(1)} %get-tuple-element.89), channel_id=1, source_target_pairs={{0,2},{2,0},{4,6},{6,4},{8,10},{10,8},{12,14},{14,12},{16,18},{18,... | collective-permute-start | bytes 3145736 | tf_op jit(solution)/shard_map/ppermute | solution.py:414
  231.1 17.6 %collective-permute-start.7 = (f32[256,1024]{1,0:T(8,128)S(1)}, f32[256,1024]{1,0:T(8,128)S(1)}, u32[]{:S(2)}, u32[]{:S(2)}) collective-permute-start(f32[256,1024]{1,0:T(8,128)S(1)} %get-tuple-element.91), channel_id=1, source_target_pairs={{0,2},{2,8},{4,6},{6,0},{8,10},{10,16},{12,14},{14,4},{16,18},{18,... | collective-permute-start | bytes 3145736 | tf_op jit(solution)/shard_map/ppermute | solution.py:549
  236.9 14.5 %collective-permute-start.8 = (f32[256,1024]{1,0:T(8,128)S(1)}, f32[256,1024]{1,0:T(8,128)S(1)}, u32[]{:S(2)}, u32[]{:S(2)}) collective-permute-start(f32[256,1024]{1,0:T(8,128)S(1)} %get-tuple-element.92), channel_id=1, source_target_pairs={{0,6},{2,0},{4,14},{6,4},{8,2},{10,8},{12,22},{14,12},{16,10},{18,... | collective-permute-start | bytes 3145736 | tf_op jit(solution)/shard_map/ppermute | solution.py:550
  242.5 17.4 %collective-permute-start.9 = (f32[256,1024]{1,0:T(8,128)S(1)}, f32[256,1024]{1,0:T(8,128)S(1)}, u32[]{:S(2)}, u32[]{:S(2)}) collective-permute-start(f32[256,1024]{1,0:T(8,128)S(1)} %get-tuple-element.94), channel_id=1, source_target_pairs={{0,2},{2,8},{4,6},{6,0},{8,10},{10,16},{12,14},{14,4},{16,18},{18,... | collective-permute-start | bytes 3145736 | tf_op jit(solution)/shard_map/ppermute | solution.py:549
  244.3 18.3 %collective-permute-start.10 = (f32[256,1024]{1,0:T(8,128)S(1)}, f32[256,1024]{1,0:T(8,128)S(1)}, u32[]{:S(2)}, u32[]{:S(2)}) collective-permute-start(f32[256,1024]{1,0:T(8,128)S(1)} %get-tuple-element.95), channel_id=1, source_target_pairs={{0,6},{2,0},{4,14},{6,4},{8,2},{10,8},{12,22},{14,12},{16,10},{18,... | collective-permute-start | bytes 3145736 | tf_op jit(solution)/shard_map/ppermute | solution.py:550
  257.0 15.8 %collective-permute-start.11 = (f32[256,1024]{1,0:T(8,128)S(1)}, f32[256,1024]{1,0:T(8,128)S(1)}, u32[]{:S(2)}, u32[]{:S(2)}) collective-permute-start(f32[256,1024]{1,0:T(8,128)S(1)} %get-tuple-element.98), channel_id=1, source_target_pairs={{0,2},{2,8},{4,6},{6,0},{8,10},{10,16},{12,14},{14,4},{16,18},{18,... | collective-permute-start | bytes 3145736 | tf_op jit(solution)/shard_map/ppermute | solution.py:549
  257.1 16.8 %collective-permute-start.12 = (f32[256,1024]{1,0:T(8,128)S(1)}, f32[256,1024]{1,0:T(8,128)S(1)}, u32[]{:S(2)}, u32[]{:S(2)}) collective-permute-start(f32[256,1024]{1,0:T(8,128)S(1)} %get-tuple-element.99), channel_id=1, source_target_pairs={{0,6},{2,0},{4,14},{6,4},{8,2},{10,8},{12,22},{14,12},{16,10},{18,... | collective-permute-start | bytes 3145736 | tf_op jit(solution)/shard_map/ppermute | solution.py:550
  268.3 14.1 %collective-permute-start.13 = (f32[256,1024]{1,0:T(8,128)S(1)}, f32[256,1024]{1,0:T(8,128)S(1)}, u32[]{:S(2)}, u32[]{:S(2)}) collective-permute-start(f32[256,1024]{1,0:T(8,128)S(1)} %get-tuple-element.101), channel_id=1, source_target_pairs={{0,2},{2,8},{4,6},{6,0},{8,10},{10,16},{12,14},{14,4},{16,18},{18,... | collective-permute-start | bytes 3145736 | tf_op jit(solution)/shard_map/ppermute | solution.py:549
  268.3 16.8 %collective-permute-start.14 = (f32[256,1024]{1,0:T(8,128)S(1)}, f32[256,1024]{1,0:T(8,128)S(1)}, u32[]{:S(2)}, u32[]{:S(2)}) collective-permute-start(f32[256,1024]{1,0:T(8,128)S(1)} %get-tuple-element.102), channel_id=1, source_target_pairs={{0,6},{2,0},{4,14},{6,4},{8,2},{10,8},{12,22},{14,12},{16,10},{18,... | collective-permute-start | bytes 3145736 | tf_op jit(solution)/shard_map/ppermute | solution.py:550
  272.8 6.7 %copy-start.4 = (f32[256,1024]{1,0:T(8,128)}, f32[256,1024]{1,0:T(8,128)S(1)}, u32[]{:S(2)}) copy-start(f32[256,1024]{1,0:T(8,128)S(1)} %get-tuple-element.129.a) | copy-start | bytes 3145732
  279.5 15.5 %collective-permute-start.15 = (f32[256,1024]{1,0:T(8,128)S(1)}, f32[256,1024]{1,0:T(8,128)S(1)}, u32[]{:S(2)}, u32[]{:S(2)}) collective-permute-start(f32[256,1024]{1,0:T(8,128)S(1)} %get-tuple-element.105), channel_id=1, source_target_pairs={{0,2},{2,8},{4,6},{6,0},{8,10},{10,16},{12,14},{14,4},{16,18},{18,... | collective-permute-start | bytes 3145736 | tf_op jit(solution)/shard_map/ppermute | solution.py:549
  279.8 16.6 %collective-permute-start.16 = (f32[256,1024]{1,0:T(8,128)S(1)}, f32[256,1024]{1,0:T(8,128)S(1)}, u32[]{:S(2)}, u32[]{:S(2)}) collective-permute-start(f32[256,1024]{1,0:T(8,128)S(1)} %get-tuple-element.106), channel_id=1, source_target_pairs={{0,6},{2,0},{4,14},{6,4},{8,2},{10,8},{12,22},{14,12},{16,10},{18,... | collective-permute-start | bytes 3145736 | tf_op jit(solution)/shard_map/ppermute | solution.py:550
  290.7 14.1 %collective-permute-start.17 = (f32[256,1024]{1,0:T(8,128)S(1)}, f32[256,1024]{1,0:T(8,128)S(1)}, u32[]{:S(2)}, u32[]{:S(2)}) collective-permute-start(f32[256,1024]{1,0:T(8,128)S(1)} %get-tuple-element.108), channel_id=1, source_target_pairs={{0,2},{2,8},{4,6},{6,0},{8,10},{10,16},{12,14},{14,4},{16,18},{18,... | collective-permute-start | bytes 3145736 | tf_op jit(solution)/shard_map/ppermute | solution.py:549
  290.8 16.8 %collective-permute-start.18 = (f32[256,1024]{1,0:T(8,128)S(1)}, f32[256,1024]{1,0:T(8,128)S(1)}, u32[]{:S(2)}, u32[]{:S(2)}) collective-permute-start(f32[256,1024]{1,0:T(8,128)S(1)} %get-tuple-element.109), channel_id=1, source_target_pairs={{0,6},{2,0},{4,14},{6,4},{8,2},{10,8},{12,22},{14,12},{16,10},{18,... | collective-permute-start | bytes 3145736 | tf_op jit(solution)/shard_map/ppermute | solution.py:550
  295.0 6.9 %copy-start.5 = (f32[256,1024]{1,0:T(8,128)}, f32[256,1024]{1,0:T(8,128)S(1)}, u32[]{:S(2)}) copy-start(f32[256,1024]{1,0:T(8,128)S(1)} %get-tuple-element.133.a) | copy-start | bytes 3145732
  302.0 14.1 %collective-permute-start.19 = (f32[256,1024]{1,0:T(8,128)S(1)}, f32[256,1024]{1,0:T(8,128)S(1)}, u32[]{:S(2)}, u32[]{:S(2)}) collective-permute-start(f32[256,1024]{1,0:T(8,128)S(1)} %get-tuple-element.111), channel_id=1, source_target_pairs={{0,2},{2,8},{4,6},{6,0},{8,10},{10,16},{12,14},{14,4},{16,18},{18,... | collective-permute-start | bytes 3145736 | tf_op jit(solution)/shard_map/ppermute | solution.py:549
  302.0 16.8 %collective-permute-start.20 = (f32[256,1024]{1,0:T(8,128)S(1)}, f32[256,1024]{1,0:T(8,128)S(1)}, u32[]{:S(2)}, u32[]{:S(2)}) collective-permute-start(f32[256,1024]{1,0:T(8,128)S(1)} %get-tuple-element.112), channel_id=1, source_target_pairs={{0,6},{2,0},{4,14},{6,4},{8,2},{10,8},{12,22},{14,12},{16,10},{18,... | collective-permute-start | bytes 3145736 | tf_op jit(solution)/shard_map/ppermute | solution.py:550
  313.2 14.1 %collective-permute-start.21 = (f32[256,1024]{1,0:T(8,128)S(1)}, f32[256,1024]{1,0:T(8,128)S(1)}, u32[]{:S(2)}, u32[]{:S(2)}) collective-permute-start(f32[256,1024]{1,0:T(8,128)S(1)} %get-tuple-element.114), channel_id=1, source_target_pairs={{0,2},{2,8},{4,6},{6,0},{8,10},{10,16},{12,14},{14,4},{16,18},{18,... | collective-permute-start | bytes 3145736 | tf_op jit(solution)/shard_map/ppermute | solution.py:549
  313.3 16.8 %collective-permute-start.22 = (f32[256,1024]{1,0:T(8,128)S(1)}, f32[256,1024]{1,0:T(8,128)S(1)}, u32[]{:S(2)}, u32[]{:S(2)}) collective-permute-start(f32[256,1024]{1,0:T(8,128)S(1)} %get-tuple-element.115), channel_id=1, source_target_pairs={{0,6},{2,0},{4,14},{6,4},{8,2},{10,8},{12,22},{14,12},{16,10},{18,... | collective-permute-start | bytes 3145736 | tf_op jit(solution)/shard_map/ppermute | solution.py:550
  324.4 14.1 %collective-permute-start.23 = (f32[256,1024]{1,0:T(8,128)S(1)}, f32[256,1024]{1,0:T(8,128)S(1)}, u32[]{:S(2)}, u32[]{:S(2)}) collective-permute-start(f32[256,1024]{1,0:T(8,128)S(1)} %get-tuple-element.117), channel_id=1, source_target_pairs={{0,2},{2,8},{4,6},{6,0},{8,10},{10,16},{12,14},{14,4},{16,18},{18,... | collective-permute-start | bytes 3145736 | tf_op jit(solution)/shard_map/ppermute | solution.py:549
  324.5 16.8 %collective-permute-start.24 = (f32[256,1024]{1,0:T(8,128)S(1)}, f32[256,1024]{1,0:T(8,128)S(1)}, u32[]{:S(2)}, u32[]{:S(2)}) collective-permute-start(f32[256,1024]{1,0:T(8,128)S(1)} %get-tuple-element.118), channel_id=1, source_target_pairs={{0,6},{2,0},{4,14},{6,4},{8,2},{10,8},{12,22},{14,12},{16,10},{18,... | collective-permute-start | bytes 3145736 | tf_op jit(solution)/shard_map/ppermute | solution.py:550
  335.7 14.1 %collective-permute-start.25 = (f32[256,1024]{1,0:T(8,128)S(1)}, f32[256,1024]{1,0:T(8,128)S(1)}, u32[]{:S(2)}, u32[]{:S(2)}) collective-permute-start(f32[256,1024]{1,0:T(8,128)S(1)} %get-tuple-element.120), channel_id=1, source_target_pairs={{0,2},{2,8},{4,6},{6,0},{8,10},{10,16},{12,14},{14,4},{16,18},{18,... | collective-permute-start | bytes 3145736 | tf_op jit(solution)/shard_map/ppermute | solution.py:549
  335.7 16.8 %collective-permute-start.26 = (f32[256,1024]{1,0:T(8,128)S(1)}, f32[256,1024]{1,0:T(8,128)S(1)}, u32[]{:S(2)}, u32[]{:S(2)}) collective-permute-start(f32[256,1024]{1,0:T(8,128)S(1)} %get-tuple-element.121), channel_id=1, source_target_pairs={{0,6},{2,0},{4,14},{6,4},{8,2},{10,8},{12,22},{14,12},{16,10},{18,... | collective-permute-start | bytes 3145736 | tf_op jit(solution)/shard_map/ppermute | solution.py:550
  346.9 14.1 %collective-permute-start.27 = (f32[256,1024]{1,0:T(8,128)S(1)}, f32[256,1024]{1,0:T(8,128)S(1)}, u32[]{:S(2)}, u32[]{:S(2)}) collective-permute-start(f32[256,1024]{1,0:T(8,128)S(1)} %get-tuple-element.123), channel_id=1, source_target_pairs={{0,2},{2,8},{4,6},{6,0},{8,10},{10,16},{12,14},{14,4},{16,18},{18,... | collective-permute-start | bytes 3145736 | tf_op jit(solution)/shard_map/ppermute | solution.py:549
  347.0 16.8 %collective-permute-start.28 = (f32[256,1024]{1,0:T(8,128)S(1)}, f32[256,1024]{1,0:T(8,128)S(1)}, u32[]{:S(2)}, u32[]{:S(2)}) collective-permute-start(f32[256,1024]{1,0:T(8,128)S(1)} %get-tuple-element.124), channel_id=1, source_target_pairs={{0,6},{2,0},{4,14},{6,4},{8,2},{10,8},{12,22},{14,12},{16,10},{18,... | collective-permute-start | bytes 3145736 | tf_op jit(solution)/shard_map/ppermute | solution.py:550
  358.1 14.1 %collective-permute-start.29 = (f32[256,1024]{1,0:T(8,128)S(1)}, f32[256,1024]{1,0:T(8,128)S(1)}, u32[]{:S(2)}, u32[]{:S(2)}) collective-permute-start(f32[256,1024]{1,0:T(8,128)S(1)} %get-tuple-element.126), channel_id=1, source_target_pairs={{0,2},{2,8},{4,6},{6,0},{8,10},{10,16},{12,14},{14,4},{16,18},{18,... | collective-permute-start | bytes 3145736 | tf_op jit(solution)/shard_map/ppermute | solution.py:549
  358.2 16.9 %collective-permute-start.30 = (f32[256,1024]{1,0:T(8,128)S(1)}, f32[256,1024]{1,0:T(8,128)S(1)}, u32[]{:S(2)}, u32[]{:S(2)}) collective-permute-start(f32[256,1024]{1,0:T(8,128)S(1)} %get-tuple-element.127), channel_id=1, source_target_pairs={{0,6},{2,0},{4,14},{6,4},{8,2},{10,8},{12,22},{14,12},{16,10},{18,... | collective-permute-start | bytes 3145736 | tf_op jit(solution)/shard_map/ppermute | solution.py:550
  370.0 15.1 %collective-permute-start.32 = (f32[256,1024]{1,0:T(8,128)}, f32[256,1024]{1,0:T(8,128)}, u32[]{:S(2)}, u32[]{:S(2)}) collective-permute-start(f32[256,1024]{1,0:T(8,128)} %get-tuple-element.130), channel_id=1, source_target_pairs={{0,2},{2,8},{4,6},{6,0},{8,10},{10,16},{12,14},{14,4},{16,18},{18,... | collective-permute-start | bytes 3145736 | tf_op jit(solution)/shard_map/ppermute | solution.py:549
  370.0 16.2 %collective-permute-start.33 = (f32[256,1024]{1,0:T(8,128)}, f32[256,1024]{1,0:T(8,128)}, u32[]{:S(2)}, u32[]{:S(2)}) collective-permute-start(f32[256,1024]{1,0:T(8,128)} %get-tuple-element.131), channel_id=1, source_target_pairs={{0,6},{2,0},{4,14},{6,4},{8,2},{10,8},{12,22},{14,12},{16,10},{18,... | collective-permute-start | bytes 3145736 | tf_op jit(solution)/shard_map/ppermute | solution.py:550
  381.5 13.3 %collective-permute-start.34 = (f32[256,1024]{1,0:T(8,128)}, f32[256,1024]{1,0:T(8,128)S(1)}, u32[]{:S(2)}, u32[]{:S(2)}) collective-permute-start(f32[256,1024]{1,0:T(8,128)} %get-tuple-element.134), channel_id=1, source_target_pairs={{0,2},{2,8},{4,6},{6,0},{8,10},{10,16},{12,14},{14,4},{16,18},{18,... | collective-permute-start | bytes 3145736 | tf_op jit(solution)/shard_map/ppermute | solution.py:549
  381.5 15.8 %collective-permute-start.35 = (f32[256,1024]{1,0:T(8,128)}, f32[256,1024]{1,0:T(8,128)}, u32[]{:S(2)}, u32[]{:S(2)}) collective-permute-start(f32[256,1024]{1,0:T(8,128)} %get-tuple-element.135), channel_id=1, source_target_pairs={{0,6},{2,0},{4,14},{6,4},{8,2},{10,8},{12,22},{14,12},{16,10},{18,... | collective-permute-start | bytes 3145736 | tf_op jit(solution)/shard_map/ppermute | solution.py:550
  382.0 4.3 %copy-start.10 = (f32[2048]{0:T(1024)S(1)}, f32[2048]{0:T(1024)}, u32[]{:S(2)}) copy-start(f32[2048]{0:T(1024)} %param.12) | copy-start | bytes 24580
  382.0 7.4 %collective-permute-start.31 = (f32[192,256]{1,0:T(8,128)S(1)}, f32[192,256]{1,0:T(8,128)S(1)}, u32[]{:S(2)}, u32[]{:S(2)}) collective-permute-start(f32[192,256]{1,0:T(8,128)S(1)} %get-tuple-element.128.here), channel_id=1, source_target_pairs={{0,1},{1,0},{2,3},{3,2},{4,5},{5,4},{6,7},{7,6},{8,9},{9,8},{10,11... | collective-permute-start | bytes 589832 | tf_op jit(solution)/shard_map/ppermute | solution.py:414
  386.2 3.2 copy-start.14
  386.2 3.3 copy-start.3
  389.5 0.7 copy-start.11
  390.4 0.7 copy-start.8
  394.8 1.0 copy-start.6
  397.3 4.2 %copy-start.1 = (f32[1024,256]{1,0:T(8,128)S(1)}, f32[1024,256]{1,0:T(8,128)}, u32[]{:S(2)}) copy-start(f32[1024,256]{1,0:T(8,128)} %param.7) | copy-start | bytes 3145732
  397.3 1.3 copy-start.7
Sparse Core Ops, SparseCore 0:
  11.3 183.2 all-gather.1
